TPU v7x, 32 devices: a whole 2x2x4 slice. The times are simulated.
32 devices in a mesh: dp: 16 (over z, x, core), mp: 2 (over y).
Axes of the slice: x: 2, y: 2, z: 4, core: 2. Of those that a mesh axis runs over, the one named last changes fastest.
Arguments:
- tokens: bfloat16 [32, 680, 1024], P('dp', 'mp'), may hold values from -6 to 6
- condition: bfloat16 [32, 1024], P('dp'), may hold values from -6 to 6
- scale_lengths: int32 [32, 10], P('dp'), may hold values from 1 to 256, 680 in all within a row
- order: int32 [16, 2], P('dp'), may hold values from 0 to 1, each once within a row
- cotangent: bfloat16 [32, 680, 1024], P('dp', 'mp'), may hold values from -6 to 6
- ada_weight: bfloat16 [1024, 6, 1024], P('dp', None, 'mp'), may hold values from -0.1875 to 0.1875
- ada_bias: bfloat16 [6, 16, 64], P(None, 'mp', 'dp'), may hold values from -3 to 3
- qkv_weight: bfloat16 [3, 1024, 1024], P(None, 'dp', 'mp'), may hold values from -0.1875 to 0.1875
- qv_bias: bfloat16 [2, 16, 64], P(None, 'mp', 'dp'), may hold values from -3 to 3
- head_log_scale: float32 [16], P('mp'), may hold values from 2.1 to 3.2
- proj_weight: bfloat16 [1024, 1024], P('mp', 'dp'), may hold values from -1 to 1
- out_bias: bfloat16 [2, 16, 64], P(None, 'mp', 'dp'), may hold values from -2 to 2
- fc1_weight: bfloat16 [1024, 4096], P('dp', 'mp'), may hold values from -0.1875 to 0.1875
- fc1_bias: bfloat16 [64, 64], P('mp', 'dp'), may hold values from -3 to 3
- fc2_weight: bfloat16 [4096, 1024], P('mp', 'dp'), may hold values from -0.09375 to 0.09375
Outputs:
- activations: bfloat16 [32, 680, 1024], P('dp', 'mp')
- tokens_grad: bfloat16 [32, 680, 1024], P('dp', 'mp')
- condition_grad: bfloat16 [32, 1024], P('dp')
- ada_weight_grad: float32 [1024, 6, 1024], P('dp', None, 'mp')
- ada_bias_grad: float32 [6, 16, 64], P(None, 'mp', 'dp')
- qkv_weight_grad: float32 [3, 1024, 1024], P(None, 'dp', 'mp')
- qv_bias_grad: float32 [2, 16, 64], P(None, 'mp', 'dp')
- head_scale_grad: float32 [16], P('mp')
- proj_weight_grad: float32 [1024, 1024], P('mp', 'dp')
- out_bias_grad: float32 [2, 16, 64], P(None, 'mp', 'dp')
- fc1_weight_grad: float32 [1024, 4096], P('dp', 'mp')
- fc1_bias_grad: float32 [64, 64], P('mp', 'dp')
- fc2_weight_grad: float32 [4096, 1024], P('mp', 'dp')
Inputs may be any that keep to these rules, and one draw needn't show every extreme that they name: `scale_lengths`: the 10 lengths of every image sum to 680, and one of them equals 256. Each row of order holds every number of 0 to 1 once.
All inputs are finite; a program needn't handle non-finite values.
Results may differ from a plain program's by a relative error of at most 0.02.
Values may be sent and summed in bfloat16 or wider, within the bound.
A program may use at most 192 MiB of HBM per device.

v0:
```python
import jax
import jax.numpy as jnp
from jax import lax
from jax.sharding import PartitionSpec as P

precise = lax.Precision.HIGHEST


def row_norm(values):
    centre = jnp.mean(values, -1, keepdims=True)
    shifted = values - centre
    inverse = lax.rsqrt(jnp.mean(shifted * shifted, -1, keepdims=True) + 1e-06)
    return (shifted * inverse, inverse)


def row_norm_back(incoming, normed, inverse):
    return inverse * (
        incoming
        - jnp.mean(incoming, -1, keepdims=True)
        - normed * jnp.mean(incoming * normed, -1, keepdims=True)
    )


def gelu_tanh(values):
    return jax.nn.gelu(values, approximate=True)


def spread(shard_rows):
    return lax.all_gather(shard_rows, "mp", axis=0, tiled=True)


def collect(partial_sum):
    return lax.psum_scatter(
        partial_sum.astype(jnp.bfloat16), "mp", scatter_dimension=0, tiled=True
    ).astype(jnp.float32)


def fetch(qkv_weight, qv_bias, proj_weight, out_bias, fc1_weight, fc1_bias, fc2_weight):
    return (
        lax.all_gather(qkv_weight, "dp", axis=1, tiled=True),
        lax.all_gather(qv_bias, "dp", axis=2, tiled=True),
        lax.all_gather(proj_weight, "dp", axis=1, tiled=True),
        lax.all_gather(out_bias, "dp", axis=2, tiled=True),
        lax.all_gather(fc1_weight, "dp", axis=0, tiled=True),
        lax.all_gather(fc1_bias, "dp", axis=1, tiled=True),
        lax.all_gather(fc2_weight, "dp", axis=1, tiled=True),
    )


def settle(grad_set):
    qkv_part, qv_part, proj_part, outb_part, fc1_part, fc1b_part, fc2_part = grad_set
    return (
        lax.psum_scatter(
            qkv_part.astype(jnp.bfloat16), "dp", scatter_dimension=1, tiled=True
        ).astype(jnp.float32),
        lax.psum_scatter(
            qv_part.astype(jnp.bfloat16), "dp", scatter_dimension=2, tiled=True
        ).astype(jnp.float32),
        lax.psum_scatter(
            proj_part.astype(jnp.bfloat16), "dp", scatter_dimension=1, tiled=True
        ).astype(jnp.float32),
        lax.psum_scatter(
            outb_part.astype(jnp.bfloat16), "dp", scatter_dimension=2, tiled=True
        ).astype(jnp.float32),
        lax.psum_scatter(
            fc1_part.astype(jnp.bfloat16), "dp", scatter_dimension=0, tiled=True
        ).astype(jnp.float32),
        lax.psum_scatter(
            fc1b_part.astype(jnp.bfloat16), "dp", scatter_dimension=1, tiled=True
        ).astype(jnp.float32),
        lax.psum_scatter(
            fc2_part.astype(jnp.bfloat16), "dp", scatter_dimension=1, tiled=True
        ).astype(jnp.float32),
    )


def on_device(
    tokens,
    condition,
    scale_lengths,
    order,
    cotangent,
    ada_weight,
    ada_bias,
    qkv_weight,
    qv_bias,
    head_log_scale,
    proj_weight,
    out_bias,
    fc1_weight,
    fc1_bias,
    fc2_weight,
):
    image_count, shard_rows, model_width = tokens.shape
    column_count = qkv_weight.shape[2]
    local_heads = qv_bias.shape[1]
    head_width = column_count // local_heads
    hidden_cols = fc1_weight.shape[1]
    own_start = lax.axis_index("mp") * column_count
    token_count = shard_rows * lax.axis_size("mp")
    ada_full, ada_bias_full = (
        lax.all_gather(ada_weight, "dp", axis=0, tiled=True),
        lax.all_gather(ada_bias, "dp", axis=2, tiled=True),
    )
    cond_float = condition.astype(jnp.float32)
    signal = jax.nn.silu(cond_float).astype(jnp.bfloat16)
    ada_flat = ada_full.reshape(model_width, 6 * column_count)
    mod_share = jnp.dot(
        signal, ada_flat, preferred_element_type=jnp.float32
    ) + ada_bias_full.reshape(6 * column_count).astype(jnp.float32)
    modulation = lax.all_gather(
        mod_share.reshape(image_count, 6, column_count), "mp", axis=2, tiled=True
    )
    head_boost = jnp.exp(head_log_scale)[None, :, None]
    positions = jnp.arange(token_count, dtype=jnp.int32)

    def place(vector):
        return lax.dynamic_update_slice(
            jnp.zeros((model_width,), jnp.float32), vector, (own_start,)
        )

    def own_columns(matrix):
        return lax.dynamic_slice_in_dim(matrix, own_start, column_count, 1)

    def rows_now():
        return fetch(qkv_weight, qv_bias, proj_weight, out_bias, fc1_weight, fc1_bias, fc2_weight)

    full_shapes = (
        (3, model_width, column_count),
        (2, local_heads, head_width),
        (column_count, model_width),
        (2, local_heads, head_width),
        (model_width, hidden_cols),
        (hidden_cols // head_width, head_width),
        (hidden_cols, model_width),
    )
    grad_start = tuple((jnp.zeros(shape_item, jnp.float32) for shape_item in full_shapes))

    def micro_step(micro_at, state_now):
        outputs, token_grads, mod_grads, weight_grads, scale_grad = state_now
        image_at = order[0, micro_at]
        residual = lax.dynamic_index_in_dim(tokens, image_at, 0, keepdims=False).astype(jnp.float32)
        image_mods = lax.dynamic_index_in_dim(modulation, image_at, 0, keepdims=False)
        lengths = lax.dynamic_index_in_dim(scale_lengths, image_at, 0, keepdims=False)
        out_grad = lax.dynamic_index_in_dim(cotangent, micro_at, 0, keepdims=False).astype(
            jnp.float32
        )
        qkv_full, qv_full, proj_full, outb_full, fc1_full, fc1b_full, fc2_full = rows_now()
        scale_ends = jnp.cumsum(lengths)
        scale_of = jnp.sum((positions[:, None] >= scale_ends[None, :]).astype(jnp.int32), 1)
        allowed = (scale_of[None, :] <= scale_of[:, None])[None]
        normed_one, inverse_one = row_norm(residual)
        input_one = spread(
            (normed_one * (1.0 + image_mods[2]) + image_mods[4]).astype(jnp.bfloat16)
        )
        projected = jnp.einsum(
            "td,cde->cte", input_one, qkv_full, preferred_element_type=jnp.float32
        )
        bias_pair = qv_full.reshape(2, column_count).astype(jnp.float32)
        queries = (projected[0] + bias_pair[0]).reshape(token_count, local_heads, head_width)
        keys_raw = projected[1].reshape(token_count, local_heads, head_width)
        values_low = (
            (projected[2] + bias_pair[1])
            .astype(jnp.bfloat16)
            .reshape(token_count, local_heads, head_width)
        )
        query_inv = lax.rsqrt(jnp.sum(queries * queries, -1, keepdims=True) + 1e-06)
        key_inv = lax.rsqrt(jnp.sum(keys_raw * keys_raw, -1, keepdims=True) + 1e-06)
        query_unit = queries * query_inv
        key_unit = keys_raw * key_inv
        query_low = (query_unit * head_boost).astype(jnp.bfloat16)
        key_low = key_unit.astype(jnp.bfloat16)

        def masked_scores():
            raw_scores = jnp.einsum(
                "qhd,khd->hqk", query_low, key_low, preferred_element_type=jnp.float32
            )
            return jnp.where(allowed, raw_scores, -1e30)

        scores = masked_scores()
        row_peak = jnp.max(scores, -1, keepdims=True)
        exp_terms = jnp.exp(scores - row_peak)
        totals = jnp.sum(exp_terms, -1, keepdims=True)
        log_total = row_peak + jnp.log(totals)
        soft_weights = exp_terms / totals
        mixed_heads = (
            jnp.einsum(
                "hqk,khd->qhd",
                soft_weights.astype(jnp.bfloat16),
                values_low,
                preferred_element_type=jnp.float32,
            )
            .astype(jnp.bfloat16)
            .reshape(token_count, column_count)
        )
        attended = collect(
            jnp.dot(mixed_heads, proj_full, preferred_element_type=jnp.float32)
            + place(outb_full[0].reshape(column_count).astype(jnp.float32))
        )
        middle = residual + image_mods[0] * attended
        normed_two, inverse_two = row_norm(middle)
        input_two = spread(
            (normed_two * (1.0 + image_mods[3]) + image_mods[5]).astype(jnp.bfloat16)
        )
        hidden = jnp.dot(
            input_two, fc1_full, preferred_element_type=jnp.float32
        ) + fc1b_full.reshape(hidden_cols).astype(jnp.float32)
        activated = gelu_tanh(hidden).astype(jnp.bfloat16)
        branch_out = collect(
            jnp.dot(activated, fc2_full, preferred_element_type=jnp.float32)
            + place(outb_full[1].reshape(column_count).astype(jnp.float32))
        )
        result = (middle + image_mods[1] * branch_out).astype(jnp.bfloat16)
        outputs = lax.dynamic_update_index_in_dim(outputs, result, micro_at, 0)
        qkv_back, qv_back, proj_back, outb_back, fc1_back, fc1b_back, fc2_back = rows_now()
        grad_branch = spread((image_mods[1] * out_grad).astype(jnp.bfloat16))
        gamma_two_grad = jnp.sum(out_grad * branch_out, 0)
        fc2_grad = jnp.dot(activated.T, grad_branch, preferred_element_type=jnp.float32)
        bias_two_grad = jnp.sum(own_columns(grad_branch).astype(jnp.float32), 0)
        act_grad = jnp.dot(grad_branch, fc2_back.T, preferred_element_type=jnp.float32)
        gelu_pull = jax.vjp(gelu_tanh, hidden)[1]
        hidden_grad = gelu_pull(act_grad)[0].astype(jnp.bfloat16)
        fc1_grad = jnp.dot(input_two.T, hidden_grad, preferred_element_type=jnp.float32)
        fc1b_grad = jnp.sum(hidden_grad.astype(jnp.float32), 0).reshape(
            hidden_cols // head_width, head_width
        )
        input_two_grad = collect(
            jnp.dot(hidden_grad, fc1_back.T, preferred_element_type=jnp.float32)
        )
        scale_two_grad = jnp.sum(input_two_grad * normed_two, 0)
        shift_two_grad = jnp.sum(input_two_grad, 0)
        middle_grad = out_grad + row_norm_back(
            input_two_grad * (1.0 + image_mods[3]), normed_two, inverse_two
        )
        grad_attended = spread((image_mods[0] * middle_grad).astype(jnp.bfloat16))
        gamma_one_grad = jnp.sum(middle_grad * attended, 0)
        proj_grad = jnp.dot(mixed_heads.T, grad_attended, preferred_element_type=jnp.float32)
        bias_one_grad = jnp.sum(own_columns(grad_attended).astype(jnp.float32), 0)
        mixed_grad = (
            jnp.dot(grad_attended, proj_back.T, preferred_element_type=jnp.float32)
            .astype(jnp.bfloat16)
            .reshape(token_count, local_heads, head_width)
        )
        soft_again = jnp.exp(masked_scores() - log_total)
        value_grad = jnp.einsum(
            "hqk,qhd->khd",
            soft_again.astype(jnp.bfloat16),
            mixed_grad,
            preferred_element_type=jnp.float32,
        )
        soft_grad = jnp.einsum(
            "qhd,khd->hqk", mixed_grad, values_low, preferred_element_type=jnp.float32
        )
        score_grad = (
            soft_again * (soft_grad - jnp.sum(soft_again * soft_grad, -1, keepdims=True))
        ).astype(jnp.bfloat16)
        query_low_grad = jnp.einsum(
            "hqk,khd->qhd", score_grad, key_low, preferred_element_type=jnp.float32
        )
        key_low_grad = jnp.einsum(
            "hqk,qhd->khd", score_grad, query_low, preferred_element_type=jnp.float32
        )
        head_grad = jnp.sum(query_low_grad * query_unit * head_boost, (0, 2))
        query_unit_grad = query_low_grad * head_boost
        query_grad = query_inv * (
            query_unit_grad - query_unit * jnp.sum(query_unit_grad * query_unit, -1, keepdims=True)
        )
        key_grad = key_inv * (
            key_low_grad - key_unit * jnp.sum(key_low_grad * key_unit, -1, keepdims=True)
        )
        triple_grad = jnp.stack(
            [
                query_grad.reshape(token_count, column_count),
                key_grad.reshape(token_count, column_count),
                value_grad.reshape(token_count, column_count),
            ]
        ).astype(jnp.bfloat16)
        qkv_grad = jnp.einsum(
            "td,cte->cde", input_one, triple_grad, preferred_element_type=jnp.float32
        )
        pair_sums = jnp.sum(triple_grad.astype(jnp.float32), 1)
        qv_grad = jnp.stack([pair_sums[0], pair_sums[2]]).reshape(2, local_heads, head_width)
        input_one_grad = collect(
            jnp.einsum("cte,cde->td", triple_grad, qkv_back, preferred_element_type=jnp.float32)
        )
        scale_one_grad = jnp.sum(input_one_grad * normed_one, 0)
        shift_one_grad = jnp.sum(input_one_grad, 0)
        residual_grad = middle_grad + row_norm_back(
            input_one_grad * (1.0 + image_mods[2]), normed_one, inverse_one
        )
        token_grads = lax.dynamic_update_index_in_dim(
            token_grads, residual_grad.astype(jnp.bfloat16), image_at, 0
        )
        image_mod_grad = jnp.stack(
            [
                gamma_one_grad,
                gamma_two_grad,
                scale_one_grad,
                scale_two_grad,
                shift_one_grad,
                shift_two_grad,
            ]
        )
        mod_grads = lax.dynamic_update_index_in_dim(mod_grads, image_mod_grad, image_at, 0)
        outb_grad = jnp.stack([bias_one_grad, bias_two_grad]).reshape(2, local_heads, head_width)
        local_grads = (qkv_grad, qv_grad, proj_grad, outb_grad, fc1_grad, fc1b_grad, fc2_grad)
        weight_grads = tuple(
            (running + addend for running, addend in zip(weight_grads, local_grads))
        )
        return (outputs, token_grads, mod_grads, weight_grads, scale_grad + head_grad)

    start_state = (
        jnp.zeros(tokens.shape, jnp.bfloat16),
        jnp.zeros(tokens.shape, jnp.bfloat16),
        jnp.zeros((image_count, 6, model_width), jnp.float32),
        grad_start,
        jnp.zeros((local_heads,), jnp.float32),
    )
    outputs, token_grads, mod_grads, weight_grads, scale_grad = lax.fori_loop(
        0, image_count, micro_step, start_state
    )
    shard_grads = settle(weight_grads)
    mod_share_grad = lax.psum_scatter(
        mod_grads.astype(jnp.bfloat16), "mp", scatter_dimension=2, tiled=True
    ).astype(jnp.float32)
    flat_grad = mod_share_grad.reshape(image_count, 6 * column_count)
    ada_grad = jnp.dot(
        signal.astype(jnp.float32).T,
        flat_grad,
        precision=precise,
        preferred_element_type=jnp.float32,
    ).reshape(model_width, 6, column_count)
    ada_bias_grad = jnp.sum(mod_share_grad, 0).reshape(6, local_heads, head_width)
    signal_grad = lax.psum(
        jnp.dot(
            flat_grad,
            ada_flat.astype(jnp.float32).T,
            precision=precise,
            preferred_element_type=jnp.float32,
        ),
        "mp",
    )
    silu_pull = jax.vjp(jax.nn.silu, cond_float)[1]
    condition_grad = silu_pull(signal_grad)[0].astype(jnp.bfloat16)
    ada_shard, ada_bias_shard = (
        lax.psum_scatter(
            ada_grad.astype(jnp.bfloat16), "dp", scatter_dimension=0, tiled=True
        ).astype(jnp.float32),
        lax.psum_scatter(
            ada_bias_grad.astype(jnp.bfloat16), "dp", scatter_dimension=2, tiled=True
        ).astype(jnp.float32),
    )
    head_scale_grad = lax.psum(scale_grad, "dp")
    qkv_shard, qv_shard, proj_shard, outb_shard, fc1_shard, fc1b_shard, fc2_shard = shard_grads
    return (
        outputs,
        token_grads,
        condition_grad,
        ada_shard,
        ada_bias_shard,
        qkv_shard,
        qv_shard,
        head_scale_grad,
        proj_shard,
        outb_shard,
        fc1_shard,
        fc1b_shard,
        fc2_shard,
    )


def solution(mesh):
    in_specs = (
        P("dp", "mp", None),
        P("dp", None),
        P("dp", None),
        P("dp", None),
        P("dp", "mp", None),
        P("dp", None, "mp"),
        P(None, "mp", "dp"),
        P(None, "dp", "mp"),
        P(None, "mp", "dp"),
        P("mp"),
        P("mp", "dp"),
        P(None, "mp", "dp"),
        P("dp", "mp"),
        P("mp", "dp"),
        P("mp", "dp"),
    )
    out_specs = (
        P("dp", "mp", None),
        P("dp", "mp", None),
        P("dp", None),
        P("dp", None, "mp"),
        P(None, "mp", "dp"),
        P(None, "dp", "mp"),
        P(None, "mp", "dp"),
        P("mp"),
        P("mp", "dp"),
        P(None, "mp", "dp"),
        P("dp", "mp"),
        P("mp", "dp"),
        P("mp", "dp"),
    )
    return jax.shard_map(
        on_device, mesh=mesh, in_specs=in_specs, out_specs=out_specs, check_vma=False
    )
```

profile of v0, /device:TPU:0, one launch (start us, length us, event | category | flops | bytes accessed | tf_op | source)
XLA Modules:
  0.0 1638.7 jit_solution(11032548064479682145)
XLA Ops:
  11.3 23.7 %all_gather.124 = bf16[6,8,64]{1,0,2:T(8,128)(2,1)S(1)} all-gather(bf16[6,8,4]{1,0,2:T(8,128)(2,1)S(1)} %copy.197), channel_id=1, replica_groups=mesh['dp'=16,'mp'=2] {'dp'}, dimensions={2}, use_global_device_ids=true | all-gather | bytes 6528 | tf_op jit(solution)/shard_map/all_gather | solution.py:103
  39.0 36.2 %all-gather.30.cloned.1.call-done = bf16[1024,6,512]{2,0,1:T(8,128)(2,1)} async-done(((bf16[64,6,512]{2,0,1:T(8,128)(2,1)}), bf16[1024,6,512]{2,0,1:T(8,128)(2,1)}) %all-gather.30.cloned.1.call-update) | async-done | bytes 6291472 | tf_op jit(solution)/shard_map/all_gather | solution.py:102
  75.2 8.6 copy.196
  94.9 1093.2 %while.36 = (s32[]{:T(128)}, bf16[2,340,1024]{2,1,0:T(8,128)(2,1)}, bf16[2,340,1024]{2,1,0:T(8,128)(2,1)}, bf16[2,6,1024]{2,1,0:T(8,128)(2,1)}, f32[3,1024,512]{...) while((s32[]{:T(128)}, bf16[2,340,1024]{2,1,0:T(8,128)(2,1)}, ...), condition=%wide.region_33.34_spmd.clone, body=%wide.region_0.33_spmd.clone.sunk | while | flops 28729032704 | bytes 609624640 | solution.py:319
  105.5 19.4 %all_gather.141 = bf16[2,8,64]{1,0,2:T(2,128)(2,1)S(1)} all-gather(bf16[2,8,4]{1,0,2:T(2,128)(2,1)} %get-tuple-element.1405), channel_id=1, replica_groups=mesh['dp'=16,'mp'=2] {'dp'}, dimensions={2}, use_global_device_ids=true | all-gather | bytes 2176 | tf_op jit(solution)/shard_map/while/body/eval_jaxpr/all_gather | solution.py:43
  124.8 17.7 %all_gather.139 = bf16[2,8,64]{1,0,2:T(2,128)(2,1)S(1)} all-gather(bf16[2,8,4]{1,0,2:T(2,128)(2,1)} %get-tuple-element.1401), channel_id=1, replica_groups=mesh['dp'=16,'mp'=2] {'dp'}, dimensions={2}, use_global_device_ids=true | all-gather | bytes 2176 | tf_op jit(solution)/shard_map/while/body/eval_jaxpr/all_gather | solution.py:41
  146.0 26.7 %all-gather.34.cloned.1.call-done = bf16[3,1024,512]{2,1,0:T(8,128)(2,1)} async-done(((bf16[3,64,512]{2,1,0:T(8,128)(2,1)}), bf16[3,1024,512]{2,1,0:T(8,128)(2,1)}) %all-gather.34.cloned.1.call-update) | async-done | bytes 3145744 | tf_op jit(solution)/shard_map/while/body/eval_jaxpr/all_gather | solution.py:40
  184.8 8.4 select_reduce_fusion.2
  193.2 8.9 fusion.217
  202.1 9.4 fusion.218
  215.2 37.8 %fusion.220 = bf16[344,1024]{1,0:T(8,128)(2,1)} fusion(bf16[680,1024]{1,0:T(8,128)(2,1)} %add_convert_fusion.10), kind=kCustom, calls=%all-reduce-scatter.clone.1 | all-reduce-scatter fusion | flops 704513 | bytes 2097664 | tf_op jit(solution)/shard_map/while
  257.8 4.9 concatenate.14
  270.3 19.3 %all-gather.17 = bf16[16,4,32]{2,1,0:T(4,128)(2,1)S(1)} all-gather(bf16[1,4,32]{2,1,0:T(4,128)(2,1)} %bitcast.352), channel_id=1, replica_groups=mesh['dp'=16,'mp'=2] {'dp'}, dimensions={0}, use_global_device_ids=true | all-gather | bytes 4352 | tf_op jit(solution)/shard_map/while/body/eval_jaxpr/all_gather | solution.py:45
  296.9 50.0 %all-gather.40.cloned.1.call-done = bf16[1024,2048]{1,0:T(8,128)(2,1)} async-done(((bf16[64,2048]{1,0:T(8,128)(2,1)}), bf16[1024,2048]{1,0:T(8,128)(2,1)}) %all-gather.40.cloned.1.call-update) | async-done | bytes 4194320 | tf_op jit(solution)/shard_map/while/body/eval_jaxpr/all_gather | solution.py:44
  346.9 8.1 fusion.223
  355.0 43.2 %all-gather.44.cloned.1.call-done = bf16[2048,1024]{0,1:T(8,128)(2,1)} async-done(((bf16[2048,64]{0,1:T(8,128)(2,1)}), bf16[2048,1024]{0,1:T(8,128)(2,1)}) %all-gather.44.cloned.1.call-update) | async-done | bytes 4194320 | tf_op jit(solution)/shard_map/while/body/eval_jaxpr/all_gather | solution.py:46
  398.1 9.5 convert_reduce_fusion.16
  413.4 22.7 %fusion.225 = bf16[344,1024]{1,0:T(8,128)(2,1)} fusion(bf16[680,1024]{1,0:T(8,128)(2,1)} %convolution_convert_fusion.5), kind=kCustom, calls=%all-reduce-scatter.2.clone.1 | all-reduce-scatter fusion | flops 704513 | bytes 2097664 | tf_op jit(solution)/shard_map/while
  440.2 8.7 add_convert_fusion.11
  457.0 5.1 concatenate.15
  471.4 11.0 select_add_fusion.12
  482.4 11.5 all-gather.46.cloned.1.call-done
  503.5 10.7 fusion.229
  514.2 12.0 multiply_reduce_fusion.12
  526.1 11.9 multiply_convert_fusion.20
  560.5 5.3 bitcast_convert_fusion.2
  565.9 36.0 %fusion.233 = (bf16[344,1024]{1,0:T(8,128)(2,1)S(1)}, bf16[344,1024]{1,0:T(8,128)(2,1)S(1)}) fusion(bf16[680,1024]{1,0:T(8,128)(2,1)} %add_convert_fusion.11, bf16[680,1024]{1,0:T(8,128)(2,1)} %bitcast_convert_fusion.2), kind=kCustom, calls=%all-reduce-scatter.4.clone.1 | all-reduce-scatter fusion | flops 1409025 | bytes 4194816 | tf_op jit(solution)/shard_map/while
  608.0 6.5 bitcast_add_fusion.2
  620.5 4.9 concatenate.16
  647.4 21.7 %all_gather.141 = bf16[2,8,64]{1,0,2:T(2,128)(2,1)S(1)} all-gather(bf16[2,8,4]{1,0,2:T(2,128)(2,1)} %get-tuple-element.1405), channel_id=1, replica_groups=mesh['dp'=16,'mp'=2] {'dp'}, dimensions={2}, use_global_device_ids=true | all-gather | bytes 2176 | tf_op jit(solution)/shard_map/while/body/eval_jaxpr/all_gather | solution.py:43
  669.1 17.8 %all_gather.139 = bf16[2,8,64]{1,0,2:T(2,128)(2,1)S(1)} all-gather(bf16[2,8,4]{1,0,2:T(2,128)(2,1)} %get-tuple-element.1401), channel_id=1, replica_groups=mesh['dp'=16,'mp'=2] {'dp'}, dimensions={2}, use_global_device_ids=true | all-gather | bytes 2176 | tf_op jit(solution)/shard_map/while/body/eval_jaxpr/all_gather | solution.py:41
  690.2 25.6 %all-gather.34.cloned.1.call-done = bf16[3,1024,512]{2,1,0:T(8,128)(2,1)} async-done(((bf16[3,64,512]{2,1,0:T(8,128)(2,1)}), bf16[3,1024,512]{2,1,0:T(8,128)(2,1)}) %all-gather.34.cloned.1.call-update) | async-done | bytes 3145744 | tf_op jit(solution)/shard_map/while/body/eval_jaxpr/all_gather | solution.py:40
  727.9 8.4 select_reduce_fusion.2
  736.4 8.9 fusion.217
  745.2 9.4 fusion.218
  758.3 37.9 %fusion.220 = bf16[344,1024]{1,0:T(8,128)(2,1)} fusion(bf16[680,1024]{1,0:T(8,128)(2,1)} %add_convert_fusion.10), kind=kCustom, calls=%all-reduce-scatter.clone.1 | all-reduce-scatter fusion | flops 704513 | bytes 2097664 | tf_op jit(solution)/shard_map/while
  801.1 4.9 concatenate.14
  813.3 18.9 %all-gather.17 = bf16[16,4,32]{2,1,0:T(4,128)(2,1)S(1)} all-gather(bf16[1,4,32]{2,1,0:T(4,128)(2,1)} %bitcast.352), channel_id=1, replica_groups=mesh['dp'=16,'mp'=2] {'dp'}, dimensions={0}, use_global_device_ids=true | all-gather | bytes 4352 | tf_op jit(solution)/shard_map/while/body/eval_jaxpr/all_gather | solution.py:45
  839.8 50.1 %all-gather.40.cloned.1.call-done = bf16[1024,2048]{1,0:T(8,128)(2,1)} async-done(((bf16[64,2048]{1,0:T(8,128)(2,1)}), bf16[1024,2048]{1,0:T(8,128)(2,1)}) %all-gather.40.cloned.1.call-update) | async-done | bytes 4194320 | tf_op jit(solution)/shard_map/while/body/eval_jaxpr/all_gather | solution.py:44
  889.9 8.1 fusion.223
  897.9 43.0 %all-gather.44.cloned.1.call-done = bf16[2048,1024]{0,1:T(8,128)(2,1)} async-done(((bf16[2048,64]{0,1:T(8,128)(2,1)}), bf16[2048,1024]{0,1:T(8,128)(2,1)}) %all-gather.44.cloned.1.call-update) | async-done | bytes 4194320 | tf_op jit(solution)/shard_map/while/body/eval_jaxpr/all_gather | solution.py:46
  941.0 9.5 convert_reduce_fusion.16
  956.2 22.7 %fusion.225 = bf16[344,1024]{1,0:T(8,128)(2,1)} fusion(bf16[680,1024]{1,0:T(8,128)(2,1)} %convolution_convert_fusion.5), kind=kCustom, calls=%all-reduce-scatter.2.clone.1 | all-reduce-scatter fusion | flops 704513 | bytes 2097664 | tf_op jit(solution)/shard_map/while
  983.0 8.7 add_convert_fusion.11
  999.9 5.1 concatenate.15
  1014.9 14.1 select_add_fusion.12
  1029.0 7.7 all-gather.46.cloned.1.call-done
  1046.3 10.7 fusion.229
  1057.0 12.0 multiply_reduce_fusion.12
  1069.0 11.9 multiply_convert_fusion.20
  1104.9 5.3 bitcast_convert_fusion.2
  1110.3 36.0 %fusion.233 = (bf16[344,1024]{1,0:T(8,128)(2,1)S(1)}, bf16[344,1024]{1,0:T(8,128)(2,1)S(1)}) fusion(bf16[680,1024]{1,0:T(8,128)(2,1)} %add_convert_fusion.11, bf16[680,1024]{1,0:T(8,128)(2,1)} %bitcast_convert_fusion.2), kind=kCustom, calls=%all-reduce-scatter.4.clone.1 | all-reduce-scatter fusion | flops 1409025 | bytes 4194816 | tf_op jit(solution)/shard_map/while
  1152.4 7.4 bitcast_add_fusion.2
  1188.7 12.6 reduce-scatter.18.cloned.1.call-done
  1205.6 5.4 copy.206
  1211.1 6.1 convert_element_type.488
  1217.3 7.4 copy.211
  1231.9 33.2 %psum.15 = f32[8]{0:T(128)} all-reduce(f32[8]{0:T(128)S(1)} %copy-done.38), channel_id=1, replica_groups=mesh['dp'=16,'mp'=2] {'dp'}, use_global_device_ids=true, to_apply=%region_41.42 | all-reduce | flops 8 | bytes 64 | tf_op jit(solution)/shard_map/psum | solution.py:353
  1271.2 58.6 %all-reduce.11 = (bf16[2,8,64]{1,2,0:T(8,128)(2,1)S(1)}, bf16[2,8,64]{1,2,0:T(8,128)(2,1)S(1)}, bf16[32,64]{0,1:T(8,128)(2,1)S(1)}) all-reduce(bf16[2,8,64]{1,2,0:T(8,128)(2,1)S(1)} %copy.207, bf16[2,8,64]{1,2,0:T(8,128)(2,1)S(1)} %copy.209, bf16[32,64]{0,1:T(8,128)(2,1)S(1)} %copy.210), channel_id=10, replica_groups=mesh['dp'=16,'mp'=2] {'dp'}, use_global_device_ids=true, to_apply=%region_40.41.clone | all-reduce | flops 4096 | bytes 16384
  1335.8 5.0 psum.14
  1344.2 45.9 %reduce-scatter.24.cloned.1.call-done = bf16[3,64,512]{2,1,0:T(8,128)(2,1)} async-done(((bf16[3,1024,512]{2,1,0:T(8,128)(2,1)}), bf16[3,64,512]{2,1,0:T(8,128)(2,1)}) %reduce-scatter.24.cloned.1.call-update) | async-done | bytes 196624 | tf_op jit(solution)/shard_map/reduce_scatter | solution.py:53
  1391.8 73.9 %reduce-scatter.28.cloned.1.call-done = bf16[64,2048]{1,0:T(8,128)(2,1)} async-done(((bf16[1024,2048]{1,0:T(8,128)(2,1)}), bf16[64,2048]{1,0:T(8,128)(2,1)}) %reduce-scatter.28.cloned.1.call-update) | async-done | bytes 262160 | tf_op jit(solution)/shard_map/reduce_scatter | solution.py:65
  1467.5 73.6 %reduce-scatter.30.cloned.1.call-done = bf16[2048,64]{0,1:T(8,128)(2,1)} async-done(((bf16[2048,1024]{0,1:T(8,128)(2,1)}), bf16[2048,64]{0,1:T(8,128)(2,1)}) %reduce-scatter.30.cloned.1.call-update) | async-done | bytes 262160 | tf_op jit(solution)/shard_map/reduce_scatter | solution.py:71
  1542.8 86.8 %reduce-scatter.20.cloned.1.call-done = bf16[64,6,512]{2,0,1:T(8,128)(2,1)} async-done(((bf16[1024,6,512]{2,0,1:T(8,128)(2,1)}), bf16[64,6,512]{2,0,1:T(8,128)(2,1)}) %reduce-scatter.20.cloned.1.call-update) | async-done | bytes 393232 | tf_op jit(solution)/shard_map/reduce_scatter | solution.py:346
  (459 shorter events, 319.0 us)
Async XLA Ops:
  7.2 68.0 %all-gather.30.cloned.1.call-start = ((), (), s32[]{:S(2)}) async-start(), calls=%async_computation.7 | async-start | bytes 6684672 | tf_op jit(solution)/shard_map/all_gather | solution.py:102
  8.0 28.9 %copy-start.21 = (bf16[2,340,1024]{2,0,1:T(2,128)(2,1)S(1)}, bf16[2,340,1024]{2,0,1:T(2,128)(2,1)}, u32[]{:S(2)}) copy-start(bf16[2,340,1024]{2,0,1:T(2,128)(2,1)} %param.21) | copy-start | bytes 4177924
  39.0 44.8 %copy-start.34 = (bf16[2,1024]{1,0:T(2,128)(2,1)S(1)}, bf16[2,1024]{1,0:T(2,128)(2,1)}, u32[]{:S(2)}) copy-start(bf16[2,1024]{1,0:T(2,128)(2,1)} %param.18) | copy-start | bytes 12292
  94.9 49.4 %all-gather.32.cloned.1.call-start = ((), (), s32[]{:S(2)}) async-start(), calls=%async_computation.15 | async-start | bytes 2113536 | tf_op jit(solution)/shard_map/while/body/eval_jaxpr/all_gather | solution.py:29
  100.9 71.8 %all-gather.34.cloned.1.call-start = ((), (), s32[]{:S(2)}) async-start(), calls=%async_computation.16 | async-start | bytes 3342336 | tf_op jit(solution)/shard_map/while/body/eval_jaxpr/all_gather | solution.py:40
  101.6 109.9 %all-gather.36.cloned.1.call-start = ((), (), s32[]{:S(2)}) async-start(), calls=%async_computation.17 | async-start | bytes 1114112 | tf_op jit(solution)/shard_map/while/body/eval_jaxpr/all_gather | solution.py:42
  102.2 187.9 %all-gather.42.cloned.1.call-start = ((), (), s32[]{:S(2)}) async-start(), calls=%async_computation.20 | async-start | bytes 2113536 | tf_op jit(solution)/shard_map/while/body/eval_jaxpr/all_gather | solution.py:29
  104.5 189.7 %all-gather.38.cloned.1.call-start = ((), (), s32[]{:S(2)}) async-start(), calls=%async_computation.18 | async-start | bytes 2113536 | tf_op jit(solution)/shard_map/while/body/eval_jaxpr/all_gather | solution.py:29
  146.0 31.0 %copy-start.13 = (bf16[680,1024,1]{1,0,2:T(8,128)(2,1)}, bf16[680,1024,1]{1,0,2:T(8,128)(2,1)S(1)}, u32[]{:S(2)}) copy-start(bf16[680,1024,1]{1,0,2:T(8,128)(2,1)S(1)} %reshape.509) | copy-start | bytes 4177924 | tf_op jit(solution)/shard_map/while
  253.7 4.1 collective-permute-start
  268.8 78.1 %all-gather.40.cloned.1.call-start = ((), (), s32[]{:S(2)}) async-start(), calls=%async_computation.19 | async-start | bytes 4456448 | tf_op jit(solution)/shard_map/while/body/eval_jaxpr/all_gather | solution.py:44
  269.5 128.6 %all-gather.44.cloned.1.call-start = ((), (), s32[]{:S(2)}) async-start(), calls=%async_computation.21 | async-start | bytes 4456448 | tf_op jit(solution)/shard_map/while/body/eval_jaxpr/all_gather | solution.py:46
  270.3 223.6 %all-gather.46.cloned.1.call-start = ((), (), s32[]{:S(2)}) async-start(), calls=%async_computation.22 | async-start | bytes 2113536 | tf_op jit(solution)/shard_map/while/body/eval_jaxpr/all_gather | solution.py:29
  398.1 11.0 copy-start.39
  436.0 12.8 slice-start
  436.9 12.0 copy-start.14
  436.9 12.0 slice-start.1
  436.9 12.0 copy-start.43
  436.9 20.1 %collective-permute-start.1 = (bf16[4,1024]{1,0:T(4,128)(2,1)S(1)}, bf16[4,1024]{1,0:T(4,128)(2,1)S(1)}, u32[]{:S(2)}, u32[]{:S(2)}) collective-permute-start(bf16[4,1024]{1,0:T(4,128)(2,1)S(1)} %slice.222), channel_id=1, source_target_pairs={{0,1},{2,3},{4,5},{6,7},{8,9},{10,11},{12,13},{14,15},{16,17},{18,... | collective-permute-start | bytes 24584 | tf_op jit(solution)/shard_map/while
  503.5 10.7 copy-start.5
  503.5 10.7 copy-start.10
  503.5 10.7 copy-start.11
  603.2 12.5 collective-permute-start.3
  606.1 14.4 collective-permute-start.2
  614.5 11.0 copy-start.1
  614.5 11.0 copy-start.19
  614.5 11.0 copy-start.23
  636.7 51.9 %all-gather.32.cloned.1.call-start = ((), (), s32[]{:S(2)}) async-start(), calls=%async_computation.15 | async-start | bytes 2113536 | tf_op jit(solution)/shard_map/while/body/eval_jaxpr/all_gather | solution.py:29
  642.8 73.0 %all-gather.34.cloned.1.call-start = ((), (), s32[]{:S(2)}) async-start(), calls=%async_computation.16 | async-start | bytes 3342336 | tf_op jit(solution)/shard_map/while/body/eval_jaxpr/all_gather | solution.py:40
  643.5 111.1 %all-gather.36.cloned.1.call-start = ((), (), s32[]{:S(2)}) async-start(), calls=%async_computation.17 | async-start | bytes 1114112 | tf_op jit(solution)/shard_map/while/body/eval_jaxpr/all_gather | solution.py:42
  644.1 188.5 %all-gather.42.cloned.1.call-start = ((), (), s32[]{:S(2)}) async-start(), calls=%async_computation.20 | async-start | bytes 2113536 | tf_op jit(solution)/shard_map/while/body/eval_jaxpr/all_gather | solution.py:29
  646.3 190.8 %all-gather.38.cloned.1.call-start = ((), (), s32[]{:S(2)}) async-start(), calls=%async_computation.18 | async-start | bytes 2113536 | tf_op jit(solution)/shard_map/while/body/eval_jaxpr/all_gather | solution.py:29
  690.2 29.8 %copy-start.13 = (bf16[680,1024,1]{1,0,2:T(8,128)(2,1)}, bf16[680,1024,1]{1,0,2:T(8,128)(2,1)S(1)}, u32[]{:S(2)}) copy-start(bf16[680,1024,1]{1,0,2:T(8,128)(2,1)S(1)} %reshape.509) | copy-start | bytes 4177924 | tf_op jit(solution)/shard_map/while
  796.9 4.1 collective-permute-start
  812.1 77.8 %all-gather.40.cloned.1.call-start = ((), (), s32[]{:S(2)}) async-start(), calls=%async_computation.19 | async-start | bytes 4456448 | tf_op jit(solution)/shard_map/while/body/eval_jaxpr/all_gather | solution.py:44
  812.6 128.3 %all-gather.44.cloned.1.call-start = ((), (), s32[]{:S(2)}) async-start(), calls=%async_computation.21 | async-start | bytes 4456448 | tf_op jit(solution)/shard_map/while/body/eval_jaxpr/all_gather | solution.py:46
  813.2 223.5 %all-gather.46.cloned.1.call-start = ((), (), s32[]{:S(2)}) async-start(), calls=%async_computation.22 | async-start | bytes 2113536 | tf_op jit(solution)/shard_map/while/body/eval_jaxpr/all_gather | solution.py:29
  941.0 11.0 copy-start.39
  978.8 12.9 slice-start
  979.7 12.0 copy-start.14
  979.7 12.0 slice-start.1
  979.7 12.0 copy-start.43
  979.7 20.1 %collective-permute-start.1 = (bf16[4,1024]{1,0:T(4,128)(2,1)S(1)}, bf16[4,1024]{1,0:T(4,128)(2,1)S(1)}, u32[]{:S(2)}, u32[]{:S(2)}) collective-permute-start(bf16[4,1024]{1,0:T(4,128)(2,1)S(1)} %slice.222), channel_id=1, source_target_pairs={{0,1},{2,3},{4,5},{6,7},{8,9},{10,11},{12,13},{14,15},{16,17},{18,... | collective-permute-start | bytes 24584 | tf_op jit(solution)/shard_map/while
  1046.3 10.7 copy-start.5
  1046.3 10.7 copy-start.10
  1046.3 10.7 copy-start.11
  1147.6 13.4 collective-permute-start.3
  1150.5 15.4 collective-permute-start.2
  1152.4 7.4 copy-start.30
  1152.4 8.1 copy-start.36
  1159.8 11.0 copy-start.1
  1159.8 11.0 copy-start.19
  1159.8 11.0 copy-start.23
  1188.1 13.2 reduce-scatter.18.cloned.1.call-start
  1188.7 152.7 %reduce-scatter.22.cloned.1.call-start = ((), (), s32[]{:S(2)}) async-start(), calls=%async_computation.10 | async-start | bytes 139264 | tf_op jit(solution)/shard_map/reduce_scatter | solution.py:349
  1202.9 139.8 %reduce-scatter.26.cloned.1.call-start = ((), (), s32[]{:S(2)}) async-start(), calls=%async_computation.12 | async-start | bytes 1114112 | tf_op jit(solution)/shard_map/reduce_scatter | solution.py:59
  1205.6 184.5 %reduce-scatter.24.cloned.1.call-start = ((), (), s32[]{:S(2)}) async-start(), calls=%async_computation.11 | async-start | bytes 3342336 | tf_op jit(solution)/shard_map/reduce_scatter | solution.py:53
  1211.1 254.6 %reduce-scatter.28.cloned.1.call-start = ((), (), s32[]{:S(2)}) async-start(), calls=%async_computation.13 | async-start | bytes 4456448 | tf_op jit(solution)/shard_map/reduce_scatter | solution.py:65
  1217.3 323.8 %reduce-scatter.30.cloned.1.call-start = ((), (), s32[]{:S(2)}) async-start(), calls=%async_computation.14 | async-start | bytes 4456448 | tf_op jit(solution)/shard_map/reduce_scatter | solution.py:71
  1224.7 404.9 %reduce-scatter.20.cloned.1.call-start = ((), (), s32[]{:S(2)}) async-start(), calls=%async_computation.9 | async-start | bytes 6684672 | tf_op jit(solution)/shard_map/reduce_scatter | solution.py:346
  1230.0 35.1 %copy-start.32 = (f32[2,8,64]{2,1,0:T(8,128)S(1)}, f32[2,8,64]{2,1,0:T(8,128)}, u32[]{:S(2)}) copy-start(f32[2,8,64]{2,1,0:T(8,128)} %get-tuple-element.647) | copy-start | bytes 12292
  1230.0 35.1 %copy-start.29 = (f32[2,8,64]{2,1,0:T(8,128)S(1)}, f32[2,8,64]{2,1,0:T(8,128)}, u32[]{:S(2)}) copy-start(f32[2,8,64]{2,1,0:T(8,128)} %get-tuple-element.650) | copy-start | bytes 12292
  1230.0 36.1 %copy-start.20 = (bf16[2,340,1024]{2,1,0:T(8,128)(2,1)S(1)}, bf16[2,340,1024]{2,1,0:T(8,128)(2,1)}, u32[]{:S(2)}) copy-start(bf16[2,340,1024]{2,1,0:T(8,128)(2,1)} %get-tuple-element.958) | copy-start | bytes 4177924
  1230.1 38.6 %copy-start.17 = (bf16[2,340,1024]{2,1,0:T(8,128)(2,1)S(1)}, bf16[2,340,1024]{2,1,0:T(8,128)(2,1)}, u32[]{:S(2)}) copy-start(bf16[2,340,1024]{2,1,0:T(8,128)(2,1)} %get-tuple-element.959) | copy-start | bytes 4177924
  (49 other events, 187.3 us)
Sparse Core Ops, SparseCore 0:
  10.2 64.9 all-gather.29
  101.0 23.9 all-gather.31
  127.2 45.4 all-gather.33
  174.7 36.7 all-gather.35
  212.9 39.0 all-gather.41
  268.9 25.0 all-gather.37
  296.1 50.7 all-gather.39
  349.1 49.0 all-gather.43
  470.9 22.9 all-gather.45
  642.9 25.4 all-gather.31
  670.6 45.1 all-gather.33
  717.8 36.7 all-gather.35
  756.2 39.1 all-gather.41
  812.2 24.8 all-gather.37
  839.1 50.7 all-gather.39
  891.9 49.0 all-gather.43
  1013.7 22.9 all-gather.45
  1191.4 9.8 reduce-scatter.17
  1205.3 55.0 reduce-scatter.21
  1263.9 56.5 reduce-scatter.25
  1324.8 65.2 reduce-scatter.23
  1394.4 71.2 reduce-scatter.27
  1469.6 71.4 reduce-scatter.29
  1545.3 84.2 reduce-scatter.19
where the time goes:
time: 1650 us; the launch traced here: 1640 us
  waiting for transfers between devices  593 us (36%)
  blocking collectives  433 us (26%)
  matrix products  259 us (16%)
  local copies, waits for them, and re-layouts  166 us (10%)
  other arithmetic  138 us (8%)
  starting transfers between devices  21.5 us (1%)
    while x6, blocking collectives  193 us
    all_gather x2, waiting for transfers between devices, fetch(): lax.all_gather(fc1_weight, 'dp', axis=0, tiled=True)  100 us
    reduce_scatter x1, waiting for transfers between devices, on_device(): lax.psum_scatter(ada_grad.astype(jnp.bfloat16), 'dp', scatter_dimension=0...  86.8 us
    all_gather x2, waiting for transfers between devices, fetch(): lax.all_gather(fc2_weight, 'dp', axis=1, tiled=True)  86.2 us
    while x170, local copies, waits for them, and re-layouts  81.9 us
    reduce_scatter x1, waiting for transfers between devices, settle(): lax.psum_scatter(fc1_part.astype(jnp.bfloat16), 'dp', scatter_dimension=0...  73.9 us
    reduce_scatter x1, waiting for transfers between devices, settle(): lax.psum_scatter(fc2_part.astype(jnp.bfloat16), 'dp', scatter_dimension=1...  73.6 us
    unnamed x1, blocking collectives  58.6 us
  transfers between devices with their start and end apart: 32, of which 15 were waited for; matrix products, arithmetic and copies ran while one was open for 22% of the time, Pallas kernels for 0%

commit v1 on v0

--- a/solution.py
+++ b/solution.py
@@ -1,7 +1,872 @@
+import functools
 import jax
 import jax.numpy as jnp
 from jax import lax
+from jax.experimental import pallas as pl
+from jax.experimental.pallas import tpu as pltpu
 from jax.sharding import PartitionSpec as P
+
+F32 = jnp.float32
+BF16 = jnp.bfloat16
+MESH = pl.DeviceIdType.MESH
+LOG2E = 1.4426950408889634
+VMEM_LIMIT = 60 * 1024 * 1024
+
+
+def mm(a, b):
+    return jnp.dot(a, b, preferred_element_type=F32)
+
+
+def mm_nt(a, b):
+    return lax.dot_general(a, b, (((1,), (1,)), ((), ())), preferred_element_type=F32)
+
+
+def mm_tn(a, b):
+    return lax.dot_general(a, b, (((0,), (0,)), ((), ())), preferred_element_type=F32)
+
+
+def norm_rows(values):
+    centre = jnp.mean(values, -1, keepdims=True)
+    shifted = values - centre
+    inverse = lax.rsqrt(jnp.mean(shifted * shifted, -1, keepdims=True) + 1e-06)
+    return shifted * inverse, inverse
+
+
+def norm_rows_back(incoming, normed, inverse):
+    return inverse * (
+        incoming
+        - jnp.mean(incoming, -1, keepdims=True)
+        - normed * jnp.mean(incoming * normed, -1, keepdims=True)
+    )
+
+
+def split_three(values):
+    high = values.astype(BF16)
+    rest = values - high.astype(F32)
+    middle = rest.astype(BF16)
+    return high, middle, (rest - middle.astype(F32)).astype(BF16)
+
+
+def forward_kernel(
+    heads, width, x_ref, mod_ref, wq_ref, wk_ref, wv_ref, wp_ref, bias_ref, vec_ref, boost_ref,
+    kmask_ref, qmask_ref,
+    mid_ref, att_ref, two_ref, ql_ref, kl_ref, vl_ref, mix_ref, stat_ref,
+    one_s, acc_s,
+):
+    step = pl.program_id(0)
+
+    @pl.when(step == 0)
+    def _():
+        normed, _ = norm_rows(x_ref[...].astype(F32))
+        one_s[...] = (normed * (1.0 + mod_ref[2:3]) + mod_ref[4:5]).astype(BF16)
+        acc_s[...] = jnp.zeros_like(acc_s)
+
+    one = one_s[...]
+    queries = mm(one, wq_ref[0]) + bias_ref[0:1]
+    keys = mm(one, wk_ref[0])
+    values = (mm(one, wv_ref[0]) + bias_ref[1:2]).astype(BF16)
+    vl_ref[...] = values
+    q_turned = queries.T
+    k_turned = keys.T
+    boost = boost_ref[0]
+    kmask = kmask_ref[...]
+    qmask = qmask_ref[...]
+    rows = q_turned.shape[1]
+    ones = jnp.ones((rows, width), BF16)
+    q_low, k_low, mixed = [], [], []
+    q_inv, k_inv, totals = [], [], []
+    for head in range(heads):
+        part = slice(head * width, (head + 1) * width)
+        q_now, k_now = q_turned[part], k_turned[part]
+        q_scale = lax.rsqrt(jnp.sum(q_now * q_now, 0, keepdims=True) + 1e-06)
+        k_scale = lax.rsqrt(jnp.sum(k_now * k_now, 0, keepdims=True) + 1e-06)
+        q_bf = (q_now * q_scale * boost[0:1, head : head + 1]).astype(BF16)
+        k_bf = (k_now * k_scale).astype(BF16)
+        scaled = q_bf.astype(F32) * LOG2E
+        high = scaled.astype(BF16)
+        rest = (scaled - high.astype(F32)).astype(BF16)
+        q_all = jnp.concatenate([high, rest, qmask], 0)
+        k_all = jnp.concatenate([k_bf, k_bf, kmask], 0)
+        weights = jnp.exp2(mm_tn(q_all, k_all)).astype(BF16)
+        v_all = jnp.concatenate([values[:, part], ones], 1)
+        summed = mm(weights, v_all)
+        total = summed[:, width:]
+        mixed.append((summed[:, :width] / total).astype(BF16))
+        totals.append(total[:, 0:1])
+        q_low.append(q_bf)
+        k_low.append(k_bf)
+        q_inv.append(q_scale)
+        k_inv.append(k_scale)
+    mixed_all = jnp.concatenate(mixed, 1)
+    mix_ref[...] = mixed_all
+    ql_ref[...] = jnp.concatenate(q_low, 0)
+    kl_ref[...] = jnp.concatenate(k_low, 0)
+    log_total = jnp.log2(jnp.concatenate(totals + totals, 1)).T
+    stat_ref[0, 0] = jnp.concatenate(q_inv + k_inv, 0)
+    stat_ref[0, 1] = log_total
+    acc_s[...] += mm_nt(mixed_all, wp_ref[0])
+
+    @pl.when(step == pl.num_programs(0) - 1)
+    def _():
+        attended = acc_s[...] + vec_ref[2:3]
+        att_ref[...] = attended.astype(BF16)
+        middle = x_ref[...].astype(F32) + mod_ref[0:1] * attended
+        mid_ref[...] = middle
+        normed, _ = norm_rows(middle)
+        two_ref[...] = (normed * (1.0 + mod_ref[3:4]) + mod_ref[5:6]).astype(BF16)
+
+
+def feed_kernel(
+    two_ref, mid_ref, cot_ref, mod_ref, vec_ref, w1_ref, w2_ref, b1_ref,
+    out_ref, gmid_ref, rows_ref, g1_ref, g2_ref, gb1_ref,
+    back_s, backt_s, twot_s, acc_s, gacc_s,
+):
+    step = pl.program_id(0)
+
+    @pl.when(step == 0)
+    def _():
+        back = (mod_ref[1:2] * cot_ref[...].astype(F32)).astype(BF16)
+        back_s[...] = back
+        backt_s[...] = back.T
+        twot_s[...] = two_ref[...].T
+        acc_s[...] = jnp.zeros_like(acc_s)
+        gacc_s[...] = jnp.zeros_like(gacc_s)
+
+    w1, w2 = w1_ref[0], w2_ref[0]
+    hidden = mm(two_ref[...], w1) + b1_ref[0:1]
+    square = hidden * hidden
+    curve = jnp.tanh(0.7978845608028654 * hidden * (1.0 + 0.044715 * square))
+    half = 0.5 * (1.0 + curve)
+    activated = (hidden * half).astype(BF16)
+    slope = half + 0.5 * hidden * (1.0 - curve * curve) * (
+        0.7978845608028654 * (1.0 + 0.134145 * square)
+    )
+    acc_s[...] += mm_nt(activated, w2)
+    g2_ref[0] = mm(backt_s[...], activated).astype(BF16)
+    hidden_grad = (mm(back_s[...], w2) * slope).astype(BF16)
+    g1_ref[0] = mm(twot_s[...], hidden_grad).astype(BF16)
+    gb1_ref[...] = jnp.broadcast_to(
+        jnp.sum(hidden_grad.astype(F32), 0, keepdims=True), gb1_ref.shape
+    )
+    gacc_s[...] += mm_nt(hidden_grad, w1)
+
+    @pl.when(step == pl.num_programs(0) - 1)
+    def _():
+        middle = mid_ref[...]
+        out_grad = cot_ref[...].astype(F32)
+        branch = acc_s[...] + vec_ref[3:4]
+        out_ref[...] = (middle + mod_ref[1:2] * branch).astype(BF16)
+        normed, inverse = norm_rows(middle)
+        grad = gacc_s[...]
+        gmid_ref[...] = out_grad + norm_rows_back(grad * (1.0 + mod_ref[3:4]), normed, inverse)
+        rows_ref[0:1] = jnp.sum(out_grad * branch, 0, keepdims=True)
+        rows_ref[1:2] = jnp.sum(grad * normed, 0, keepdims=True)
+        rows_ref[2:3] = jnp.sum(grad, 0, keepdims=True)
+        rows_ref[3:4] = jnp.sum(back_s[...].astype(F32), 0, keepdims=True)
+        rows_ref[4:8] = jnp.zeros((4, rows_ref.shape[1]), F32)
+
+
+def backward_kernel(
+    heads, width, levels, x_ref, gmid_ref, att_ref, mod_ref, ql_ref, kl_ref, vl_ref, mix_ref,
+    stat_ref, wq_ref, wk_ref, wv_ref, wp_ref, boost_ref, kmask_ref, qmask_ref,
+    tok_ref, rows_ref, gq_ref, gk_ref, gv_ref, gp_ref, sums_ref,
+    ga_s, gat_s, onet_s, acc_s,
+):
+    step = pl.program_id(0)
+
+    @pl.when(step == 0)
+    def _():
+        attend_grad = (mod_ref[0:1] * gmid_ref[...]).astype(BF16)
+        ga_s[...] = attend_grad
+        gat_s[...] = attend_grad.T
+        normed, _ = norm_rows(x_ref[...].astype(F32))
+        onet_s[...] = (normed * (1.0 + mod_ref[2:3]) + mod_ref[4:5]).astype(BF16).T
+        acc_s[...] = jnp.zeros_like(acc_s)
+        rows_ref[2:3] = jnp.sum(attend_grad.astype(F32), 0, keepdims=True)
+
+    gp_ref[0] = mm(gat_s[...], mix_ref[...]).astype(BF16)
+    mixed_grad = mm(ga_s[...], wp_ref[0]).astype(BF16)
+    mixed_turned = mixed_grad.T
+    v_turned = vl_ref[...].T
+    q_plain = ql_ref[...].T
+    boost = boost_ref[0]
+    kmask, qmask = kmask_ref[...], qmask_ref[...]
+    rows = kmask.shape[1]
+    place = lax.broadcasted_iota(jnp.int32, (16, rows), 0)
+
+    def pieces(row, first):
+        high, mid, low = split_three(row)
+        zero = jnp.zeros((16, rows), BF16)
+        out = jnp.where(place == first, jnp.broadcast_to(high, zero.shape), zero)
+        out = jnp.where(place == first + 1, jnp.broadcast_to(mid, zero.shape), out)
+        return jnp.where(place == first + 2, jnp.broadcast_to(low, zero.shape), out)
+
+    dq_rows, dk_rows, dv_cols, scales = [], [], [], []
+    for head in range(heads):
+        part = slice(head * width, (head + 1) * width)
+        lift = boost[0:1, head : head + 1]
+        q_bf, k_bf = ql_ref[part], kl_ref[part]
+        q_float = q_bf.astype(F32)
+        scaled = q_float * LOG2E
+        high = scaled.astype(BF16)
+        rest = (scaled - high.astype(F32)).astype(BF16)
+        log_total = stat_ref[0, 1, head : head + 1]
+        q_all = jnp.concatenate([high, rest, qmask + pieces(-log_total, levels + 1)], 0)
+        k_all = jnp.concatenate([k_bf, k_bf, kmask], 0)
+        soft = jnp.exp2(mm_tn(k_all, q_all))
+        product = soft * mm_tn(v_turned[part], mixed_turned[part])
+        delta = jnp.sum(product, 0, keepdims=True)
+        scores_grad = (product - soft * delta).astype(BF16)
+        dv_cols.append(mm(soft.astype(BF16), mixed_grad[:, part]))
+        dq_low = mm(k_bf, scores_grad)
+        dk_low = mm(scores_grad, q_plain[:, part]).T
+        q_inv = stat_ref[0, 0, head : head + 1]
+        k_inv = stat_ref[0, 0, heads + head : heads + head + 1]
+        q_unit = q_float * (1.0 / lift)
+        k_unit = k_bf.astype(F32)
+        along = dq_low * q_float
+        scales.append(jnp.broadcast_to(jnp.sum(along), (1, 128)))
+        dq_unit = dq_low * lift
+        dq_rows.append(q_inv * (dq_unit - q_unit * jnp.sum(along, 0, keepdims=True)))
+        dk_rows.append(k_inv * (dk_low - k_unit * jnp.sum(dk_low * k_unit, 0, keepdims=True)))
+    dq = jnp.concatenate(dq_rows, 0).T.astype(BF16)
+    dk = jnp.concatenate(dk_rows, 0).T.astype(BF16)
+    dv = jnp.concatenate(dv_cols, 1).astype(BF16)
+    one_turned = onet_s[...]
+    gq_ref[0] = mm(one_turned, dq).astype(BF16)
+    gk_ref[0] = mm(one_turned, dk).astype(BF16)
+    gv_ref[0] = mm(one_turned, dv).astype(BF16)
+    acc_s[...] += mm_nt(dq, wq_ref[0]) + mm_nt(dk, wk_ref[0]) + mm_nt(dv, wv_ref[0])
+    span = dq.shape[1]
+    sums_ref[0, 0:1, :] = jnp.sum(dq.astype(F32), 0, keepdims=True)
+    sums_ref[0, 1:2, :] = jnp.sum(dv.astype(F32), 0, keepdims=True)
+    sums_ref[0, 2:4, :] = jnp.zeros((2, span), F32)
+    for head in range(heads):
+        sums_ref[0, 4 + head : 5 + head, :] = jnp.broadcast_to(scales[head][:, 0:1], (1, span))
+
+    @pl.when(step == pl.num_programs(0) - 1)
+    def _():
+        grad = acc_s[...]
+        normed, inverse = norm_rows(x_ref[...].astype(F32))
+        middle_grad = gmid_ref[...]
+        tok_ref[...] = (
+            middle_grad + norm_rows_back(grad * (1.0 + mod_ref[2:3]), normed, inverse)
+        ).astype(BF16)
+        rows_ref[0:1] = jnp.sum(grad * normed, 0, keepdims=True)
+        rows_ref[1:2] = jnp.sum(grad, 0, keepdims=True)
+        rows_ref[3:4] = jnp.sum(middle_grad * att_ref[...].astype(F32), 0, keepdims=True)
+        rows_ref[4:8] = jnp.zeros((4, rows_ref.shape[1]), F32)
+
+
+def whole(shape):
+    return pl.BlockSpec(shape, lambda g: (0,) * len(shape))
+
+
+def run_forward(x, mods, qkv, projt, vecs, boosts, kmask, qmask, width=64):
+    rows, model = x.shape
+    heads = 256 // width
+    groups = model // 256
+    per = qkv.shape[2] // 3 // 256
+    half = lambda base: pl.BlockSpec((1, model, 256), lambda g: (g // per, 0, base * per + g % per))
+    return pl.pallas_call(
+        functools.partial(forward_kernel, heads, width),
+        grid=(groups,),
+        in_specs=[
+            whole(x.shape), whole(mods.shape), half(0), half(1), half(2), half(0),
+            pl.BlockSpec((8, 256), lambda g: (0, g)), whole(vecs.shape),
+            pl.BlockSpec((1, 8, 128), lambda g: (g, 0, 0)), whole(kmask.shape), whole(qmask.shape),
+        ],
+        out_shape=[
+            jax.ShapeDtypeStruct((rows, model), F32),
+            jax.ShapeDtypeStruct((rows, model), BF16),
+            jax.ShapeDtypeStruct((rows, model), BF16),
+            jax.ShapeDtypeStruct((model, rows), BF16),
+            jax.ShapeDtypeStruct((model, rows), BF16),
+            jax.ShapeDtypeStruct((rows, model), BF16),
+            jax.ShapeDtypeStruct((rows, model), BF16),
+            jax.ShapeDtypeStruct((groups, 2, 8, rows), F32),
+        ],
+        out_specs=[
+            whole((rows, model)), whole((rows, model)), whole((rows, model)),
+            pl.BlockSpec((256, rows), lambda g: (g, 0)),
+            pl.BlockSpec((256, rows), lambda g: (g, 0)),
+            pl.BlockSpec((rows, 256), lambda g: (0, g)),
+            pl.BlockSpec((rows, 256), lambda g: (0, g)),
+            pl.BlockSpec((1, 2, 8, rows), lambda g: (g, 0, 0, 0)),
+        ],
+        scratch_shapes=[pltpu.VMEM((rows, model), BF16), pltpu.VMEM((rows, model), F32)],
+        compiler_params=pltpu.CompilerParams(vmem_limit_bytes=VMEM_LIMIT),
+        name="attend",
+    )(x, mods, qkv, qkv, qkv, projt, vecs, vecs, boosts, kmask, qmask)
+
+
+def run_feed(two, middle, cot, mods, vecs, fc1, fc2t, b1, block=512):
+    rows, model = two.shape
+    cols = fc1.shape[2]
+    per = cols // block
+    steps = 2 * per
+    weight = pl.BlockSpec((1, model, block), lambda g: (g // per, 0, g % per))
+    return pl.pallas_call(
+        feed_kernel,
+        grid=(steps,),
+        in_specs=[
+            whole(two.shape), whole(middle.shape), whole(cot.shape), whole(mods.shape), whole(vecs.shape),
+            weight, weight, pl.BlockSpec((8, block), lambda g: (0, g)),
+        ],
+        out_shape=[
+            jax.ShapeDtypeStruct((rows, model), BF16),
+            jax.ShapeDtypeStruct((rows, model), F32),
+            jax.ShapeDtypeStruct((8, model), F32),
+            jax.ShapeDtypeStruct(fc1.shape, BF16),
+            jax.ShapeDtypeStruct(fc2t.shape, BF16),
+            jax.ShapeDtypeStruct((8, 2 * cols), F32),
+        ],
+        out_specs=[
+            whole((rows, model)), whole((rows, model)), whole((8, model)), weight, weight,
+            pl.BlockSpec((8, block), lambda g: (0, g)),
+        ],
+        scratch_shapes=[
+            pltpu.VMEM((rows, model), BF16), pltpu.VMEM((model, rows), BF16), pltpu.VMEM((model, rows), BF16),
+            pltpu.VMEM((rows, model), F32), pltpu.VMEM((rows, model), F32),
+        ],
+        compiler_params=pltpu.CompilerParams(vmem_limit_bytes=VMEM_LIMIT),
+        name="feed",
+    )(two, middle, cot, mods, vecs, fc1, fc2t, b1)
+
+
+def run_backward(levels, x, gmid, att, mods, saved, qkv, projt, boosts, kmask, qmask, width=64):
+    q_low, k_low, v_low, mixed, stats = saved
+    rows, model = x.shape
+    heads = 256 // width
+    groups = model // 256
+    per = qkv.shape[2] // 3 // 256
+    half = lambda base: pl.BlockSpec((1, model, 256), lambda g: (g // per, 0, base * per + g % per))
+    turned = pl.BlockSpec((256, rows), lambda g: (g, 0))
+    plain = pl.BlockSpec((rows, 256), lambda g: (0, g))
+    grad = jax.ShapeDtypeStruct(projt.shape, BF16)
+    return pl.pallas_call(
+        functools.partial(backward_kernel, heads, width, levels),
+        grid=(groups,),
+        in_specs=[
+            whole(x.shape), whole(gmid.shape), whole(att.shape), whole(mods.shape),
+            turned, turned, plain, plain, pl.BlockSpec((1, 2, 8, rows), lambda g: (g, 0, 0, 0)),
+            half(0), half(1), half(2), half(0),
+            pl.BlockSpec((1, 8, 128), lambda g: (g, 0, 0)), whole(kmask.shape), whole(qmask.shape),
+        ],
+        out_shape=[
+            jax.ShapeDtypeStruct((rows, model), BF16), jax.ShapeDtypeStruct((8, model), F32),
+            grad, grad, grad, grad, jax.ShapeDtypeStruct((groups, 8, 256), F32),
+        ],
+        out_specs=[
+            whole((rows, model)), whole((8, model)), half(0), half(0), half(0), half(0),
+            pl.BlockSpec((1, 8, 256), lambda g: (g, 0, 0)),
+        ],
+        scratch_shapes=[
+            pltpu.VMEM((rows, model), BF16), pltpu.VMEM((model, rows), BF16), pltpu.VMEM((model, rows), BF16),
+            pltpu.VMEM((rows, model), F32),
+        ],
+        compiler_params=pltpu.CompilerParams(vmem_limit_bytes=VMEM_LIMIT),
+        name="attend_back",
+    )(x, gmid, att, mods, q_low, k_low, v_low, mixed, stats, qkv, qkv, qkv, projt, boosts, kmask, qmask)
+
+
+def build_masks(lengths, half_rows, padded):
+    count = lengths.shape[0]
+    steps = jnp.arange(count, dtype=jnp.int32)
+    ends = jnp.sum(jnp.where(steps[None, :] <= steps[:, None], lengths[None, :], 0), 1)
+    place = jnp.arange(2 * padded, dtype=jnp.int32)
+    part, inside = place // padded, place % padded
+    token = part * half_rows + inside
+    level = jnp.sum((token[None, :] >= ends[:, None]).astype(jnp.int32), 0)
+    real = inside < half_rows
+    entry = jnp.arange(16, dtype=jnp.int32)[:, None]
+    key_level = jnp.where(real, level, count)[None]
+    kmask = (entry == key_level) | ((entry > count) & (entry < count + 4))
+    query_level = jnp.where(real, level, count - 1)[None]
+    qmask = (entry > query_level) & (entry <= count)
+    return kmask.astype(BF16), jnp.where(qmask, -32768.0, 0.0).astype(BF16)
+
+
+def where_am_i():
+    dp, y = lax.axis_index("dp"), lax.axis_index("mp")
+    return dp // 4, (dp // 2) % 2, dp % 2, y
+
+
+def device(z, x, c, y):
+    return (z * 4 + x * 2 + c, y)
+
+
+def greet(line, z, x, c, y):
+    barrier = pltpu.get_barrier_semaphore()
+
+    def signal(target):
+        pl.semaphore_signal(barrier, inc=1, device_id=target, device_id_type=MESH)
+
+    signal(device(z, x, 1 - c, y))
+    signal(device(z, 1 - x, c, y))
+    signal(device(z, x, c, 1 - y))
+
+    @pl.when(z > 0)
+    def _():
+        signal(device(z - 1, x, c, y))
+
+    @pl.when(z < line - 1)
+    def _():
+        signal(device(z + 1, x, c, y))
+
+    ends = (z == 0).astype(jnp.int32) + (z == line - 1).astype(jnp.int32)
+    pl.semaphore_wait(barrier, 5 - ends)
+
+
+def run_ticks(count, stages):
+    for tick in range(count + len(stages) - 1):
+        for at, stage in enumerate(stages):
+            if 0 <= tick - at < count:
+                stage(tick - at)
+
+
+def gather_kernel(chunks, line, n_seg, n_pair, *refs):
+    ins, pair_in = refs[:n_seg], refs[n_seg : n_seg + n_pair]
+    outs = refs[n_seg + n_pair : 2 * n_seg + n_pair]
+    pair_out = refs[2 * n_seg + n_pair : 2 * (n_seg + n_pair)]
+    local_sem, pair_local, pair_send, pair_recv, z_send, z_recv, send_sem, recv_sem = refs[2 * (n_seg + n_pair) :]
+    z, x, c, y = where_am_i()
+    own = [pltpu.make_async_copy(i, o.at[y, z, x, c], local_sem.at[s]) for s, (i, o) in enumerate(zip(ins, outs))]
+    for copy in own:
+        copy.start()
+    greet(line, z, x, c, y)
+    pairs = []
+    for p in range(n_pair):
+        pairs.append(pltpu.make_async_copy(pair_in[p].at[y], pair_out[p].at[y], pair_local.at[p]))
+        pairs.append(
+            pltpu.make_async_remote_copy(
+                pair_in[p].at[1 - y], pair_out[p].at[y], pair_send.at[p], pair_recv.at[p],
+                device_id=device(z, x, c, 1 - y), device_id_type=MESH,
+            )
+        )
+    for copy in own:
+        copy.wait()
+
+    def hop(k, way, j):
+        seg, _, start, cols = chunks[k]
+        out, step = outs[seg], 1 - 2 * way
+        going, coming = z - step * j, z - step * (j + 1)
+        sends = (going >= 0) & (going < line) & (z + step >= 0) & (z + step < line)
+        receives = (coming >= 0) & (coming < line)
+
+        def copy(owner):
+            ref = out.at[y, owner, x, c, :, pl.ds(start, cols)]
+            return pltpu.make_async_remote_copy(
+                ref, ref, z_send.at[k, way, j], z_recv.at[k, way, j],
+                device_id=device(z + step, x, c, y), device_id_type=MESH,
+            )
+
+        return sends, (lambda: copy(going)), receives, (lambda: copy(coming))
+
+    def group(k, slot, yy, xx, target):
+        seg, _, start, cols = chunks[k]
+        ref = outs[seg].at[yy, :, xx, c, :, pl.ds(start, cols)]
+        return pltpu.make_async_remote_copy(
+            ref, ref, send_sem.at[k, slot], recv_sem.at[k, slot], device_id=target, device_id_type=MESH
+        )
+
+    x_side, y_side, sibling = device(z, 1 - x, c, y), device(z, x, c, 1 - y), device(z, x, 1 - c, y)
+
+    def groups(k):
+        if chunks[k][1] == 0:
+            return [(y, x), (y, 1 - x), (1 - y, x), (1 - y, 1 - x)], x_side, y_side
+        return [(y, x), (1 - y, x), (y, 1 - x), (1 - y, 1 - x)], y_side, x_side
+
+    def z_stage(j):
+        def stage(k):
+            for way in range(2):
+                if j > 0:
+                    _, _, receives, landed = hop(k, way, j - 1)
+
+                    @pl.when(receives)
+                    def _():
+                        landed().wait_recv()
+
+                if j < line - 1:
+                    sends, copy, _, _ = hop(k, way, j)
+
+                    @pl.when(sends)
+                    def _():
+                        copy().start()
+
+        return stage
+
+    def first_stage(k):
+        order, first, second = groups(k)
+        group(k, 0, *order[0], first).start()
+        group(k, 1, *order[0], second).start()
+        group(k, 3, *order[0], sibling).start()
+
+    def second_stage(k):
+        order, first, second = groups(k)
+        group(k, 0, *order[1], first).wait_recv()
+        group(k, 2, *order[1], second).start()
+        group(k, 4, *order[1], sibling).start()
+
+    def last_stage(k):
+        order, first, second = groups(k)
+        group(k, 1, *order[2], second).wait_recv()
+        group(k, 5, *order[2], sibling).start()
+        group(k, 2, *order[3], second).wait_recv()
+        group(k, 6, *order[3], sibling).start()
+
+    def first_with_pairs(k):
+        first_stage(k)
+        if k == 1:
+            for copy in pairs:
+                copy.start()
+
+    def z_last_and_first(k):
+        z_stage(line - 1)(k)
+        first_with_pairs(k)
+
+    run_ticks(len(chunks), [z_stage(j) for j in range(line - 1)] + [z_last_and_first, second_stage, last_stage])
+    for copy in pairs:
+        copy.wait()
+    for k in range(len(chunks)):
+        order, first, second = groups(k)
+        for way in range(2):
+            for j in range(line - 1):
+                sends, copy, _, _ = hop(k, way, j)
+
+                @pl.when(sends)
+                def _():
+                    copy().wait_send()
+
+        for slot, at in ((0, 0), (1, 0), (2, 1), (3, 0), (4, 1), (5, 2), (6, 3)):
+            group(k, slot, *order[at], sibling).wait_send()
+        for slot, at in ((3, 0), (4, 1), (5, 2), (6, 3)):
+            group(k, slot, *order[at], sibling).wait_recv()
+
+
+def run_gather(chunks, segments, pairs, line, collective_id):
+    n_seg, n_pair, count = len(segments), len(pairs), len(chunks)
+    anywhere = pl.BlockSpec(memory_space=pl.ANY)
+    made = pl.pallas_call(
+        functools.partial(gather_kernel, chunks, line, n_seg, n_pair),
+        out_shape=[jax.ShapeDtypeStruct((2, line, 2, 2) + s.shape, s.dtype) for s in segments]
+        + [jax.ShapeDtypeStruct(p.shape, p.dtype) for p in pairs],
+        in_specs=[anywhere] * (n_seg + n_pair),
+        out_specs=[anywhere] * (n_seg + n_pair),
+        scratch_shapes=[
+            pltpu.SemaphoreType.DMA((n_seg,)), pltpu.SemaphoreType.DMA((n_pair,)),
+            pltpu.SemaphoreType.DMA((n_pair,)), pltpu.SemaphoreType.DMA((n_pair,)),
+            pltpu.SemaphoreType.DMA((count, 2, line - 1)), pltpu.SemaphoreType.DMA((count, 2, line - 1)),
+            pltpu.SemaphoreType.DMA((count, 7)), pltpu.SemaphoreType.DMA((count, 7)),
+        ],
+        compiler_params=pltpu.CompilerParams(collective_id=collective_id, has_side_effects=True),
+        name="gather_weights",
+    )(*segments, *pairs)
+    return made[:n_seg], made[n_seg:]
+
+
+def add_into(target, source, pieces, target_at, source_at):
+    def body(i, carry):
+        t, s = target_at(i), source_at(i)
+        target[t] = target[t] + source[s]
+        return carry
+
+    lax.fori_loop(0, pieces, body, 0)
+
+
+def scatter_kernel(chunks, line, n_seg, n_pair, *refs):
+    count = len(chunks)
+    ins, pair_in = refs[:n_seg], refs[n_seg : n_seg + n_pair]
+    outs = refs[n_seg + n_pair : 2 * n_seg + n_pair]
+    pair_out = refs[2 * n_seg + n_pair : 2 * (n_seg + n_pair)]
+    rest = refs[2 * (n_seg + n_pair) :]
+    core_b, first_b, second_b, up_b, down_b, own_b = (rest[i * count : (i + 1) * count] for i in range(6))
+    pair_local, pair_send, pair_recv, own_sem, send_sem, recv_sem, z_send, z_recv = rest[6 * count :]
+    z, x, c, y = where_am_i()
+    x_side, y_side, sibling = device(z, 1 - x, c, y), device(z, x, c, 1 - y), device(z, x, 1 - c, y)
+    greet(line, z, x, c, y)
+
+    def remote(source, target, send, recv, to):
+        return pltpu.make_async_remote_copy(source, target, send, recv, device_id=to, device_id_type=MESH)
+
+    pairs = []
+    for p in range(n_pair):
+        pairs.append(pltpu.make_async_copy(pair_in[p].at[y], pair_out[p].at[y], pair_local.at[p]))
+        pairs.append(remote(pair_in[p].at[1 - y], pair_out[p].at[y], pair_send.at[p], pair_recv.at[p], y_side))
+
+    def core_copy(k):
+        seg, _, start, cols = chunks[k]
+        source = ins[seg].at[:, :, :, 1 - c, :, pl.ds(start, cols)]
+        return remote(source, core_b[k], send_sem.at[k, 0], recv_sem.at[k, 0], sibling)
+
+    def own_copy(k):
+        seg, _, start, cols = chunks[k]
+        return pltpu.make_async_copy(ins[seg].at[:, :, :, c, :, pl.ds(start, cols)], own_b[k], own_sem.at[k])
+
+    def first_copy(k):
+        if chunks[k][1] == 0:
+            return remote(core_b[k].at[1 - y], first_b[k], send_sem.at[k, 1], recv_sem.at[k, 1], y_side)
+        return remote(core_b[k].at[:, :, 1 - x], first_b[k], send_sem.at[k, 1], recv_sem.at[k, 1], x_side)
+
+    def second_copy(k):
+        if chunks[k][1] == 0:
+            return remote(first_b[k].at[:, 1 - x], second_b[k], send_sem.at[k, 2], recv_sem.at[k, 2], x_side)
+        return remote(first_b[k].at[1 - y], second_b[k], send_sem.at[k, 2], recv_sem.at[k, 2], y_side)
+
+    def line_copy(k, way, owner):
+        landing = (up_b, down_b)[way][k]
+        return remote(
+            second_b[k].at[owner], landing.at[owner], z_send.at[k, way, owner], z_recv.at[k, way, owner],
+            device(z + 1 - 2 * way, x, c, y),
+        )
+
+    def core_stage(k):
+        core_copy(k).start()
+        own_copy(k).start()
+
+    def first_stage(k):
+        core_copy(k).wait_recv()
+        own_copy(k).wait()
+        at = lambda i: (i // (2 * line), (i // 2) % line, i % 2)
+        add_into(core_b[k], own_b[k], 4 * line, at, at)
+        first_copy(k).start()
+
+    def second_stage(k):
+        first_copy(k).wait_recv()
+        if chunks[k][1] == 0:
+            add_into(first_b[k], core_b[k], 2 * line, lambda i: (i // 2, i % 2), lambda i: (y, i // 2, i % 2))
+        else:
+            add_into(first_b[k], core_b[k], 2 * line, lambda i: (i // line, i % line), lambda i: (i // line, i % line, x))
+        second_copy(k).start()
+
+    def third_stage(k):
+        second_copy(k).wait_recv()
+        if chunks[k][1] == 0:
+            add_into(second_b[k], first_b[k], line, lambda i: (i,), lambda i: (i, x))
+        else:
+            add_into(second_b[k], first_b[k], line, lambda i: (i,), lambda i: (y, i))
+
+    def line_stage(j):
+        def stage(k):
+            if j == 0:
+                third_stage(k)
+            for way in range(2):
+                place = j if way == 0 else line - 1 - j
+                owners = range(line - 1, place, -1) if way == 0 else range(place)
+
+                @pl.when(z == place)
+                def _():
+                    for owner in owners:
+                        if j > 0:
+                            line_copy(k, way, owner).wait_recv()
+                            second_b[k][owner] = second_b[k][owner] + (up_b, down_b)[way][k][owner]
+                        line_copy(k, way, owner).start()
+
+        return stage
+
+    def last_stage(k):
+        seg, _, start, cols = chunks[k]
+        total = second_b[k].at[z]
+        outs[seg][:, pl.ds(start, cols)] = total[...].astype(F32)
+        for way in range(2):
+
+            @pl.when((z > 0) if way == 0 else (z < line - 1))
+            def _():
+                line_copy(k, way, z).wait_recv()
+                part = (up_b, down_b)[way][k][z]
+                outs[seg][:, pl.ds(start, cols)] += part.astype(F32)
+
+    def core_with_pairs(k):
+        core_stage(k)
+        if k == 1:
+            for copy in pairs:
+                copy.start()
+
+    run_ticks(count, [core_with_pairs, first_stage, second_stage] + [line_stage(j) for j in range(line - 1)] + [last_stage])
+    for copy in pairs:
+        copy.wait()
+    for k in range(count):
+        core_copy(k).wait_send()
+        first_copy(k).wait_send()
+        second_copy(k).wait_send()
+        for way in range(2):
+            for owner in range(line):
+
+                @pl.when((z < owner) if way == 0 else (z > owner))
+                def _():
+                    line_copy(k, way, owner).wait_send()
+
+
+def run_scatter(chunks, segments, pairs, line, collective_id):
+    n_seg, n_pair, count = len(segments), len(pairs), len(chunks)
+    anywhere = pl.BlockSpec(memory_space=pl.ANY)
+    inside = pl.BlockSpec(memory_space=pltpu.VMEM)
+    core_b, first_b, second_b, own_b = [], [], [], []
+    for seg, kind, _, cols in chunks:
+        rows = segments[seg].shape[4]
+        core_b.append(pltpu.VMEM((2, line, 2, rows, cols), BF16))
+        first_b.append(pltpu.VMEM(((line, 2) if kind == 0 else (2, line)) + (rows, cols), BF16))
+        second_b.append(pltpu.VMEM((line, rows, cols), BF16))
+        own_b.append(pltpu.VMEM((2, line, 2, rows, cols), BF16))
+    made = pl.pallas_call(
+        functools.partial(scatter_kernel, chunks, line, n_seg, n_pair),
+        out_shape=[jax.ShapeDtypeStruct(s.shape[4:], F32) for s in segments]
+        + [jax.ShapeDtypeStruct(p.shape, p.dtype) for p in pairs],
+        in_specs=[anywhere] * (n_seg + n_pair),
+        out_specs=[inside] * n_seg + [anywhere] * n_pair,
+        scratch_shapes=core_b + first_b + second_b + second_b + second_b + own_b
+        + [
+            pltpu.SemaphoreType.DMA((n_pair,)), pltpu.SemaphoreType.DMA((n_pair,)), pltpu.SemaphoreType.DMA((n_pair,)),
+            pltpu.SemaphoreType.DMA((count,)),
+            pltpu.SemaphoreType.DMA((count, 3)), pltpu.SemaphoreType.DMA((count, 3)),
+            pltpu.SemaphoreType.DMA((count, 2, line)), pltpu.SemaphoreType.DMA((count, 2, line)),
+        ],
+        compiler_params=pltpu.CompilerParams(
+            collective_id=collective_id, has_side_effects=True, vmem_limit_bytes=60 * 1024 * 1024
+        ),
+        name="scatter_grads",
+    )(*segments, *pairs)
+    return made[:n_seg], made[n_seg:]
+
+
+def pad_rows(values, padded):
+    return jnp.pad(values, ((0, 0), (0, padded - values.shape[1]), (0, 0)))
+
+
+def chunk_list():
+    return [(0, 0, 0, 128), (2, 0, 0, 256), (2, 1, 256, 256), (1, 0, 0, 768), (1, 1, 768, 768)] + [
+        (segment, part % 2, part * 512, 512) for segment in (3, 4) for part in range(4)
+    ]
+
+
+def scatter_list():
+    return [(segment, part % 2, part * 512, 512) for segment in (6, 5) for part in range(4)] + [
+        (segment, part, part * 256, 256) for segment in (4, 1, 2, 3) for part in range(2)
+    ] + [(0, 0, 0, 128)]
+
+
+def on_device_paired(
+    tokens, condition, scale_lengths, order, cotangent, ada_weight, ada_bias, qkv_weight, qv_bias,
+    head_log_scale, proj_weight, out_bias, fc1_weight, fc1_bias, fc2_weight,
+):
+    n_dp, mine = lax.axis_size("dp"), lax.axis_index("mp")
+    line = n_dp // 4
+    slots, half_rows, model = tokens.shape
+    padded = -(-half_rows // 16) * 16
+    rows = 2 * padded
+    local_heads, width = qv_bias.shape[1], 64
+    own_cols = qkv_weight.shape[2]
+    own_rows = qkv_weight.shape[1]
+    hidden_cols = fc1_weight.shape[1]
+    groups = 2 * own_cols // 256
+    swap = order[0, 0] != 0
+
+    def to_slots(values):
+        return jnp.where(swap, values[::-1], values)
+
+    scale_parts = split_three(head_log_scale)
+    small = jnp.concatenate(
+        [qv_bias.reshape(-1), out_bias.reshape(-1), fc1_bias.reshape(-1)] + list(scale_parts)
+    )
+    small = jnp.pad(small, (0, 16 * 128 - small.shape[0])).reshape(16, 128)
+    segments = [
+        small,
+        jnp.concatenate([qkv_weight[0], qkv_weight[1], qkv_weight[2]], 1),
+        proj_weight.T,
+        fc1_weight,
+        fc2_weight.T,
+    ]
+    full, pair = run_gather(
+        chunk_list(), segments, [pad_rows(to_slots(tokens), padded), pad_rows(cotangent, padded)], line, 1
+    )
+    small_full = full[0].reshape(2, n_dp, 16 * 128)
+    qkv, projt, fc1, fc2t = (f.reshape(2, model, f.shape[-1]) for f in full[1:])
+    x, cot = (p.reshape(rows, model) for p in pair)
+    entries = qv_bias.shape[2]
+    vectors = (2 + 2) * local_heads + fc1_bias.shape[0]
+    spread_small = small_full[:, :, : vectors * entries].reshape(2, n_dp, vectors, entries)
+    spread_small = spread_small.transpose(0, 2, 1, 3).reshape(2, vectors, n_dp * entries).astype(F32)
+    block_rows = spread_small[:, : 4 * local_heads].reshape(2, 4, own_cols).transpose(1, 0, 2).reshape(4, model)
+    vecs = jnp.pad(block_rows, ((0, 4), (0, 0)))
+    hidden_bias = jnp.broadcast_to(spread_small[:, 4 * local_heads :].reshape(1, 2 * hidden_cols), (8, 2 * hidden_cols))
+    scale_at = vectors * entries
+    scale_all = sum(
+        small_full[:, 0, scale_at + i * local_heads : scale_at + (i + 1) * local_heads].astype(F32) for i in range(3)
+    )
+    boost = jnp.exp(scale_all.reshape(groups, -1))
+    boosts = jnp.zeros((groups, 8, 128), F32).at[:, 0, : boost.shape[1]].set(boost)
+
+    cond_slots = to_slots(condition).astype(F32)
+    signal = jax.nn.silu(cond_slots).astype(BF16)
+    signal_rows = lax.all_to_all(
+        signal.reshape(slots, n_dp, own_rows).transpose(1, 0, 2), "dp", 0, 0, tiled=True
+    ).reshape(n_dp * slots, own_rows)
+    ada_flat = ada_weight.reshape(own_rows, 6 * own_cols)
+    bias_own = lax.dynamic_update_slice(
+        jnp.zeros((6, local_heads, width), F32), ada_bias.astype(F32), (0, 0, lax.axis_index("dp") * ada_bias.shape[2])
+    )
+    products = jnp.dot(signal_rows, ada_flat, preferred_element_type=F32) + bias_own.reshape(1, 6 * own_cols)
+    arrived = lax.all_to_all(products, ("dp", "mp"), 0, 0, tiled=True)
+    modulation = arrived.reshape(n_dp, 2, 6, own_cols).sum(0).transpose(1, 0, 2).reshape(6, model)
+    mods = jnp.pad(modulation, ((0, 2), (0, 0)))
+
+    lengths = lax.dynamic_index_in_dim(to_slots(scale_lengths), mine, 0, keepdims=False)
+    kmask, qmask = build_masks(lengths, half_rows, padded)
+    middle, attended, two, q_low, k_low, v_low, mixed, stats = run_forward(
+        x, mods, qkv, projt, vecs, boosts, kmask, qmask, width
+    )
+    result, grad_middle, feed_rows, g_fc1, g_fc2t, g_hidden = run_feed(
+        two, middle, cot, mods, vecs, fc1, fc2t, hidden_bias
+    )
+    token_grad, back_rows, g_q, g_k, g_v, g_projt, sums = run_backward(
+        scale_lengths.shape[1], x, grad_middle, attended, mods, (q_low, k_low, v_low, mixed, stats), qkv, projt,
+        boosts, kmask, qmask, width,
+    )
+
+    bias_grads = jnp.stack([sums[:, 0].reshape(model), sums[:, 1].reshape(model), back_rows[2], feed_rows[3]])
+    bias_grads = bias_grads.reshape(4, 2, local_heads, n_dp, entries).transpose(1, 3, 0, 2, 4)
+    hidden_grads = g_hidden[0].reshape(2, fc1_bias.shape[0], n_dp, entries).transpose(0, 2, 1, 3)
+    scale_grads = jnp.broadcast_to(sums[:, 4:, 0].reshape(2, 1, local_heads), (2, n_dp, local_heads))
+    small_grads = jnp.concatenate(
+        [bias_grads.reshape(2, n_dp, -1), hidden_grads.reshape(2, n_dp, -1), scale_grads], 2
+    ).astype(BF16)
+    small_grads = jnp.pad(small_grads, ((0, 0), (0, 0), (0, 16 * 128 - small_grads.shape[2])))
+    owned = [g.reshape(2, line, 2, 2, own_rows, g.shape[-1]) for g in (g_q, g_k, g_v, g_projt, g_fc1, g_fc2t)]
+    totals, halves = run_scatter(
+        scatter_list(), [small_grads.reshape(2, line, 2, 2, 16, 128)] + owned,
+        [t.reshape(2, padded, model) for t in (result, token_grad)], line, 2,
+    )
+    small_total = totals[0].reshape(-1)
+    bias_total = small_total[: 4 * local_heads * entries].reshape(2, 2, local_heads, entries)
+    hidden_total = small_total[4 * local_heads * entries : scale_at].reshape(fc1_bias.shape)
+    scale_total = small_total[scale_at : scale_at + local_heads]
+    qkv_total = jnp.stack(totals[1:4])
+    activations = halves[0][:, :half_rows]
+    tokens_grad = to_slots(halves[1][:, :half_rows])
+
+    grad_mods = jnp.stack(
+        [back_rows[3], feed_rows[0], back_rows[0], feed_rows[1], back_rows[1], feed_rows[2]]
+    ).reshape(6, 2, own_cols).transpose(1, 0, 2)
+    both = lax.all_to_all(grad_mods, "mp", 0, 0, tiled=True)
+    all_mods = lax.all_gather(both, "dp", axis=0, tiled=True).reshape(n_dp * slots, 6 * own_cols)
+    ada_weight_grad = lax.dot_general(
+        signal_rows.astype(F32), all_mods, (((0,), (0,)), ((), ())), precision=precise, preferred_element_type=F32
+    ).reshape(ada_weight.shape)
+    ada_bias_grad = lax.dynamic_slice_in_dim(
+        jnp.sum(all_mods, 0).reshape(6, local_heads, width), lax.axis_index("dp") * entries, entries, 2
+    )
+    signal_part = lax.dot_general(
+        all_mods, ada_flat.astype(F32), (((1,), (1,)), ((), ())), precision=precise, preferred_element_type=F32
+    )
+    signal_part = lax.psum(signal_part, "mp").reshape(n_dp, slots, own_rows)
+    signal_grad = lax.all_to_all(signal_part, "dp", 0, 0, tiled=True).transpose(1, 0, 2).reshape(slots, model)
+    pull = jax.vjp(jax.nn.silu, cond_slots)[1]
+    condition_grad = to_slots(pull(signal_grad)[0]).astype(BF16)
+    return (
+        activations, tokens_grad, condition_grad, ada_weight_grad, ada_bias_grad, qkv_total, bias_total[0],
+        scale_total, totals[4].T, bias_total[1], totals[5], hidden_total, totals[6].T,
+    )
+
 
 precise = lax.Precision.HIGHEST
 
@@ -74,7 +939,7 @@
     )
 
 
-def on_device(
+def on_device_shared(
     tokens,
     condition,
     scale_lengths,
@@ -146,7 +1011,8 @@
             jnp.float32
         )
         qkv_full, qv_full, proj_full, outb_full, fc1_full, fc1b_full, fc2_full = rows_now()
-        scale_ends = jnp.cumsum(lengths)
+        steps = jnp.arange(lengths.shape[0], dtype=jnp.int32)
+        scale_ends = jnp.sum(jnp.where(steps[None, :] <= steps[:, None], lengths[None, :], 0), 1)
         scale_of = jnp.sum((positions[:, None] >= scale_ends[None, :]).astype(jnp.int32), 1)
         allowed = (scale_of[None, :] <= scale_of[:, None])[None]
         normed_one, inverse_one = row_norm(residual)
@@ -402,6 +1268,8 @@
         P("mp", "dp"),
         P("mp", "dp"),
     )
+    line, spare = divmod(mesh.shape["dp"], 4)
+    paired = mesh.shape["mp"] == 2 and spare == 0 and line > 1
     return jax.shard_map(
-        on_device, mesh=mesh, in_specs=in_specs, out_specs=out_specs, check_vma=False
-    )
+        on_device_paired if paired else on_device_shared, mesh=mesh, in_specs=in_specs, out_specs=out_specs, check_vma=False
+    )

time: 1650 us -> 594 us (0.36)
  waiting for transfers between devices: 593 us -> 15.2 us
  Pallas kernels: 0 us -> 471 us
  blocking collectives: 433 us -> 28.2 us
  matrix products: 259 us -> 2.39 us
  other arithmetic: 138 us -> 8.42 us
  local copies, waits for them, and re-layouts: 166 us -> 43.4 us
    pallas_call x0 -> x5, Pallas kernels: none -> 471 us  [the longest x1 178 us: run_gather(): pl.pallas_call(functools.partial(gather_kernel, chunks, line, n_seg, n_pa...]
    all_gather x17 -> x0, waiting for transfers between devices: 294 us -> none  [the longest x2 100 us: fetch(): lax.all_gather(fc1_weight, 'dp', axis=0, tiled=True)]
    reduce_scatter x7 -> x0, waiting for transfers between devices: 293 us -> none  [the longest x1 86.8 us: on_device(): lax.psum_scatter(ada_grad.astype(jnp.bfloat16), 'dp', scatter_dimension=0...]
    dot_general x39 -> x3, matrix products: 259 us -> 2.39 us  [the longest x1 1.6 us: on_device_paired(): lax.dot_general(signal_rows.astype(F32), all_mods, (((0,), (0,)), ((), ()...]
    while x6 -> x0, blocking collectives: 193 us -> none
    all_gather x8 -> x1, blocking collectives: 143 us -> 21.1 us  [on_device_paired(): lax.all_gather(both, 'dp', axis=0, tiled=True)]
    while x173 -> x0, local copies, waits for them, and re-layouts: 97.4 us -> none
    unnamed x1 -> x0, blocking collectives: 58.6 us -> none
  transfers between devices with their start and end apart: 32 -> 4, of which waited for: 15 -> 2; matrix products, arithmetic and copies ran while one was open for 22% -> 5% of each run, Pallas kernels for 0% -> 58%
where the time goes in v1:
time: 594 us; the launch traced here: 588 us
  Pallas kernels  471 us (79%)
  local copies, waits for them, and re-layouts  43.4 us (7%)
  blocking collectives  28.2 us (5%)
  starting transfers between devices  17.6 us (3%)
  waiting for transfers between devices  15.2 us (3%)
  other arithmetic  8.42 us (1%)
    pallas_call x1, Pallas kernels, run_gather(): pl.pallas_call(functools.partial(gather_kernel, chunks, line, n_seg, n_pa...  178 us
    pallas_call x1, Pallas kernels, run_scatter(): pl.pallas_call(functools.partial(scatter_kernel, chunks, line, n_seg, n_p...  162 us
    pallas_call x1, Pallas kernels, run_feed(): pl.pallas_call(feed_kernel, grid=(steps,), in_specs=[whole(two.shape), wh...  53.3 us
    pallas_call x1, Pallas kernels, run_backward(): pl.pallas_call(functools.partial(backward_kernel, heads, width, levels),...  49.2 us
    pallas_call x1, Pallas kernels, run_forward(): pl.pallas_call(functools.partial(forward_kernel, heads, width), grid=(gro...  27.5 us
    all_gather x1, blocking collectives, on_device_paired(): lax.all_gather(both, 'dp', axis=0, tiled=True)  21.1 us
    unnamed x44, local copies, waits for them, and re-layouts  17 us
  transfers between devices with their start and end apart: 4, of which 2 were waited for; matrix products, arithmetic and copies ran while one was open for 5% of the time, Pallas kernels for 58%

profile of v1, /device:TPU:0, one launch (start us, length us, event | category | flops | bytes accessed | tf_op | source)
XLA Modules:
  0.0 588.1 jit_solution(2204412261115036591)
XLA Ops:
  0.6 2.7 rev.16
  4.0 0.7 fusion.18
  4.8 0.6 copy.198
  5.5 7.4 %all-to-all-start = ((bf16[16,2,64]{2,1,0:T(2,128)(2,1)}), bf16[16,2,64]{2,1,0:T(2,128)(2,1)S(1)}, u32[]{:S(2)}, u32[]{:S(2)}) async-start(bf16[16,2,64]{2,1,0:T(2,128)(2,1)} %bitcast.90), calls=%async_computation | async-start | bytes 16384 | tf_op jit(solution)/shard_map/all_to_all | solution.py:801
  12.8 0.9 slice_bitcast_fusion.2
  13.7 0.7 subtract_convert_fusion
  14.5 0.8 copy.142
  15.4 0.8 copy.140
  16.2 0.8 copy.141
  17.2 0.6 pad_bitcast_fusion.refs_0_
  17.8 1.7 copy.143
  19.9 1.0 copy-done.1
  21.3 1.3 pad.29.refs_5_
  22.5 1.2 pad.30.refs_6_
  23.8 0.7 pad_maximum_fusion.1.refs_1_
  24.5 178.4 %gather_weights.1 = (bf16[2,4,2,2,16,128]{5,4,3,2,1,0:T(8,128)(2,1)}, bf16[2,4,2,2,64,1536]{5,4,3,2,1,0:T(8,128)(2,1)}, bf16[2,4,2,2,64,512]{5,4,3,2,1,0:T(8,128...) custom-call(bf16[16,128]{1,0:T(8,128)(2,1)} %pad_bitcast_fusion.refs, ...), custom_call_target="tpu_custom_call" | custom-call | tf_op jit(solution)/shard_map/gather_weights/pallas_call | solution.py:550
  202.9 1.0 reshape.309
  204.9 0.6 scatter.4.boost_ref
  205.5 0.6 pad.32.bias_ref.vec_ref
  206.9 1.2 copy.149
  208.1 3.5 all-to-all-start.1
  211.7 0.7 fusion.12.kmask_ref
  212.3 0.7 select_convert_fusion.qmask_ref
  213.0 11.4 %all-to-all-done.1 = f32[32,1,3072]{2,1,0:T(1,128)S(1)} async-done(((f32[32,1,3072]{2,1,0:T(1,128)}), f32[32,1,3072]{2,1,0:T(1,128)S(1)}, u32[]{:S(2)}, u32[]{:S(2)}) %all-to-all-start.1) | async-done | bytes 393248 | tf_op jit(solution)/shard_map/all_to_all | solution.py:809
  224.4 0.9 reduce.3
  225.6 0.6 pad.31.mod_ref
  226.2 27.5 %attend.1 = (f32[704,1024]{1,0:T(8,128)}, bf16[704,1024]{1,0:T(8,128)(2,1)}, bf16[704,1024]{1,0:T(8,128)(2,1)}, bf16[1024,704]{1,0:T(8,128)(2,1)}, bf16[1024,704...) custom-call(bf16[704,1024]{1,0:T(8,128)(2,1)} %bitcast.105, ...), custom_call_target="tpu_custom_call" | custom-call | tf_op jit(solution)/shard_map/attend/pallas_call | solution.py:271
  253.7 0.7 broadcast_in_dim.64.b1_ref
  254.4 53.3 %feed.1 = (bf16[704,1024]{1,0:T(8,128)(2,1)}, f32[704,1024]{1,0:T(8,128)}, f32[8,1024]{1,0:T(8,128)}, bf16[2,1024,2048]{2,1,0:T(8,128)(2,1)}, bf16[2,1024,2048]{2,1,0:T(8,128)(2,1)}, /*index=5*/f32[8,4096]{1,0:T(8,128)}) custom-call(bf16[704,1024]{1,0:T(8,128)(2,1)} %get-tuple-element.66.two_ref, f32[704,1024]{1,0:T(8,128)} %get-tuple-element.67.mid_ref, ...), custom_call_target="tpu_custom_call" | custom-call | tf_op jit(solution)/shard_map/feed/pallas_call | solution.py:309
  307.7 49.2 %attend_back.1 = (bf16[704,1024]{1,0:T(8,128)(2,1)}, f32[8,1024]{1,0:T(8,128)}, bf16[2,1024,512]{2,1,0:T(8,128)(2,1)}, bf16[2,1024,512]{2,1,0:T(8,128)(2,1)}, bf...) custom-call(bf16[704,1024]{1,0:T(8,128)(2,1)} %bitcast.106, ...), custom_call_target="tpu_custom_call" | custom-call | tf_op jit(solution)/shard_map/attend_back/pallas_call | solution.py:347
  356.9 0.8 convert.35
  357.7 0.8 fusion.24
  358.5 0.8 fusion.26
  359.3 0.9 fusion.35
  361.8 1.0 fusion.14
  362.8 0.6 reshape_squeeze.5
  364.0 0.7 copy.182
  364.6 0.7 stack.31
  365.3 3.3 all-to-all-start.2
  368.6 162.5 %scatter_grads.1 = (f32[16,128]{1,0:T(8,128)}, f32[64,512]{1,0:T(8,128)}, f32[64,512]{1,0:T(8,128)}, f32[64,512]{1,0:T(8,128)}, f32[64,512]{1,0:T(8,128)}, /*ind...) custom-call(bf16[2,4,2,2,16,128]{5,4,3,2,1,0:T(8,128)(2,1)} %bitcast.119, ...), custom_call_target="tpu_custom_call" | custom-call | tf_op jit(solution)/shard_map/scatter_grads/pallas_call | solution.py:711
  531.0 1.5 slice.136
  532.9 0.8 slice_reduce_fusion.3
  533.7 0.8 pad_maximum_fusion
  534.5 0.8 slice_reduce_fusion.2
  535.3 2.5 copy.171
  538.0 2.5 copy.170
  540.6 0.7 copy.175
  541.3 0.7 copy.173
  542.1 0.7 copy.174
  542.8 1.2 slice.158
  544.0 21.1 %all_gather.3 = f32[32,6,512]{2,1,0:T(8,128)S(1)} all-gather(f32[2,6,512]{2,1,0:T(8,128)S(1)} %all-to-all-done.2), channel_id=1, replica_groups=mesh['dp'=16,'mp'=2] {'dp'}, dimensions={0}, use_global_device_ids=true | all-gather | bytes 417792 | tf_op jit(solution)/shard_map/all_gather | solution.py:851
  565.1 0.6 fusion.4
  565.7 7.1 %psum.7 = f32[16,2,64]{2,1,0:T(2,128)S(1)} all-reduce(f32[16,2,64]{2,1,0:T(2,128)S(1)} %bitcast.134), channel_id=1, replica_groups=mesh['dp'=16,'mp'=2] {'mp'}, use_global_device_ids=true, to_apply=%region_3.4 | all-reduce | flops 2048 | bytes 16384 | tf_op jit(solution)/shard_map/psum | solution.py:861
  572.9 0.7 reshape.362
  573.6 3.5 all-to-all-start.3
  577.1 1.6 fusion.1
  578.8 0.7 copy.172
  579.5 3.8 all-to-all-done.3
  583.3 0.5 broadcast.185
  583.9 0.7 reduce.28
  585.0 0.6 select_convert_fusion.1
  585.6 0.7 copy.203
  586.3 0.8 copy.204
  587.1 0.8 copy.205
  (93 shorter events, 6.8 us)
Async XLA Ops:
  5.5 201.3 %all-to-all-start = ((bf16[16,2,64]{2,1,0:T(2,128)(2,1)}), bf16[16,2,64]{2,1,0:T(2,128)(2,1)S(1)}, u32[]{:S(2)}, u32[]{:S(2)}) async-start(bf16[16,2,64]{2,1,0:T(2,128)(2,1)} %bitcast.90), calls=%async_computation | async-start | bytes 16384 | tf_op jit(solution)/shard_map/all_to_all | solution.py:801
  19.5 1.3 copy-start.1
  24.5 179.9 %copy-start.12 = (s32[2,10]{1,0:T(2,128)S(1)}, s32[2,10]{1,0:T(2,128)}, u32[]{:S(2)}) copy-start(s32[2,10]{1,0:T(2,128)} %param.19) | copy-start | bytes 244
  202.9 3.2 copy-start.11
  202.9 3.7 copy-start
  208.1 16.3 %all-to-all-start.1 = ((f32[32,1,3072]{2,1,0:T(1,128)}), f32[32,1,3072]{2,1,0:T(1,128)S(1)}, u32[]{:S(2)}, u32[]{:S(2)}) async-start(f32[32,1,3072]{2,1,0:T(1,128)} %copy.149), calls=%async_computation.1 | async-start | bytes 786432 | tf_op jit(solution)/shard_map/all_to_all | solution.py:809
  307.7 51.5 %copy-start.10 = (f32[8,1024]{1,0:T(8,128)S(1)}, f32[8,1024]{1,0:T(8,128)}, u32[]{:S(2)}) copy-start(f32[8,1024]{1,0:T(8,128)} %get-tuple-element.80) | copy-start | bytes 98308
  365.3 178.7 %all-to-all-start.2 = ((f32[2,6,512]{2,1,0:T(8,128)}), f32[2,6,512]{2,1,0:T(8,128)S(1)}, u32[]{:S(2)}, u32[]{:S(2)}) async-start(f32[2,6,512]{2,1,0:T(8,128)} %bitcast.38), calls=%async_computation.2 | async-start | bytes 65536 | tf_op jit(solution)/shard_map/all_to_all | solution.py:850
  532.5 1.2 copy-start.6
  532.5 1.2 copy-start.7
  532.5 1.2 copy-start.8
  534.5 3.3 copy-start.2
  565.1 19.6 %copy-start.9 = (bf16[2,1024]{1,0:T(2,128)(2,1)S(1)}, bf16[2,1024]{1,0:T(2,128)(2,1)}, u32[]{:S(2)}) copy-start(bf16[2,1024]{1,0:T(2,128)(2,1)} %param.18) | copy-start | bytes 12292
  565.1 20.5 %copy-start.5 = (f32[64,512]{1,0:T(8,128)S(1)}, f32[64,512]{1,0:T(8,128)}, u32[]{:S(2)}) copy-start(f32[64,512]{1,0:T(8,128)} %get-tuple-element.96) | copy-start | bytes 393220
  565.1 21.2 %copy-start.4 = (f32[64,2048]{1,0:T(8,128)S(1)}, f32[64,2048]{1,0:T(8,128)}, u32[]{:S(2)}) copy-start(f32[64,2048]{1,0:T(8,128)} %get-tuple-element.213) | copy-start | bytes 1572868
  565.7 21.3 %copy-start.3 = (f32[64,2048]{1,0:T(8,128)S(1)}, f32[64,2048]{1,0:T(8,128)}, u32[]{:S(2)}) copy-start(f32[64,2048]{1,0:T(8,128)} %get-tuple-element.98) | copy-start | bytes 1572868
  573.6 9.8 %all-to-all-start.3 = ((f32[16,1,128]{2,1,0:T(1,128)}), f32[16,1,128]{2,1,0:T(1,128)S(1)}, u32[]{:S(2)}, u32[]{:S(2)}) async-start(f32[16,1,128]{2,1,0:T(1,128)} %reshape.362), calls=%async_computation.3 | async-start | bytes 16384 | tf_op jit(solution)/shard_map/all_to_all | solution.py:862

commit v2 on v0

--- a/solution.py
+++ b/solution.py
@@ -1,7 +1,1025 @@
+import functools
 import jax
 import jax.numpy as jnp
 from jax import lax
+from jax.experimental import pallas as pl
+from jax.experimental.pallas import tpu as pltpu
 from jax.sharding import PartitionSpec as P
+
+F32 = jnp.float32
+BF16 = jnp.bfloat16
+MESH = pl.DeviceIdType.MESH
+LOG2E = 1.4426950408889634
+VMEM_LIMIT = 60 * 1024 * 1024
+
+
+def mm(a, b):
+    return jnp.dot(a, b, preferred_element_type=F32)
+
+
+def mm_nt(a, b):
+    return lax.dot_general(a, b, (((1,), (1,)), ((), ())), preferred_element_type=F32)
+
+
+def mm_tn(a, b):
+    return lax.dot_general(a, b, (((0,), (0,)), ((), ())), preferred_element_type=F32)
+
+
+def norm_rows(values):
+    centre = jnp.mean(values, -1, keepdims=True)
+    shifted = values - centre
+    inverse = lax.rsqrt(jnp.mean(shifted * shifted, -1, keepdims=True) + 1e-06)
+    return shifted * inverse, inverse
+
+
+def norm_rows_back(incoming, normed, inverse):
+    return inverse * (
+        incoming
+        - jnp.mean(incoming, -1, keepdims=True)
+        - normed * jnp.mean(incoming * normed, -1, keepdims=True)
+    )
+
+
+def split_three(values):
+    high = values.astype(BF16)
+    rest = values - high.astype(F32)
+    middle = rest.astype(BF16)
+    return high, middle, (rest - middle.astype(F32)).astype(BF16)
+
+
+def build_masks(lengths, half_rows, padded):
+    count = lengths.shape[0]
+    steps = jnp.arange(count, dtype=jnp.int32)
+    ends = jnp.sum(jnp.where(steps[None, :] <= steps[:, None], lengths[None, :], 0), 1)
+    place = jnp.arange(2 * padded, dtype=jnp.int32)
+    part, inside = place // padded, place % padded
+    token = part * half_rows + inside
+    level = jnp.sum((token[None, :] >= ends[:, None]).astype(jnp.int32), 0)
+    real = inside < half_rows
+    entry = jnp.arange(16, dtype=jnp.int32)[:, None]
+    key_level = jnp.where(real, level, count)[None]
+    kmask = (entry == key_level) | ((entry > count) & (entry < count + 4))
+    query_level = jnp.where(real, level, count - 1)[None]
+    qmask = (entry > query_level) & (entry <= count)
+    return kmask.astype(BF16), jnp.where(qmask, -32768.0, 0.0).astype(BF16)
+
+
+def device(z, x, c, y):
+    return (z * 4 + x * 2 + c, y)
+
+
+def where_am_i():
+    dp, y = lax.axis_index("dp"), lax.axis_index("mp")
+    return dp // 4, (dp // 2) % 2, dp % 2, y
+
+
+def remote(source, target, send, recv, to):
+    return pltpu.make_async_remote_copy(source, target, send, recv, device_id=to, device_id_type=MESH)
+
+
+def greet_all(total):
+    me = lax.axis_index("dp") * 2 + lax.axis_index("mp")
+    barrier = pltpu.get_barrier_semaphore()
+
+    def signal(step, carry):
+        to = lax.rem(me + step, total)
+        pl.semaphore_signal(barrier, inc=1, device_id=(to // 2, to % 2), device_id_type=MESH)
+        return carry
+
+    lax.fori_loop(1, total, signal, 0)
+    pl.semaphore_wait(barrier, total - 1)
+
+
+class Exchange:
+    def __init__(self, total, block_of, landing, send, recv):
+        self.total, self.block_of, self.landing, self.send, self.recv = total, block_of, landing, send, recv
+        self.me = lax.axis_index("dp") * 2 + lax.axis_index("mp")
+
+    def copy(self, step):
+        to = lax.rem(self.me + step, self.total)
+        return remote(
+            self.block_of(to), self.landing.at[self.me], self.send.at[step], self.recv.at[step], (to // 2, to % 2)
+        )
+
+    def own(self):
+        return pltpu.make_async_copy(self.block_of(self.me), self.landing.at[self.me], self.send.at[0])
+
+    def each(self, act):
+        def body(step, carry):
+            act(self.copy(step))
+            return carry
+
+        lax.fori_loop(1, self.total, body, 0)
+
+    def start(self):
+        self.own().start()
+        self.each(lambda copy: copy.start())
+
+    def wait(self):
+        self.own().wait()
+        self.each(lambda copy: copy.wait())
+
+
+class Ticks:
+    def __init__(self, count, stages):
+        self.count, self.stages = count, stages
+        self.total = count + len(stages) - 1
+
+    def run(self, since, until):
+        for tick in range(since, until):
+            for at, stage in enumerate(self.stages):
+                if 0 <= tick - at < self.count:
+                    stage(tick - at)
+
+
+class Gather:
+    def __init__(self, chunks, line, outs, z_send, z_recv, send_sem, recv_sem):
+        self.chunks, self.line, self.outs = chunks, line, outs
+        self.z_send, self.z_recv, self.send_sem, self.recv_sem = z_send, z_recv, send_sem, recv_sem
+        self.z, self.x, self.c, self.y = where_am_i()
+        z, x, c, y = self.z, self.x, self.c, self.y
+        self.x_side, self.y_side, self.sibling = device(z, 1 - x, c, y), device(z, x, c, 1 - y), device(z, x, 1 - c, y)
+
+    def hop(self, k, way, j):
+        seg, _, start, cols = self.chunks[k]
+        z, x, c, y, line = self.z, self.x, self.c, self.y, self.line
+        step = 1 - 2 * way
+        going, coming = z - step * j, z - step * (j + 1)
+        sends = (going >= 0) & (going < line) & (z + step >= 0) & (z + step < line)
+        receives = (coming >= 0) & (coming < line)
+
+        def copy(owner):
+            ref = self.outs[seg].at[y, owner, x, c, :, pl.ds(start, cols)]
+            return remote(ref, ref, self.z_send.at[k, way, j], self.z_recv.at[k, way, j], device(z + step, x, c, y))
+
+        return sends, (lambda: copy(going)), receives, (lambda: copy(coming))
+
+    def group(self, k, slot, at, target):
+        seg, _, start, cols = self.chunks[k]
+        ref = self.outs[seg].at[at[0], :, at[1], self.c, :, pl.ds(start, cols)]
+        return remote(ref, ref, self.send_sem.at[k, slot], self.recv_sem.at[k, slot], target)
+
+    def groups(self, k):
+        x, y = self.x, self.y
+        if self.chunks[k][1] == 0:
+            return [(y, x), (y, 1 - x), (1 - y, x), (1 - y, 1 - x)], self.x_side, self.y_side
+        return [(y, x), (1 - y, x), (y, 1 - x), (1 - y, 1 - x)], self.y_side, self.x_side
+
+    def line_stage(self, j):
+        def stage(k):
+            for way in range(2):
+                if j > 0:
+                    _, _, receives, landed = self.hop(k, way, j - 1)
+
+                    @pl.when(receives)
+                    def _():
+                        landed().wait_recv()
+
+                if j < self.line - 1:
+                    sends, copy, _, _ = self.hop(k, way, j)
+
+                    @pl.when(sends)
+                    def _():
+                        copy().start()
+
+        return stage
+
+    def first_stage(self, k):
+        self.line_stage(self.line - 1)(k)
+        order, first, second = self.groups(k)
+        self.group(k, 0, order[0], first).start()
+        self.group(k, 1, order[0], second).start()
+        self.group(k, 3, order[0], self.sibling).start()
+
+    def second_stage(self, k):
+        order, first, second = self.groups(k)
+        self.group(k, 0, order[1], first).wait_recv()
+        self.group(k, 2, order[1], second).start()
+        self.group(k, 4, order[1], self.sibling).start()
+
+    def last_stage(self, k):
+        order, first, second = self.groups(k)
+        self.group(k, 1, order[2], second).wait_recv()
+        self.group(k, 5, order[2], self.sibling).start()
+        self.group(k, 2, order[3], second).wait_recv()
+        self.group(k, 6, order[3], self.sibling).start()
+
+    def stages(self):
+        return [self.line_stage(j) for j in range(self.line - 1)] + [self.first_stage, self.second_stage, self.last_stage]
+
+    def finish(self, k):
+        order, _, _ = self.groups(k)
+        for slot, at in ((3, 0), (4, 1), (5, 2), (6, 3)):
+            self.group(k, slot, order[at], self.sibling).wait_recv()
+
+    def sent(self):
+        for k in range(len(self.chunks)):
+            order, _, _ = self.groups(k)
+            for way in range(2):
+                for j in range(self.line - 1):
+                    sends, copy, _, _ = self.hop(k, way, j)
+
+                    @pl.when(sends)
+                    def _():
+                        copy().wait_send()
+
+            for slot, at in ((0, 0), (1, 0), (2, 1), (3, 0), (4, 1), (5, 2), (6, 3)):
+                self.group(k, slot, order[at], self.sibling).wait_send()
+
+
+def add_into(target, source, pieces, target_at, source_at):
+    def body(i, carry):
+        t, s = target_at(i), source_at(i)
+        target[t] = target[t] + source[s]
+        return carry
+
+    lax.fori_loop(0, pieces, body, 0)
+
+
+class Scatter:
+    def __init__(self, chunks, line, sources, totals, landing, core_s, own_s, first_b, second_b, line_b, sems):
+        self.chunks, self.line, self.sources, self.totals = chunks, line, sources, totals
+        self.landing, self.core_s, self.own_s = landing, core_s, own_s
+        self.first_b, self.second_b, self.line_b = first_b, second_b, line_b
+        self.own_sem, self.load_sem, self.send_sem, self.recv_sem, self.z_send, self.z_recv = sems
+        self.z, self.x, self.c, self.y = where_am_i()
+        z, x, c, y = self.z, self.x, self.c, self.y
+        self.x_side, self.y_side, self.sibling = device(z, 1 - x, c, y), device(z, x, c, 1 - y), device(z, x, 1 - c, y)
+
+    def core_copy(self, k):
+        seg, _, start, cols = self.chunks[k]
+        source = self.sources[seg].at[:, :, :, 1 - self.c, :, pl.ds(start, cols)]
+        return remote(source, self.landing[k], self.send_sem.at[k, 0], self.recv_sem.at[k, 0], self.sibling)
+
+    def core(self, k):
+        return self.core_s.at[k % 3, :, :, :, :, pl.ds(0, self.chunks[k][3])]
+
+    def own(self, k):
+        return self.own_s.at[k % 2, :, :, :, :, pl.ds(0, self.chunks[k][3])]
+
+    def own_copy(self, k):
+        seg, _, start, cols = self.chunks[k]
+        source = self.sources[seg].at[:, :, :, self.c, :, pl.ds(start, cols)]
+        return pltpu.make_async_copy(source, self.own(k), self.own_sem.at[k])
+
+    def load_copy(self, k):
+        return pltpu.make_async_copy(self.landing[k], self.core(k), self.load_sem.at[k])
+
+    def first_copy(self, k):
+        core, sems = self.core(k), (self.send_sem.at[k, 1], self.recv_sem.at[k, 1])
+        if self.chunks[k][1] == 0:
+            return remote(core.at[1 - self.y], self.first_b[k], *sems, self.y_side)
+        return remote(core.at[:, :, 1 - self.x], self.first_b[k], *sems, self.x_side)
+
+    def second_copy(self, k):
+        first, sems = self.first_b[k], (self.send_sem.at[k, 2], self.recv_sem.at[k, 2])
+        if self.chunks[k][1] == 0:
+            return remote(first.at[:, 1 - self.x], self.second_b[k], *sems, self.x_side)
+        return remote(first.at[1 - self.y], self.second_b[k], *sems, self.y_side)
+
+    def line_copy(self, k, way, owner):
+        to = device(self.z + 1 - 2 * way, self.x, self.c, self.y)
+        return remote(
+            self.second_b[k].at[owner], self.line_b[k].at[owner + 1 - way],
+            self.z_send.at[k, way, owner], self.z_recv.at[k, way, owner], to,
+        )
+
+    def core_stage(self, k):
+        self.core_copy(k).start()
+
+    def load_stage(self, k):
+        self.core_copy(k).wait_recv()
+        self.load_copy(k).start()
+        self.own_copy(k).start()
+
+    def first_stage(self, k):
+        line = self.line
+        self.load_copy(k).wait()
+        self.own_copy(k).wait()
+        at = lambda i: (i // (2 * line), (i // 2) % line, i % 2)
+        add_into(self.core(k), self.own(k), 4 * line, at, at)
+        self.first_copy(k).start()
+
+    def second_stage(self, k):
+        line, x, y = self.line, self.x, self.y
+        self.first_copy(k).wait_recv()
+        if self.chunks[k][1] == 0:
+            add_into(self.first_b[k], self.core(k), 2 * line, lambda i: (i // 2, i % 2), lambda i: (y, i // 2, i % 2))
+        else:
+            add_into(
+                self.first_b[k], self.core(k), 2 * line,
+                lambda i: (i // line, i % line), lambda i: (i // line, i % line, x),
+            )
+        self.second_copy(k).start()
+        self.first_copy(k).wait_send()
+
+    def third_stage(self, k):
+        x, y = self.x, self.y
+        self.second_copy(k).wait_recv()
+        if self.chunks[k][1] == 0:
+            add_into(self.second_b[k], self.first_b[k], self.line, lambda i: (i,), lambda i: (i, x))
+        else:
+            add_into(self.second_b[k], self.first_b[k], self.line, lambda i: (i,), lambda i: (y, i))
+
+    def line_stage(self, j):
+        def stage(k):
+            if j == 0:
+                self.third_stage(k)
+            for way in range(2):
+                place = j if way == 0 else self.line - 1 - j
+                owners = range(self.line - 1, place, -1) if way == 0 else range(place)
+
+                @pl.when(self.z == place)
+                def _():
+                    for owner in owners:
+                        if j > 0:
+                            self.line_copy(k, way, owner).wait_recv()
+                            self.second_b[k][owner] = self.second_b[k][owner] + self.line_b[k][owner + 1 - way]
+                        self.line_copy(k, way, owner).start()
+
+        return stage
+
+    def last_stage(self, k):
+        seg, _, start, cols = self.chunks[k]
+        z = self.z
+        total = self.totals[seg]
+        total[:, pl.ds(start, cols)] = self.second_b[k][z].astype(F32)
+        for way in range(2):
+
+            @pl.when((z > 0) if way == 0 else (z < self.line - 1))
+            def _():
+                self.line_copy(k, way, z).wait_recv()
+                total[:, pl.ds(start, cols)] += self.line_b[k][z + 1 - way].astype(F32)
+
+    def stages(self):
+        return (
+            [self.core_stage, self.load_stage, self.first_stage, self.second_stage]
+            + [self.line_stage(j) for j in range(self.line - 1)]
+            + [self.last_stage]
+        )
+
+    def sent(self):
+        for k in range(len(self.chunks)):
+            self.core_copy(k).wait_send()
+            self.second_copy(k).wait_send()
+            for way in range(2):
+                for owner in range(self.line):
+
+                    @pl.when((self.z < owner) if way == 0 else (self.z > owner))
+                    def _():
+                        self.line_copy(k, way, owner).wait_send()
+
+
+def switch_on(index, cases):
+    for at, act in cases.items():
+        pl.when(index == at)(act)
+
+
+def columns(start, size):
+    return pl.ds(pl.multiple_of(start, 128), size)
+
+
+def ahead_kernel(chunks, line, width, *refs):
+    (products, seg_qkv, seg_proj, seg_fc1, seg_fc2, tok, cot, vecs, hidden_bias, boosts, kmask_ref, qmask_ref,
+     qkv_f, proj_f, fc1_f, fc2_f, x_f, cot_f, g1_f, g2_f,
+     mod_ref, ql_ref, kl_ref, vl_ref, mix_ref, stat_ref, out_ref, gmid_ref, rows_ref, gb1_ref,
+     arrived, att_ref, x_s, cot_s, one_s, acc_s, mid_s, twot_s, back_s, backt_s, gacc_s, w_s, grad_s,
+     a_send, a_recv, local_sem, pair_sem, z_send, z_recv, send_sem, recv_sem, load_sem, w_sem, grad_sem) = refs
+    z, x, c, y = where_am_i()
+    total = 8 * line
+    padded, model = tok.shape[1], tok.shape[2]
+    half_cols = mod_ref.shape[1] // 2
+    heads = 256 // width
+    outs = [qkv_f, proj_f, fc1_f, fc2_f]
+    own = [
+        pltpu.make_async_copy(i, o.at[y, z, x, c], local_sem.at[s])
+        for s, (i, o) in enumerate(zip([seg_qkv, seg_proj, seg_fc1, seg_fc2], outs))
+    ]
+    for copy in own:
+        copy.start()
+    mine, others = pl.ds(y * padded, padded), pl.ds((1 - y) * padded, padded)
+    pairs = []
+    for p, (source, target, inside) in enumerate(((tok, x_f, x_s), (cot, cot_f, cot_s))):
+        partner = device(z, x, c, 1 - y)
+        pairs.append((
+            pltpu.make_async_copy(source.at[y], target.at[mine], pair_sem.at[p, 0]),
+            remote(source.at[1 - y], target.at[mine], pair_sem.at[p, 1], pair_sem.at[p, 2], partner),
+            pltpu.make_async_copy(target, inside, pair_sem.at[p, 3]),
+        ))
+    exchange = Exchange(total, lambda to: products.at[to], arrived, a_send, a_recv)
+    gather = Gather(chunks, line, outs, z_send, z_recv, send_sem, recv_sem)
+    ticks = Ticks(len(chunks), gather.stages())
+    greet_all(total)
+    exchange.start()
+    for copy in pairs[0][:2]:
+        copy.start()
+    for copy in own:
+        copy.wait()
+
+    def load_attend(i):
+        half, sub, slot = i % 2, i // 2, i % 2
+        return [
+            pltpu.make_async_copy(
+                qkv_f.at[half, :, :, :, :, pl.ds(sub * 768, 768)], w_s.at[slot, :, :, :, :, pl.ds(0, 768)],
+                w_sem.at[slot, 0],
+            ),
+            pltpu.make_async_copy(
+                proj_f.at[half, :, :, :, :, pl.ds(sub * 256, 256)], w_s.at[slot, :, :, :, :, pl.ds(768, 256)],
+                w_sem.at[slot, 1],
+            ),
+        ]
+
+    def load_feed(half, part):
+        return [
+            pltpu.make_async_copy(
+                ref.at[half, :, :, :, :, columns(part * 512, 512)],
+                w_s.at[half, :, :, :, :, pl.ds(at * 512, 512)], w_sem.at[half, at],
+            )
+            for at, ref in enumerate((fc1_f, fc2_f))
+        ]
+
+    def start_loads(copies):
+        for copy in copies:
+            copy.start()
+
+    def wait_loads(copies):
+        for copy in copies:
+            copy.wait()
+
+    ticks.run(0, 2)
+    exchange.wait()
+    parts = jnp.sum(arrived[...].reshape(total // 2, 2, 8, half_cols), 0)
+    mod_ref[:, :half_cols] = parts[0]
+    mod_ref[:, half_cols:] = parts[1]
+    ticks.run(2, 4)
+    wait_loads(pairs[0][:2])
+    pairs[0][2].start()
+    start_loads(pairs[1][:2])
+    pairs[0][2].wait()
+    ticks.run(4, 5)
+    normed, _ = norm_rows(x_s[...].astype(F32))
+    one_s[...] = (normed * (1.0 + mod_ref[2:3]) + mod_ref[4:5]).astype(BF16)
+    acc_s[...] = jnp.zeros_like(acc_s)
+    ticks.run(5, 7)
+    gather.finish(0)
+    gather.finish(1)
+    start_loads(load_attend(0))
+    start_loads(load_attend(1))
+    ones = jnp.ones((x_s.shape[0], width), BF16)
+
+    def attend(i, carry):
+        def before_third():
+            ticks.run(8, 9)
+            gather.finish(2)
+            gather.finish(3)
+            start_loads(load_attend(2))
+            start_loads(load_attend(3))
+
+        switch_on(i, {1: lambda: ticks.run(7, 8), 2: before_third, 3: lambda: ticks.run(9, 10)})
+        slot = lax.rem(i, 2)
+        at = slot * 2 + i // 2
+        wait_loads([
+            pltpu.make_async_copy(
+                qkv_f.at[0, :, :, :, :, pl.ds(0, 768)], w_s.at[slot, :, :, :, :, pl.ds(0, 768)], w_sem.at[slot, 0]
+            ),
+            pltpu.make_async_copy(
+                proj_f.at[0, :, :, :, :, pl.ds(0, 256)], w_s.at[slot, :, :, :, :, pl.ds(768, 256)], w_sem.at[slot, 1]
+            ),
+        ])
+        cols = columns(at * 256, 256)
+        turned = pl.ds(pl.multiple_of(at * 256, 256), 256)
+        weights = w_s[slot].reshape(model, 1024)
+        projected = mm(one_s[...], weights[:, :768])
+        queries = projected[:, :256] + vecs[0:1, cols]
+        keys = projected[:, 256:512]
+        values = (projected[:, 512:] + vecs[1:2, cols]).astype(BF16)
+        vl_ref[:, cols] = values
+        q_turned, k_turned = queries.T, keys.T
+        boost = boosts[at]
+        kmask, qmask = kmask_ref[...], qmask_ref[...]
+        q_low, k_low, mixed, q_inv, k_inv, totals = [], [], [], [], [], []
+        for head in range(heads):
+            part = slice(head * width, (head + 1) * width)
+            q_now, k_now = q_turned[part], k_turned[part]
+            q_scale = lax.rsqrt(jnp.sum(q_now * q_now, 0, keepdims=True) + 1e-06)
+            k_scale = lax.rsqrt(jnp.sum(k_now * k_now, 0, keepdims=True) + 1e-06)
+            q_bf = (q_now * q_scale * boost[0:1, head : head + 1]).astype(BF16)
+            k_bf = (k_now * k_scale).astype(BF16)
+            scaled = q_bf.astype(F32) * LOG2E
+            high = scaled.astype(BF16)
+            rest = (scaled - high.astype(F32)).astype(BF16)
+            q_all = jnp.concatenate([high, rest, qmask], 0)
+            k_all = jnp.concatenate([k_bf, k_bf, kmask], 0)
+            soft = jnp.exp2(mm_tn(q_all, k_all)).astype(BF16)
+            summed = mm(soft, jnp.concatenate([values[:, part], ones], 1))
+            total_now = summed[:, width:]
+            mixed.append((summed[:, :width] / total_now).astype(BF16))
+            totals.append(total_now[:, 0:1])
+            q_low.append(q_bf)
+            k_low.append(k_bf)
+            q_inv.append(q_scale)
+            k_inv.append(k_scale)
+        mixed_all = jnp.concatenate(mixed, 1)
+        mix_ref[:, cols] = mixed_all
+        ql_ref[turned, :] = jnp.concatenate(q_low, 0)
+        kl_ref[turned, :] = jnp.concatenate(k_low, 0)
+        stat_ref[at, 0] = jnp.concatenate(q_inv + k_inv, 0)
+        stat_ref[at, 1] = jnp.log2(jnp.concatenate(totals + totals, 1)).T
+        acc_s[...] += mm_nt(mixed_all, weights[:, 768:])
+        return carry
+
+    lax.fori_loop(0, 4, attend, 0)
+    ticks.run(10, 11)
+    wait_loads(pairs[1][:2])
+    pairs[1][2].start()
+    attended = acc_s[...] + vecs[2:3]
+    att_ref[...] = attended.astype(BF16)
+    middle = x_s[...].astype(F32) + mod_ref[0:1] * attended
+    mid_s[...] = middle
+    normed, _ = norm_rows(middle)
+    two = (normed * (1.0 + mod_ref[3:4]) + mod_ref[5:6]).astype(BF16)
+    one_s[...] = two
+    twot_s[...] = two.T
+    pairs[1][2].wait()
+    back = (mod_ref[1:2] * cot_s[...].astype(F32)).astype(BF16)
+    back_s[...] = back
+    backt_s[...] = back.T
+    acc_s[...] = jnp.zeros_like(acc_s)
+    gacc_s[...] = jnp.zeros_like(gacc_s)
+
+    def store_feed(half, part):
+        return [
+            pltpu.make_async_copy(
+                grad_s.at[half, at], ref.at[half, :, :, :, :, columns(part * 512, 512)], grad_sem.at[half, at]
+            )
+            for at, ref in enumerate((g1_f, g2_f))
+        ]
+
+    def feed(i, carry):
+        half, part = lax.rem(i, 2), i // 2
+
+        def before(p):
+            def act():
+                if p > 0:
+                    ticks.run(10 + 2 * p, 11 + 2 * p)
+                gather.finish(4 + 2 * p)
+                gather.finish(5 + 2 * p)
+                start_loads(load_feed(0, p))
+                start_loads(load_feed(1, p))
+
+            return act
+
+        cases = {2 * p: before(p) for p in range(4)}
+        cases.update({2 * p + 1: (lambda p=p: ticks.run(11 + 2 * p, 12 + 2 * p)) for p in range(3)})
+        switch_on(i, cases)
+        wait_loads(load_feed(half, part))
+        weights = w_s[half].reshape(model, 1024)
+        w1, w2 = weights[:, :512], weights[:, 512:]
+        spot = columns(half * (hidden_bias.shape[1] // 2) + part * 512, 512)
+        hidden = mm(one_s[...], w1) + hidden_bias[0:1, spot]
+        square = hidden * hidden
+        curve = jnp.tanh(0.7978845608028654 * hidden * (1.0 + 0.044715 * square))
+        level = 0.5 * (1.0 + curve)
+        activated = (hidden * level).astype(BF16)
+        slope = level + 0.5 * hidden * (1.0 - curve * curve) * (
+            0.7978845608028654 * (1.0 + 0.134145 * square)
+        )
+        acc_s[...] += mm_nt(activated, w2)
+
+        @pl.when(i >= 2)
+        def _():
+            wait_loads(store_feed(half, part))
+
+        grad_s[half, 1] = mm(backt_s[...], activated).astype(BF16).reshape(grad_s.shape[2:])
+        hidden_grad = (mm(back_s[...], w2) * slope).astype(BF16)
+        grad_s[half, 0] = mm(twot_s[...], hidden_grad).astype(BF16).reshape(grad_s.shape[2:])
+        start_loads(store_feed(half, part))
+        gb1_ref[0:1, spot] = jnp.sum(hidden_grad.astype(F32), 0, keepdims=True)
+        gacc_s[...] += mm_nt(hidden_grad, w1)
+        return carry
+
+    lax.fori_loop(0, 8, feed, 0)
+    middle = mid_s[...]
+    out_grad = cot_s[...].astype(F32)
+    branch = acc_s[...] + vecs[3:4]
+    out_ref[...] = (middle + mod_ref[1:2] * branch).astype(BF16)
+    normed, inverse = norm_rows(middle)
+    grad = gacc_s[...]
+    middle_grad = out_grad + norm_rows_back(grad * (1.0 + mod_ref[3:4]), normed, inverse)
+    gmid_ref[...] = middle_grad
+    rows_ref[0:1] = jnp.sum(out_grad * branch, 0, keepdims=True)
+    rows_ref[1:2] = jnp.sum(grad * normed, 0, keepdims=True)
+    rows_ref[2:3] = jnp.sum(grad, 0, keepdims=True)
+    rows_ref[3:4] = jnp.sum(back_s[...].astype(F32), 0, keepdims=True)
+    rows_ref[4:5] = jnp.sum(middle_grad * att_ref[...].astype(F32), 0, keepdims=True)
+    rows_ref[5:8] = jnp.zeros((3, model), F32)
+    gb1_ref[1:8] = jnp.zeros((7, gb1_ref.shape[1]), F32)
+    for half in range(2):
+        wait_loads(store_feed(half, 3))
+    gather.sent()
+
+
+def run_ahead(chunks, line, products, segments, tok, cot, vecs, hidden_bias, boosts, kmask, qmask, width, cid):
+    padded, model = tok.shape[1:]
+    rows = 2 * padded
+    total, count = 8 * line, len(chunks)
+    own_rows = segments[0].shape[0]
+    hidden_cols = hidden_bias.shape[1]
+    anywhere, inside = pl.BlockSpec(memory_space=pl.ANY), pl.BlockSpec(memory_space=pltpu.VMEM)
+    full = [jax.ShapeDtypeStruct((2, line, 2, 2) + s.shape, BF16) for s in segments]
+    flat = jax.ShapeDtypeStruct((rows, model), BF16)
+    turned = jax.ShapeDtypeStruct((model, rows), BF16)
+    block = (line, 2, 2, own_rows)
+    dma = pltpu.SemaphoreType.DMA
+    return pl.pallas_call(
+        functools.partial(ahead_kernel, chunks, line, width),
+        in_specs=[anywhere] * 7 + [inside] * 5,
+        out_shape=full + [flat, flat, full[2], full[3]] + [
+            jax.ShapeDtypeStruct((8, model), F32), turned, turned, flat, flat,
+            jax.ShapeDtypeStruct((model // 256, 2, 8, rows), F32), flat,
+            jax.ShapeDtypeStruct((rows, model), F32), jax.ShapeDtypeStruct((8, model), F32),
+            jax.ShapeDtypeStruct((8, hidden_cols), F32),
+        ],
+        out_specs=[anywhere] * 8 + [inside] * 10,
+        scratch_shapes=[
+            pltpu.VMEM(products.shape, F32), pltpu.VMEM((rows, model), BF16),
+            pltpu.VMEM((rows, model), BF16), pltpu.VMEM((rows, model), BF16),
+            pltpu.VMEM((rows, model), BF16), pltpu.VMEM((rows, model), F32), pltpu.VMEM((rows, model), F32),
+            pltpu.VMEM((model, rows), BF16), pltpu.VMEM((rows, model), BF16), pltpu.VMEM((model, rows), BF16),
+            pltpu.VMEM((rows, model), F32), pltpu.VMEM((2,) + block + (1024,), BF16),
+            pltpu.VMEM((2, 2) + block + (512,), BF16),
+            dma((total,)), dma((total,)), dma((4,)), dma((2, 4)),
+            dma((count, 2, line - 1)), dma((count, 2, line - 1)), dma((count, 7)), dma((count, 7)),
+            dma((2,)), dma((2, 2)), dma((2, 2)),
+        ],
+        compiler_params=pltpu.CompilerParams(
+            collective_id=cid, has_side_effects=True, vmem_limit_bytes=VMEM_LIMIT
+        ),
+        name="ahead",
+    )(products, *segments, tok, cot, vecs, hidden_bias, boosts, kmask, qmask)
+
+
+def behind_kernel(chunks, line, width, levels, *refs):
+    count = len(chunks)
+    (x_f, qkv_f, proj_f, g1_f, g2_f, result, ql_f, kl_f, vl_f, mix_f,
+     gmid_ref, mod_ref, feed_rows, stat_ref, boosts, kmask_ref, qmask_ref) = refs[:17]
+    (gqkv_f, gproj_f, act_pair, tok_pair) = refs[17:21]
+    landing = refs[21 : 21 + count]
+    (t_qkv, t_proj, t_fc1, t_fc2, sums_ref, rows_ref, mods_ref) = refs[21 + count : 28 + count]
+    rest = refs[28 + count :]
+    first_b, second_b, line_b = rest[:count], rest[count : 2 * count], rest[2 * count : 3 * count]
+    (core_s, own_s, x_s, ga_s, gat_s, onet_s, acc_s, turn_s, flat_s, w_s, grad_s, gm_s,
+     a_send, a_recv, pair_sem, x_sem, w_sem, grad_sem,
+     own_sem, load_sem, send_sem, recv_sem, z_send, z_recv) = rest[3 * count :]
+    z, x, c, y = where_am_i()
+    total = 8 * line
+    padded, model = result.shape[0] // 2, result.shape[1]
+    half_cols = model // 2
+    heads = 256 // width
+    partner = device(z, x, c, 1 - y)
+    scatter = Scatter(
+        chunks, line, [gqkv_f, gproj_f, g1_f, g2_f], [t_qkv, t_proj, t_fc1, t_fc2], landing, core_s, own_s,
+        first_b, second_b, line_b, (own_sem, load_sem, send_sem, recv_sem, z_send, z_recv),
+    )
+    ticks = Ticks(count, scatter.stages())
+    mine, others = pl.ds(y * padded, padded), pl.ds((1 - y) * padded, padded)
+    pairs = [
+        (
+            pltpu.make_async_copy(source.at[mine], target.at[y], pair_sem.at[p, 0]),
+            remote(source.at[others], target.at[y], pair_sem.at[p, 1], pair_sem.at[p, 2], partner),
+        )
+        for p, (source, target) in enumerate(((result, act_pair), (x_s, tok_pair)))
+    ]
+    load_x = pltpu.make_async_copy(x_f, x_s, x_sem.at[0])
+    load_x.start()
+    greet_all(total)
+    ticks.run(0, 1)
+
+    def load_group(i):
+        slot = lax.rem(i, 2)
+        sub, at = i // 2, slot * 2 + i // 2
+        turned = pl.ds(pl.multiple_of(at * 256, 256), 256)
+        cols = columns(at * 256, 256)
+        pieces = [
+            (qkv_f.at[slot, :, :, :, :, columns(sub * 768, 768)], w_s.at[slot, :, :, :, :, pl.ds(0, 768)]),
+            (proj_f.at[slot, :, :, :, :, columns(sub * 256, 256)], w_s.at[slot, :, :, :, :, pl.ds(768, 256)]),
+            (ql_f.at[turned], turn_s.at[slot, 0]),
+            (kl_f.at[turned], turn_s.at[slot, 1]),
+            (vl_f.at[:, cols], flat_s.at[slot, 0]),
+            (mix_f.at[:, cols], flat_s.at[slot, 1]),
+        ]
+        return [pltpu.make_async_copy(s, t, w_sem.at[slot, n]) for n, (s, t) in enumerate(pieces)]
+
+    def store_group(i):
+        half, sub = lax.rem(i, 2), i // 2
+        return [
+            pltpu.make_async_copy(
+                grad_s.at[:, :, :, :, pl.ds(0, 768)], gqkv_f.at[half, :, :, :, :, columns(sub * 768, 768)],
+                grad_sem.at[0],
+            ),
+            pltpu.make_async_copy(
+                grad_s.at[:, :, :, :, pl.ds(768, 256)], gproj_f.at[half, :, :, :, :, columns(sub * 256, 256)],
+                grad_sem.at[1],
+            ),
+        ]
+
+    def start_loads(copies):
+        for copy in copies:
+            copy.start()
+
+    def wait_loads(copies):
+        for copy in copies:
+            copy.wait()
+
+    start_loads(load_group(0))
+    ticks.run(1, 2)
+    attend_grad = (mod_ref[0:1] * gmid_ref[...]).astype(BF16)
+    ga_s[...] = attend_grad
+    gat_s[...] = attend_grad.T
+    rows_ref[2:3] = jnp.sum(attend_grad.astype(F32), 0, keepdims=True)
+    ticks.run(2, 3)
+    load_x.wait()
+    normed, _ = norm_rows(x_s[...].astype(F32))
+    onet_s[...] = (normed * (1.0 + mod_ref[2:3]) + mod_ref[4:5]).astype(BF16).T
+    acc_s[...] = jnp.zeros_like(acc_s)
+    kmask, qmask = kmask_ref[...], qmask_ref[...]
+    rows = kmask.shape[1]
+    place = lax.broadcasted_iota(jnp.int32, (16, rows), 0)
+
+    def pieces_of(row, first):
+        high, mid, low = split_three(row)
+        zero = jnp.zeros((16, rows), BF16)
+        out = jnp.where(place == first, jnp.broadcast_to(high, zero.shape), zero)
+        out = jnp.where(place == first + 1, jnp.broadcast_to(mid, zero.shape), out)
+        return jnp.where(place == first + 2, jnp.broadcast_to(low, zero.shape), out)
+
+    def group(i, carry):
+        slot = lax.rem(i, 2)
+        at = slot * 2 + i // 2
+
+        @pl.when(i < 3)
+        def _():
+            start_loads(load_group(i + 1))
+
+        wait_loads(load_group(i))
+        boost = boosts[at]
+        weights = w_s[slot].reshape(model, 1024)
+        mixed = flat_s[slot, 1]
+        values = flat_s[slot, 0]
+        q_all_low, k_all_low = turn_s[slot, 0], turn_s[slot, 1]
+        mixed_grad = mm(ga_s[...], weights[:, 768:]).astype(BF16)
+        mixed_turned, v_turned, q_plain = mixed_grad.T, values.T, q_all_low.T
+        dq_rows, dk_rows, dv_cols, scales = [], [], [], []
+        for head in range(heads):
+            if head == 2:
+                switch_on(i, {n: (lambda n=n: ticks.run(3 + 2 * n, 4 + 2 * n)) for n in range(4)})
+            part = slice(head * width, (head + 1) * width)
+            lift = boost[0:1, head : head + 1]
+            q_bf, k_bf = q_all_low[part], k_all_low[part]
+            q_float = q_bf.astype(F32)
+            scaled = q_float * LOG2E
+            high = scaled.astype(BF16)
+            low = (scaled - high.astype(F32)).astype(BF16)
+            log_total = stat_ref[at, 1, head : head + 1]
+            q_all = jnp.concatenate([high, low, qmask + pieces_of(-log_total, levels + 1)], 0)
+            k_all = jnp.concatenate([k_bf, k_bf, kmask], 0)
+            soft = jnp.exp2(mm_tn(k_all, q_all))
+            product = soft * mm_tn(v_turned[part], mixed_turned[part])
+            delta = jnp.sum(product, 0, keepdims=True)
+            scores_grad = (product - soft * delta).astype(BF16)
+            dv_cols.append(mm(soft.astype(BF16), mixed_grad[:, part]))
+            dq_low = mm(k_bf, scores_grad)
+            dk_low = mm(scores_grad, q_plain[:, part]).T
+            q_inv = stat_ref[at, 0, head : head + 1]
+            k_inv = stat_ref[at, 0, heads + head : heads + head + 1]
+            k_unit = k_bf.astype(F32)
+            along = dq_low * q_float
+            scales.append(jnp.sum(along, keepdims=True))
+            dq_rows.append(
+                q_inv * (dq_low * lift - q_float * (1.0 / lift) * jnp.sum(along, 0, keepdims=True))
+            )
+            dk_rows.append(k_inv * (dk_low - k_unit * jnp.sum(dk_low * k_unit, 0, keepdims=True)))
+        dq = jnp.concatenate(dq_rows, 0).T.astype(BF16)
+        dk = jnp.concatenate(dk_rows, 0).T.astype(BF16)
+        dv = jnp.concatenate(dv_cols, 1).astype(BF16)
+        triple = jnp.concatenate([dq, dk, dv], 1)
+
+        @pl.when(i > 0)
+        def _():
+            wait_loads(store_group(i))
+
+        shape = grad_s.shape[:4]
+        grad_s[:, :, :, :, 0:768] = mm(onet_s[...], triple).astype(BF16).reshape(shape + (768,))
+        grad_s[:, :, :, :, 768:1024] = mm(gat_s[...], mixed).astype(BF16).reshape(shape + (256,))
+        start_loads(store_group(i))
+        acc_s[...] += mm_nt(triple, weights[:, :768])
+        sums_ref[at, 0:1, :] = jnp.sum(dq.astype(F32), 0, keepdims=True)
+        sums_ref[at, 1:2, :] = jnp.sum(dv.astype(F32), 0, keepdims=True)
+        sums_ref[at, 2:4, :] = jnp.zeros((2, 256), F32)
+        for head in range(heads):
+            sums_ref[at, 4 + head : 5 + head, :] = jnp.broadcast_to(scales[head], (1, 256))
+
+        def end(n):
+            def act():
+                if n == 1:
+                    start_loads(pairs[0])
+                ticks.run(4 + 2 * n, 5 + 2 * n)
+
+            return act
+
+        switch_on(i, {n: end(n) for n in range(3)})
+        return carry
+
+    lax.fori_loop(0, 4, group, 0)
+    wait_loads(store_group(3))
+    ticks.run(10, 11)
+    grad = acc_s[...]
+    normed, inverse = norm_rows(x_s[...].astype(F32))
+    x_s[...] = (
+        gmid_ref[...] + norm_rows_back(grad * (1.0 + mod_ref[2:3]), normed, inverse)
+    ).astype(BF16)
+    start_loads(pairs[1])
+    rows_ref[0:1] = jnp.sum(grad * normed, 0, keepdims=True)
+    rows_ref[1:2] = jnp.sum(grad, 0, keepdims=True)
+    rows_ref[3:8] = jnp.zeros((5, model), F32)
+    for n, row in enumerate((feed_rows[4:5], feed_rows[0:1], rows_ref[0:1], feed_rows[1:2], rows_ref[1:2], feed_rows[2:3])):
+        for half in range(2):
+            gm_s[half, n : n + 1] = row[:, half * half_cols : (half + 1) * half_cols]
+    gm_s[:, 6:8] = jnp.zeros((2, 2, half_cols), F32)
+    exchange = Exchange(total, lambda to: gm_s.at[lax.rem(to, 2)], mods_ref, a_send, a_recv)
+    exchange.start()
+    ticks.run(11, ticks.total)
+    exchange.wait()
+    for pair in pairs:
+        wait_loads(pair)
+    scatter.sent()
+
+
+def run_behind(chunks, line, levels, saved, inner, width, cid):
+    x_f, qkv_f, proj_f, g1_f, g2_f, result, ql, kl, vl, mix = saved
+    rows, model = x_f.shape
+    total, count = 8 * line, len(chunks)
+    own_rows = qkv_f.shape[4]
+    anywhere, inside = pl.BlockSpec(memory_space=pl.ANY), pl.BlockSpec(memory_space=pltpu.VMEM)
+    dma = pltpu.SemaphoreType.DMA
+    landing, first_b, second_b, line_b = [], [], [], []
+    for _, kind, _, cols in chunks:
+        landing.append(jax.ShapeDtypeStruct((2, line, 2, own_rows, cols), BF16))
+        first_b.append(pltpu.VMEM(((line, 2) if kind == 0 else (2, line)) + (own_rows, cols), BF16))
+        second_b.append(pltpu.VMEM((line, own_rows, cols), BF16))
+        line_b.append(pltpu.VMEM((line + 1, own_rows, cols), BF16))
+    most = max(chunk[3] for chunk in chunks)
+    sources = [qkv_f, proj_f, g1_f, g2_f]
+    block = (line, 2, 2, own_rows)
+    made = pl.pallas_call(
+        functools.partial(behind_kernel, chunks, line, width, levels),
+        in_specs=[anywhere] * 10 + [inside] * 7,
+        out_shape=[jax.ShapeDtypeStruct(qkv_f.shape, BF16), jax.ShapeDtypeStruct(proj_f.shape, BF16)]
+        + [jax.ShapeDtypeStruct((2, rows // 2, model), BF16)] * 2 + landing
+        + [jax.ShapeDtypeStruct(s.shape[4:], F32) for s in sources]
+        + [
+            jax.ShapeDtypeStruct((model // 256, 8, 256), F32), jax.ShapeDtypeStruct((8, model), F32),
+            jax.ShapeDtypeStruct((total, 8, model // 2), F32),
+        ],
+        out_specs=[anywhere] * (4 + count) + [inside] * 7,
+        scratch_shapes=first_b + second_b + line_b + [
+            pltpu.VMEM((3, 2, line, 2, own_rows, most), BF16), pltpu.VMEM((2, 2, line, 2, own_rows, most), BF16),
+            pltpu.VMEM((rows, model), BF16), pltpu.VMEM((rows, model), BF16), pltpu.VMEM((model, rows), BF16),
+            pltpu.VMEM((model, rows), BF16), pltpu.VMEM((rows, model), F32), pltpu.VMEM((2, 2, 256, rows), BF16),
+            pltpu.VMEM((2, 2, rows, 256), BF16), pltpu.VMEM((2,) + block + (1024,), BF16),
+            pltpu.VMEM(block + (1024,), BF16), pltpu.VMEM((2, 8, model // 2), F32),
+            dma((total,)), dma((total,)), dma((2, 3)), dma((1,)), dma((2, 6)), dma((2,)),
+            dma((count,)), dma((count,)), dma((count, 3)), dma((count, 3)),
+            dma((count, 2, line)), dma((count, 2, line)),
+        ],
+        compiler_params=pltpu.CompilerParams(
+            collective_id=cid, has_side_effects=True, vmem_limit_bytes=VMEM_LIMIT
+        ),
+        name="behind",
+    )(*saved, *inner)
+    return made[2], made[3], made[4 + count :]
+
+
+def pad_rows(values, padded):
+    return jnp.pad(values, ((0, 0), (0, padded - values.shape[1]), (0, 0)))
+
+
+def gather_list():
+    return [(0, 1, 0, 768), (1, 1, 0, 256), (0, 0, 768, 768), (1, 1, 256, 256)] + [
+        (segment, int((segment, part) not in ((2, 1), (3, 3))), part * 512, 512) for part in range(4) for segment in (2, 3)
+    ]
+
+
+def scatter_list():
+    return [
+        (segment, int((segment, part) not in ((2, 1), (3, 3))), part * 512, 512) for part in range(4) for segment in (2, 3)
+    ] + [(0, 0, 0, 512), (0, 1, 512, 256), (1, 1, 0, 256), (0, 1, 768, 512), (0, 1, 1280, 256), (1, 0, 256, 256)]
+
+
+def on_device_paired(
+    tokens, condition, scale_lengths, order, cotangent, ada_weight, ada_bias, qkv_weight, qv_bias,
+    head_log_scale, proj_weight, out_bias, fc1_weight, fc1_bias, fc2_weight,
+):
+    n_dp, mine = lax.axis_size("dp"), lax.axis_index("mp")
+    line = n_dp // 4
+    slots, half_rows, model = tokens.shape
+    padded = -(-half_rows // 16) * 16
+    rows = 2 * padded
+    local_heads, width = qv_bias.shape[1], 64
+    own_cols = qkv_weight.shape[2]
+    own_rows = qkv_weight.shape[1]
+    hidden_cols = fc1_weight.shape[1]
+    groups = 2 * own_cols // 256
+    swap = order[0, 0] != 0
+    entries = qv_bias.shape[2]
+    vectors = 4 * local_heads + fc1_bias.shape[0]
+    scale_at = vectors * entries
+    n_dev = 2 * n_dp
+
+    def to_slots(values):
+        return jnp.stack([jnp.where(swap, values[1], values[0]), jnp.where(swap, values[0], values[1])])
+
+    cond_slots = to_slots(condition).astype(F32)
+    signal = jax.nn.silu(cond_slots).astype(BF16)
+    small = jnp.concatenate(
+        [qv_bias.reshape(-1), out_bias.reshape(-1), fc1_bias.reshape(-1)] + list(split_three(head_log_scale))
+    )
+    signal_out = signal.reshape(slots, n_dp, own_rows).transpose(1, 0, 2).reshape(n_dp, 1, slots * own_rows)
+    letters = jnp.concatenate(
+        [jnp.broadcast_to(signal_out, (n_dp, 2, slots * own_rows)), jnp.broadcast_to(small, (n_dp, 2) + small.shape)], 2
+    ).reshape(n_dev, -1)
+    letters = lax.all_to_all(letters, ("dp", "mp"), 0, 0, tiled=True).reshape(n_dp, 2, -1)
+    signal_rows = letters[:, 0, : slots * own_rows].reshape(n_dev, own_rows)
+    small_full = letters[:, :, slots * own_rows :].transpose(1, 0, 2)
+    spread_small = small_full[:, :, :scale_at].reshape(2, n_dp, vectors, entries)
+    spread_small = spread_small.transpose(0, 2, 1, 3).reshape(2, vectors, n_dp * entries).astype(F32)
+    block_rows = spread_small[:, : 4 * local_heads].reshape(2, 4, own_cols).transpose(1, 0, 2).reshape(4, model)
+    vecs = jnp.pad(block_rows, ((0, 4), (0, 0)))
+    hidden_bias = spread_small[:, 4 * local_heads :].reshape(1, 2 * hidden_cols)
+    scale_all = sum(
+        small_full[:, 0, scale_at + i * local_heads : scale_at + (i + 1) * local_heads].astype(F32) for i in range(3)
+    )
+    boost = jnp.exp(scale_all.reshape(groups, -1))
+    boosts = jnp.zeros((groups, 8, 128), F32).at[:, 0, : boost.shape[1]].set(boost)
+
+    ada_flat = ada_weight.reshape(own_rows, 6 * own_cols)
+    bias_own = lax.dynamic_update_slice(
+        jnp.zeros((6, local_heads, width), F32), ada_bias.astype(F32), (0, 0, lax.axis_index("dp") * entries)
+    )
+    products = jnp.dot(signal_rows, ada_flat, preferred_element_type=F32) + bias_own.reshape(1, 6 * own_cols)
+    products = jnp.pad(products.reshape(n_dev, 6, own_cols), ((0, 0), (0, 2), (0, 0)))
+
+    lengths = lax.dynamic_index_in_dim(to_slots(scale_lengths), mine, 0, keepdims=False)
+    kmask, qmask = build_masks(lengths, half_rows, padded)
+    segments = [
+        qkv_weight.reshape(3, own_rows, 2, 256).transpose(1, 2, 0, 3).reshape(own_rows, 3 * own_cols),
+        proj_weight.T, fc1_weight, fc2_weight.T,
+    ]
+    (qkv_f, proj_f, _, _, x_f, _, g1_f, g2_f, mods, q_low, k_low, v_low, mixed, stats, result, grad_middle,
+     feed_rows, g_hidden) = run_ahead(
+        gather_list(), line, products, segments, pad_rows(to_slots(tokens), padded), pad_rows(cotangent, padded),
+        vecs, hidden_bias, boosts, kmask, qmask, width, 1,
+    )
+    act_pair, tok_pair, (t_qkv, t_proj, t_fc1, t_fc2, sums, back_rows, arrived) = run_behind(
+        scatter_list(), line, scale_lengths.shape[1],
+        [x_f, qkv_f, proj_f, g1_f, g2_f, result, q_low, k_low, v_low, mixed],
+        [grad_middle, mods, feed_rows, stats, boosts, kmask, qmask], width, 2,
+    )
+    qkv_total = t_qkv.reshape(own_rows, 2, 3, 256).transpose(2, 0, 1, 3).reshape(qkv_weight.shape)
+    activations = act_pair[:, :half_rows]
+    tokens_grad = to_slots(tok_pair[:, :half_rows])
+
+    all_mods = arrived[:, :6].reshape(n_dev, 6 * own_cols)
+    ada_weight_grad = lax.dot_general(
+        signal_rows.astype(F32), all_mods, (((0,), (0,)), ((), ())), precision=precise, preferred_element_type=F32
+    ).reshape(ada_weight.shape)
+    ada_bias_grad = lax.dynamic_slice_in_dim(
+        jnp.sum(all_mods, 0).reshape(6, local_heads, width), lax.axis_index("dp") * entries, entries, 2
+    )
+    signal_part = lax.dot_general(
+        all_mods, ada_flat.astype(F32), (((1,), (1,)), ((), ())), precision=precise, preferred_element_type=F32
+    )
+    bias_grads = jnp.stack([sums[:, 0].reshape(model), sums[:, 1].reshape(model), back_rows[2], feed_rows[3]])
+    bias_grads = bias_grads.reshape(4, 2, local_heads, n_dp, entries).transpose(3, 1, 0, 2, 4)
+    hidden_grads = g_hidden[0].reshape(2, fc1_bias.shape[0], n_dp, entries).transpose(2, 0, 1, 3)
+    scale_grads = jnp.broadcast_to(sums[:, 4:, 0].reshape(1, 2, local_heads), (n_dp, 2, local_heads))
+    signal_part = jnp.broadcast_to(signal_part.reshape(n_dp, 1, slots * own_rows), (n_dp, 2, slots * own_rows))
+    letters = jnp.concatenate(
+        [signal_part, bias_grads.reshape(n_dp, 2, -1), hidden_grads.reshape(n_dp, 2, -1), scale_grads], 2
+    ).reshape(n_dev, -1)
+    letters = lax.all_to_all(letters, ("dp", "mp"), 0, 0, tiled=True).reshape(n_dp, 2, -1)
+    signal_grad = letters[:, :, : slots * own_rows].sum(1).reshape(n_dp, slots, own_rows)
+    signal_grad = signal_grad.transpose(1, 0, 2).reshape(slots, model)
+    small_total = letters[:, :, slots * own_rows :].sum((0, 1))
+    bias_total = small_total[: 4 * local_heads * entries].reshape(2, 2, local_heads, entries)
+    hidden_total = small_total[4 * local_heads * entries : scale_at].reshape(fc1_bias.shape)
+    pull = jax.vjp(jax.nn.silu, cond_slots)[1]
+    condition_grad = to_slots(pull(signal_grad)[0]).astype(BF16)
+    return (
+        activations, tokens_grad, condition_grad, ada_weight_grad, ada_bias_grad, qkv_total, bias_total[0],
+        small_total[scale_at:], t_proj.T, bias_total[1], t_fc1, hidden_total, t_fc2.T,
+    )
+
 
 precise = lax.Precision.HIGHEST
 
@@ -74,7 +1092,7 @@
     )
 
 
-def on_device(
+def on_device_shared(
     tokens,
     condition,
     scale_lengths,
@@ -146,7 +1164,8 @@
             jnp.float32
         )
         qkv_full, qv_full, proj_full, outb_full, fc1_full, fc1b_full, fc2_full = rows_now()
-        scale_ends = jnp.cumsum(lengths)
+        steps = jnp.arange(lengths.shape[0], dtype=jnp.int32)
+        scale_ends = jnp.sum(jnp.where(steps[None, :] <= steps[:, None], lengths[None, :], 0), 1)
         scale_of = jnp.sum((positions[:, None] >= scale_ends[None, :]).astype(jnp.int32), 1)
         allowed = (scale_of[None, :] <= scale_of[:, None])[None]
         normed_one, inverse_one = row_norm(residual)
@@ -402,6 +1421,8 @@
         P("mp", "dp"),
         P("mp", "dp"),
     )
+    line, spare = divmod(mesh.shape["dp"], 4)
+    paired = mesh.shape["mp"] == 2 and spare == 0 and line > 1
     return jax.shard_map(
-        on_device, mesh=mesh, in_specs=in_specs, out_specs=out_specs, check_vma=False
-    )
+        on_device_paired if paired else on_device_shared, mesh=mesh, in_specs=in_specs, out_specs=out_specs, check_vma=False
+    )

time: 1650 us -> 466 us (0.28)
  waiting for transfers between devices: 593 us -> 0.01 us
  blocking collectives: 433 us -> 0 us
  Pallas kernels: 0 us -> 398 us
  matrix products: 259 us -> 2.38 us
  other arithmetic: 138 us -> 7.92 us
  local copies, waits for them, and re-layouts: 166 us -> 37.3 us
    pallas_call x0 -> x2, Pallas kernels: none -> 398 us  [the longest x1 220 us: run_ahead(): pl.pallas_call(functools.partial(ahead_kernel, chunks, line, width), in_s...]
    all_gather x17 -> x0, waiting for transfers between devices: 294 us -> none  [the longest x2 100 us: fetch(): lax.all_gather(fc1_weight, 'dp', axis=0, tiled=True)]
    reduce_scatter x7 -> x0, waiting for transfers between devices: 293 us -> none  [the longest x1 86.8 us: on_device(): lax.psum_scatter(ada_grad.astype(jnp.bfloat16), 'dp', scatter_dimension=0...]
    dot_general x39 -> x3, matrix products: 259 us -> 2.38 us  [the longest x1 1.6 us: on_device_paired(): lax.dot_general(signal_rows.astype(F32), all_mods, (((0,), (0,)), ((), ()...]
    while x6 -> x0, blocking collectives: 193 us -> none
    all_gather x8 -> x0, blocking collectives: 143 us -> none  [the longest x2 41.1 us: fetch(): lax.all_gather(out_bias, 'dp', axis=2, tiled=True)]
    while x173 -> x0, local copies, waits for them, and re-layouts: 97.4 us -> none
    unnamed x1 -> x0, blocking collectives: 58.6 us -> none
  transfers between devices with their start and end apart: 32 -> 2, of which waited for: 15 -> 0; matrix products, arithmetic and copies ran while one was open for 22% -> 5% of each run, Pallas kernels for 0% -> 0%
where the time goes in v2:
time: 466 us; the launch traced here: 459 us
  Pallas kernels  398 us (85%)
  local copies, waits for them, and re-layouts  37.3 us (8%)
  starting transfers between devices  11.5 us (2%)
  other arithmetic  7.92 us (2%)
    pallas_call x1, Pallas kernels, run_ahead(): pl.pallas_call(functools.partial(ahead_kernel, chunks, line, width), in_s...  220 us
    pallas_call x1, Pallas kernels, run_behind(): pl.pallas_call(functools.partial(behind_kernel, chunks, line, width, leve...  178 us
    unnamed x36, local copies, waits for them, and re-layouts  15 us
    all_to_all x2, starting transfers between devices, on_device_paired(): lax.all_to_all(letters, ('dp', 'mp'), 0, 0, tiled=True).reshape(n_dp, 2, -1)  11.5 us
  transfers between devices with their start and end apart: 2, of which 0 were waited for; matrix products, arithmetic and copies ran while one was open for 5% of the time, Pallas kernels for 0%

profile of v2, /device:TPU:0, one launch (start us, length us, event | category | flops | bytes accessed | tf_op | source)
XLA Modules:
  0.0 459.3 jit_solution(9367240573249103717)
XLA Ops:
  1.3 0.8 fusion.35
  2.4 0.7 subtract_convert_fusion
  3.1 0.8 copy.202
  4.0 0.8 copy.200
  4.9 0.8 copy.201
  6.0 0.5 broadcast.197
  6.5 0.8 reduce.34
  7.3 0.7 reshape.323
  8.0 7.3 %all-to-all-start = ((bf16[32,2,204]{2,1,0:T(2,128)(2,1)}), bf16[32,2,204]{2,1,0:T(2,128)(2,1)S(1)}, u32[]{:S(2)}, u32[]{:S(2)}) async-start(bf16[32,2,204]{2,1,0:T(2,128)(2,1)} %reshape.323), calls=%async_computation | async-start | bytes 65536 | tf_op jit(solution)/shard_map/all_to_all | solution.py:951
  15.4 0.8 broadcast_select_fusion.11
  16.4 4.2 fusion.37
  20.6 0.7 fusion.8.refs_10_.refs_15_
  21.3 0.7 select_convert_fusion.refs_11_.refs_16_
  22.0 0.4 broadcast_select_fusion.3
  22.4 1.2 fusion.2.refs_5_
  23.8 0.2 dynamic_update_slice.3
  24.1 1.8 copy.209
  25.9 0.2 copy.256
  26.1 0.9 reshape.274.refs_1_
  27.0 1.2 pad.22.refs_6_
  28.4 0.2 reduce.5
  28.8 0.2 convolution_add_fusion
  29.0 0.2 reshape.272
  29.2 0.8 pad.20.refs_0_
  30.6 0.6 pad.23.refs_7_
  31.3 0.7 reshape.277.refs_8_
  32.1 0.6 scatter.4.refs_9_.refs_14_
  32.7 219.9 %ahead.1 = (bf16[2,4,2,2,64,1536]{5,4,3,2,1,0:T(8,128)(2,1)}, bf16[2,4,2,2,64,512]{5,4,3,2,1,0:T(8,128)(2,1)}, bf16[2,4,2,2,64,2048]{5,4,3,2,1,0:T(8,128)(2,1)},...) custom-call(f32[32,8,512]{2,1,0:T(8,128)} %pad.20.refs_0_, ...), custom_call_target="tpu_custom_call" | custom-call | tf_op jit(solution)/shard_map/ahead/pallas_call | solution.py:634
  252.6 177.9 %behind.1 = (bf16[2,4,2,2,64,1536]{5,4,3,2,1,0:T(8,128)(2,1)}, bf16[2,4,2,2,64,512]{5,4,3,2,1,0:T(8,128)(2,1)}, bf16[2,352,1024]{2,1,0:T(8,128)(2,1)}, bf16[2,35...) custom-call(bf16[704,1024]{1,0:T(8,128)(2,1)} %get-tuple-element.49., ...), custom_call_target="tpu_custom_call" | custom-call | tf_op jit(solution)/shard_map/behind/pallas_call | solution.py:874
  430.6 0.9 slice_reduce_fusion.8
  431.5 0.8 slice_reduce_fusion.4
  432.3 0.8 slice_reduce_fusion.5
  433.3 0.1 copy.219
  433.4 0.2 stack.52
  433.6 0.1 copy.220
  433.7 0.2 stack.49
  433.9 0.1 copy.217
  434.1 0.2 stack.50
  434.2 0.1 copy.218
  434.4 0.6 copy.221
  435.0 0.3 concatenate.25
  435.4 0.6 convolution_bitcast_fusion
  436.2 1.0 slice_reduce_fusion.2
  437.2 0.5 reshape_squeeze.8
  437.7 0.2 copy.222
  437.9 0.3 concatenate.26
  438.2 0.7 copy.223
  438.9 4.2 all-to-all-start.1
  443.4 2.5 copy.228
  446.0 2.5 copy.227
  448.6 0.3 reshape.283
  448.8 0.2 copy.226
  449.1 1.1 reshape.284
  450.2 1.6 fusion.3
  451.9 0.7 copy.229
  452.6 0.2 reduce.14
  452.9 0.5 slice.187
  453.8 0.7 copy.232
  454.5 0.7 copy.230
  455.3 0.7 copy.231
  456.0 0.6 pad_maximum_fusion.2
  456.6 0.7 copy.262
  457.2 0.8 copy.263
  458.0 0.8 copy.264
  (90 shorter events, 4.0 us)
Async XLA Ops:
  8.0 20.2 %all-to-all-start = ((bf16[32,2,204]{2,1,0:T(2,128)(2,1)}), bf16[32,2,204]{2,1,0:T(2,128)(2,1)S(1)}, u32[]{:S(2)}, u32[]{:S(2)}) async-start(bf16[32,2,204]{2,1,0:T(2,128)(2,1)} %reshape.323), calls=%async_computation | async-start | bytes 65536 | tf_op jit(solution)/shard_map/all_to_all | solution.py:951
  22.4 1.3 copy-start.9
  22.4 1.7 copy-start
  24.1 1.8 copy-start.7
  430.6 4.7 %copy-start.5 = (f32[32,8,512]{2,1,0:T(8,128)S(1)}, f32[32,8,512]{2,1,0:T(8,128)}, u32[]{:S(2)}) copy-start(f32[32,8,512]{2,1,0:T(8,128)} %get-tuple-element.65) | copy-start | bytes 1572868
  436.0 7.1 %copy-start.2 = (bf16[2,352,1024]{2,1,0:T(8,128)(2,1)S(1)}, bf16[2,352,1024]{2,1,0:T(8,128)(2,1)}, u32[]{:S(2)}) copy-start(bf16[2,352,1024]{2,1,0:T(8,128)(2,1)} %get-tuple-element.64) | copy-start | bytes 4325380
  438.9 13.7 %all-to-all-start.1 = ((f32[32,1,392]{2,1,0:T(1,128)}), f32[32,1,392]{2,1,0:T(1,128)S(1)}, u32[]{:S(2)}, u32[]{:S(2)}) async-start(f32[32,1,392]{2,1,0:T(1,128)} %copy.223), calls=%async_computation.1 | async-start | bytes 131072 | tf_op jit(solution)/shard_map/all_to_all | solution.py:1010
  443.4 2.5 copy-start.1
  446.0 2.5 copy-start.6
  449.0 7.5 %copy-start.8 = (f32[64,512]{1,0:T(8,128)S(1)}, f32[64,512]{1,0:T(8,128)}, u32[]{:S(2)}) copy-start(f32[64,512]{1,0:T(8,128)} %get-tuple-element.70) | copy-start | bytes 393220
  449.1 8.2 %copy-start.4 = (f32[64,2048]{1,0:T(8,128)S(1)}, f32[64,2048]{1,0:T(8,128)}, u32[]{:S(2)}) copy-start(f32[64,2048]{1,0:T(8,128)} %get-tuple-element.218) | copy-start | bytes 1572868
  450.2 7.8 %copy-start.3 = (f32[64,2048]{1,0:T(8,128)S(1)}, f32[64,2048]{1,0:T(8,128)}, u32[]{:S(2)}) copy-start(f32[64,2048]{1,0:T(8,128)} %get-tuple-element.72) | copy-start | bytes 1572868

commit v3 on v2

--- a/solution.py
+++ b/solution.py
@@ -98,11 +98,11 @@
     def copy(self, step):
         to = lax.rem(self.me + step, self.total)
         return remote(
-            self.block_of(to), self.landing.at[self.me], self.send.at[step], self.recv.at[step], (to // 2, to % 2)
+            self.block_of(to), self.landing, self.send.at[step], self.recv.at[step], (to // 2, to % 2)
         )
 
     def own(self):
-        return pltpu.make_async_copy(self.block_of(self.me), self.landing.at[self.me], self.send.at[0])
+        return pltpu.make_async_copy(self.block_of(self.me), self.landing, self.send.at[0])
 
     def each(self, act):
         def body(step, carry):
@@ -133,30 +133,28 @@
 
 
 class Gather:
-    def __init__(self, chunks, line, outs, z_send, z_recv, send_sem, recv_sem):
-        self.chunks, self.line, self.outs = chunks, line, outs
+    def __init__(self, batches, line, sources, outs, z_send, z_recv, send_sem, recv_sem):
+        self.batches, self.line, self.sources, self.outs = batches, line, sources, outs
+        self.chunks = [chunk for batch in batches for chunk in batch]
         self.z_send, self.z_recv, self.send_sem, self.recv_sem = z_send, z_recv, send_sem, recv_sem
         self.z, self.x, self.c, self.y = where_am_i()
         z, x, c, y = self.z, self.x, self.c, self.y
         self.x_side, self.y_side, self.sibling = device(z, 1 - x, c, y), device(z, x, c, 1 - y), device(z, x, 1 - c, y)
 
-    def hop(self, k, way, j):
-        seg, _, start, cols = self.chunks[k]
-        z, x, c, y, line = self.z, self.x, self.c, self.y, self.line
-        step = 1 - 2 * way
-        going, coming = z - step * j, z - step * (j + 1)
-        sends = (going >= 0) & (going < line) & (z + step >= 0) & (z + step < line)
-        receives = (coming >= 0) & (coming < line)
-
-        def copy(owner):
-            ref = self.outs[seg].at[y, owner, x, c, :, pl.ds(start, cols)]
-            return remote(ref, ref, self.z_send.at[k, way, j], self.z_recv.at[k, way, j], device(z + step, x, c, y))
-
-        return sends, (lambda: copy(going)), receives, (lambda: copy(coming))
+    def part(self, k, yy, zz, xx):
+        seg, _, start, cols, row, rows = self.chunks[k]
+        return self.outs[seg].at[yy, zz, xx, self.c, pl.ds(row, rows), pl.ds(start, cols)]
+
+    def along(self, k, step):
+        seg, _, start, cols, row, rows = self.chunks[k]
+        source = self.sources[seg].at[pl.ds(row, rows), pl.ds(start, cols)]
+        to = device(lax.rem(self.z + step, self.line), self.x, self.c, self.y)
+        return remote(
+            source, self.part(k, self.y, self.z, self.x), self.z_send.at[k, step - 1], self.z_recv.at[k, step - 1], to
+        )
 
     def group(self, k, slot, at, target):
-        seg, _, start, cols = self.chunks[k]
-        ref = self.outs[seg].at[at[0], :, at[1], self.c, :, pl.ds(start, cols)]
+        ref = self.part(k, at[0], slice(None), at[1])
         return remote(ref, ref, self.send_sem.at[k, slot], self.recv_sem.at[k, slot], target)
 
     def groups(self, k):
@@ -165,64 +163,52 @@
             return [(y, x), (y, 1 - x), (1 - y, x), (1 - y, 1 - x)], self.x_side, self.y_side
         return [(y, x), (1 - y, x), (y, 1 - x), (1 - y, 1 - x)], self.y_side, self.x_side
 
-    def line_stage(self, j):
-        def stage(k):
-            for way in range(2):
-                if j > 0:
-                    _, _, receives, landed = self.hop(k, way, j - 1)
-
-                    @pl.when(receives)
-                    def _():
-                        landed().wait_recv()
-
-                if j < self.line - 1:
-                    sends, copy, _, _ = self.hop(k, way, j)
-
-                    @pl.when(sends)
-                    def _():
-                        copy().start()
-
-        return stage
-
-    def first_stage(self, k):
-        self.line_stage(self.line - 1)(k)
+    def step(self, k, stage):
         order, first, second = self.groups(k)
-        self.group(k, 0, order[0], first).start()
-        self.group(k, 1, order[0], second).start()
-        self.group(k, 3, order[0], self.sibling).start()
-
-    def second_stage(self, k):
-        order, first, second = self.groups(k)
-        self.group(k, 0, order[1], first).wait_recv()
-        self.group(k, 2, order[1], second).start()
-        self.group(k, 4, order[1], self.sibling).start()
-
-    def last_stage(self, k):
-        order, first, second = self.groups(k)
-        self.group(k, 1, order[2], second).wait_recv()
-        self.group(k, 5, order[2], self.sibling).start()
-        self.group(k, 2, order[3], second).wait_recv()
-        self.group(k, 6, order[3], self.sibling).start()
+        if stage == 0:
+            for step in range(1, self.line):
+                self.along(k, step).start()
+        elif stage == 1:
+            for step in range(1, self.line):
+                self.along(k, step).wait_recv()
+            self.group(k, 0, order[0], first).start()
+            self.group(k, 1, order[0], second).start()
+            self.group(k, 3, order[0], self.sibling).start()
+        elif stage == 2:
+            self.group(k, 0, order[1], first).wait_recv()
+            self.group(k, 2, order[1], second).start()
+            self.group(k, 4, order[1], self.sibling).start()
+        else:
+            self.group(k, 1, order[2], second).wait_recv()
+            self.group(k, 5, order[2], self.sibling).start()
+            self.group(k, 2, order[3], second).wait_recv()
+            self.group(k, 6, order[3], self.sibling).start()
+
+    def members(self, batch):
+        before = sum(len(b) for b in self.batches[:batch])
+        return range(before, before + len(self.batches[batch]))
 
     def stages(self):
-        return [self.line_stage(j) for j in range(self.line - 1)] + [self.first_stage, self.second_stage, self.last_stage]
-
-    def finish(self, k):
-        order, _, _ = self.groups(k)
-        for slot, at in ((3, 0), (4, 1), (5, 2), (6, 3)):
-            self.group(k, slot, order[at], self.sibling).wait_recv()
+        def make(stage):
+            def act(batch):
+                for k in self.members(batch):
+                    self.step(k, stage)
+
+            return act
+
+        return [make(stage) for stage in range(4)]
+
+    def finish(self, batch):
+        for k in self.members(batch):
+            order, _, _ = self.groups(k)
+            for slot, at in ((3, 0), (4, 1), (5, 2), (6, 3)):
+                self.group(k, slot, order[at], self.sibling).wait_recv()
 
     def sent(self):
         for k in range(len(self.chunks)):
             order, _, _ = self.groups(k)
-            for way in range(2):
-                for j in range(self.line - 1):
-                    sends, copy, _, _ = self.hop(k, way, j)
-
-                    @pl.when(sends)
-                    def _():
-                        copy().wait_send()
-
+            for step in range(1, self.line):
+                self.along(k, step).wait_send()
             for slot, at in ((0, 0), (1, 0), (2, 1), (3, 0), (4, 1), (5, 2), (6, 3)):
                 self.group(k, slot, order[at], self.sibling).wait_send()
 
@@ -237,30 +223,45 @@
 
 
 class Scatter:
-    def __init__(self, chunks, line, sources, totals, landing, core_s, own_s, first_b, second_b, line_b, sems):
-        self.chunks, self.line, self.sources, self.totals = chunks, line, sources, totals
+    def __init__(self, batches, line, sources, totals, landing, core_s, own_s, first_b, second_b, line_b, sems):
+        self.batches, self.line, self.sources, self.totals = batches, line, sources, totals
+        self.chunks = [chunk for batch in batches for chunk in batch]
         self.landing, self.core_s, self.own_s = landing, core_s, own_s
         self.first_b, self.second_b, self.line_b = first_b, second_b, line_b
         self.own_sem, self.load_sem, self.send_sem, self.recv_sem, self.z_send, self.z_recv = sems
         self.z, self.x, self.c, self.y = where_am_i()
         z, x, c, y = self.z, self.x, self.c, self.y
         self.x_side, self.y_side, self.sibling = device(z, 1 - x, c, y), device(z, x, c, 1 - y), device(z, x, 1 - c, y)
+        self.spot = {}
+        for b, batch in enumerate(batches):
+            column = 0
+            for k in self.members(b):
+                self.spot[k] = (b, column)
+                column += self.chunks[k][3]
+
+    def members(self, batch):
+        before = sum(len(b) for b in self.batches[:batch])
+        return range(before, before + len(self.batches[batch]))
+
+    def source(self, k, c):
+        seg, _, start, cols = self.chunks[k]
+        return self.sources[seg].at[:, :, :, c, :, pl.ds(start, cols)]
 
     def core_copy(self, k):
-        seg, _, start, cols = self.chunks[k]
-        source = self.sources[seg].at[:, :, :, 1 - self.c, :, pl.ds(start, cols)]
-        return remote(source, self.landing[k], self.send_sem.at[k, 0], self.recv_sem.at[k, 0], self.sibling)
+        return remote(
+            self.source(k, 1 - self.c), self.landing[k], self.send_sem.at[k, 0], self.recv_sem.at[k, 0], self.sibling
+        )
 
     def core(self, k):
-        return self.core_s.at[k % 3, :, :, :, :, pl.ds(0, self.chunks[k][3])]
+        batch, column = self.spot[k]
+        return self.core_s.at[batch % 3, :, :, :, :, pl.ds(column, self.chunks[k][3])]
 
     def own(self, k):
-        return self.own_s.at[k % 2, :, :, :, :, pl.ds(0, self.chunks[k][3])]
+        batch, column = self.spot[k]
+        return self.own_s.at[batch % 2, :, :, :, :, pl.ds(column, self.chunks[k][3])]
 
     def own_copy(self, k):
-        seg, _, start, cols = self.chunks[k]
-        source = self.sources[seg].at[:, :, :, self.c, :, pl.ds(start, cols)]
-        return pltpu.make_async_copy(source, self.own(k), self.own_sem.at[k])
+        return pltpu.make_async_copy(self.source(k, self.c), self.own(k), self.own_sem.at[k])
 
     def load_copy(self, k):
         return pltpu.make_async_copy(self.landing[k], self.core(k), self.load_sem.at[k])
@@ -277,97 +278,67 @@
             return remote(first.at[:, 1 - self.x], self.second_b[k], *sems, self.x_side)
         return remote(first.at[1 - self.y], self.second_b[k], *sems, self.y_side)
 
-    def line_copy(self, k, way, owner):
-        to = device(self.z + 1 - 2 * way, self.x, self.c, self.y)
+    def line_copy(self, k, step):
+        owner = lax.rem(self.z + step, self.line)
         return remote(
-            self.second_b[k].at[owner], self.line_b[k].at[owner + 1 - way],
-            self.z_send.at[k, way, owner], self.z_recv.at[k, way, owner], to,
-        )
-
-    def core_stage(self, k):
-        self.core_copy(k).start()
-
-    def load_stage(self, k):
-        self.core_copy(k).wait_recv()
-        self.load_copy(k).start()
-        self.own_copy(k).start()
-
-    def first_stage(self, k):
-        line = self.line
-        self.load_copy(k).wait()
-        self.own_copy(k).wait()
-        at = lambda i: (i // (2 * line), (i // 2) % line, i % 2)
-        add_into(self.core(k), self.own(k), 4 * line, at, at)
-        self.first_copy(k).start()
-
-    def second_stage(self, k):
-        line, x, y = self.line, self.x, self.y
-        self.first_copy(k).wait_recv()
-        if self.chunks[k][1] == 0:
-            add_into(self.first_b[k], self.core(k), 2 * line, lambda i: (i // 2, i % 2), lambda i: (y, i // 2, i % 2))
+            self.second_b[k].at[owner], self.line_b[k].at[step - 1],
+            self.z_send.at[k, step - 1], self.z_recv.at[k, step - 1], device(owner, self.x, self.c, self.y),
+        )
+
+    def step(self, k, stage):
+        line, x, y, z = self.line, self.x, self.y, self.z
+        early = self.chunks[k][1] == 0
+        if stage == 0:
+            self.core_copy(k).start()
+        elif stage == 1:
+            self.core_copy(k).wait_recv()
+            self.load_copy(k).start()
+            self.own_copy(k).start()
+        elif stage == 2:
+            self.load_copy(k).wait()
+            self.own_copy(k).wait()
+            at = lambda i: (i // (2 * line), (i // 2) % line, i % 2)
+            add_into(self.core(k), self.own(k), 4 * line, at, at)
+            self.first_copy(k).start()
+        elif stage == 3:
+            self.first_copy(k).wait_recv()
+            if early:
+                there, here = (lambda i: (i // 2, i % 2)), (lambda i: (y, i // 2, i % 2))
+            else:
+                there, here = (lambda i: (i // line, i % line)), (lambda i: (i // line, i % line, x))
+            add_into(self.first_b[k], self.core(k), 2 * line, there, here)
+            self.second_copy(k).start()
+            self.first_copy(k).wait_send()
+        elif stage == 4:
+            self.second_copy(k).wait_recv()
+            here = (lambda i: (i, x)) if early else (lambda i: (y, i))
+            add_into(self.second_b[k], self.first_b[k], line, lambda i: (i,), here)
+            for step in range(1, line):
+                self.line_copy(k, step).start()
         else:
-            add_into(
-                self.first_b[k], self.core(k), 2 * line,
-                lambda i: (i // line, i % line), lambda i: (i // line, i % line, x),
-            )
-        self.second_copy(k).start()
-        self.first_copy(k).wait_send()
-
-    def third_stage(self, k):
-        x, y = self.x, self.y
-        self.second_copy(k).wait_recv()
-        if self.chunks[k][1] == 0:
-            add_into(self.second_b[k], self.first_b[k], self.line, lambda i: (i,), lambda i: (i, x))
-        else:
-            add_into(self.second_b[k], self.first_b[k], self.line, lambda i: (i,), lambda i: (y, i))
-
-    def line_stage(self, j):
-        def stage(k):
-            if j == 0:
-                self.third_stage(k)
-            for way in range(2):
-                place = j if way == 0 else self.line - 1 - j
-                owners = range(self.line - 1, place, -1) if way == 0 else range(place)
-
-                @pl.when(self.z == place)
-                def _():
-                    for owner in owners:
-                        if j > 0:
-                            self.line_copy(k, way, owner).wait_recv()
-                            self.second_b[k][owner] = self.second_b[k][owner] + self.line_b[k][owner + 1 - way]
-                        self.line_copy(k, way, owner).start()
-
-        return stage
-
-    def last_stage(self, k):
-        seg, _, start, cols = self.chunks[k]
-        z = self.z
-        total = self.totals[seg]
-        total[:, pl.ds(start, cols)] = self.second_b[k][z].astype(F32)
-        for way in range(2):
-
-            @pl.when((z > 0) if way == 0 else (z < self.line - 1))
-            def _():
-                self.line_copy(k, way, z).wait_recv()
-                total[:, pl.ds(start, cols)] += self.line_b[k][z + 1 - way].astype(F32)
+            seg, _, start, cols = self.chunks[k]
+            total = self.second_b[k][z].astype(F32)
+            for step in range(1, line):
+                self.line_copy(k, step).wait_recv()
+                total = total + self.line_b[k][step - 1].astype(F32)
+            self.totals[seg][:, pl.ds(start, cols)] = total
 
     def stages(self):
-        return (
-            [self.core_stage, self.load_stage, self.first_stage, self.second_stage]
-            + [self.line_stage(j) for j in range(self.line - 1)]
-            + [self.last_stage]
-        )
+        def make(stage):
+            def act(batch):
+                for k in self.members(batch):
+                    self.step(k, stage)
+
+            return act
+
+        return [make(stage) for stage in range(6)]
 
     def sent(self):
         for k in range(len(self.chunks)):
             self.core_copy(k).wait_send()
             self.second_copy(k).wait_send()
-            for way in range(2):
-                for owner in range(self.line):
-
-                    @pl.when((self.z < owner) if way == 0 else (self.z > owner))
-                    def _():
-                        self.line_copy(k, way, owner).wait_send()
+            for step in range(1, self.line):
+                self.line_copy(k, step).wait_send()
 
 
 def switch_on(index, cases):
@@ -379,15 +350,25 @@
     return pl.ds(pl.multiple_of(start, 128), size)
 
 
-def ahead_kernel(chunks, line, width, *refs):
-    (products, seg_qkv, seg_proj, seg_fc1, seg_fc2, tok, cot, vecs, hidden_bias, boosts, kmask_ref, qmask_ref,
-     qkv_f, proj_f, fc1_f, fc2_f, x_f, cot_f, g1_f, g2_f,
-     mod_ref, ql_ref, kl_ref, vl_ref, mix_ref, stat_ref, out_ref, gmid_ref, rows_ref, gb1_ref,
-     arrived, att_ref, x_s, cot_s, one_s, acc_s, mid_s, twot_s, back_s, backt_s, gacc_s, w_s, grad_s,
-     a_send, a_recv, local_sem, pair_sem, z_send, z_recv, send_sem, recv_sem, load_sem, w_sem, grad_sem) = refs
+def owner_maps(owners, entries, width, model):
+    inner = model // width * entries
+    at = lax.broadcasted_iota(jnp.int32, (inner, model), 1)
+    place = lax.broadcasted_iota(jnp.int32, (inner, model), 0)
+    spread = jnp.where(at // width * entries + at % entries == place, 1.0, 0.0).astype(BF16)
+    at = lax.broadcasted_iota(jnp.int32, (owners, model), 1)
+    owner = lax.broadcasted_iota(jnp.int32, (owners, model), 0)
+    return spread, jnp.where(at % width // entries == owner, 1.0, 0.0)
+
+
+def ahead_kernel(batches, line, width, *refs):
+    (signals, ada, extra, seg_qkv, seg_proj, seg_fc1, seg_fc2, tok, cot, kmask_ref, qmask_ref,
+     qkv_f, proj_f, fc1_f, fc2_f, g1_f, g2_f, ql_f, kl_f, vl_f, mix_f, x_f,
+     boosts, mod_ref, stat_ref, out_ref, gmid_ref, rows_ref, gb1_ref, sig_s, ada_flat,
+     products, arrived, vecs, hidden_bias, x_s, ql_ref, kl_ref, vl_ref, mix_ref, att_ref, cot_s, one_s, acc_s, mid_s, twot_s, back_s, backt_s, gacc_s, w_s, grad_s,
+     a_send, a_recv, b_send, b_recv, save_sem, local_sem, pair_sem, z_send, z_recv, send_sem, recv_sem, w_sem, grad_sem) = refs
     z, x, c, y = where_am_i()
     total = 8 * line
-    padded, model = tok.shape[1], tok.shape[2]
+    padded, model = tok.shape[1:]
     half_cols = mod_ref.shape[1] // 2
     heads = 256 // width
     outs = [qkv_f, proj_f, fc1_f, fc2_f]
@@ -397,21 +378,27 @@
     ]
     for copy in own:
         copy.start()
-    mine, others = pl.ds(y * padded, padded), pl.ds((1 - y) * padded, padded)
-    pairs = []
-    for p, (source, target, inside) in enumerate(((tok, x_f, x_s), (cot, cot_f, cot_s))):
-        partner = device(z, x, c, 1 - y)
-        pairs.append((
-            pltpu.make_async_copy(source.at[y], target.at[mine], pair_sem.at[p, 0]),
-            remote(source.at[1 - y], target.at[mine], pair_sem.at[p, 1], pair_sem.at[p, 2], partner),
-            pltpu.make_async_copy(target, inside, pair_sem.at[p, 3]),
-        ))
-    exchange = Exchange(total, lambda to: products.at[to], arrived, a_send, a_recv)
-    gather = Gather(chunks, line, outs, z_send, z_recv, send_sem, recv_sem)
-    ticks = Ticks(len(chunks), gather.stages())
+    mine = pl.ds(y * padded, padded)
+    pairs = [
+        (
+            pltpu.make_async_copy(source.at[y], inside.at[mine], pair_sem.at[p, 0]),
+            remote(
+                source.at[1 - y], inside.at[mine], pair_sem.at[p, 1], pair_sem.at[p, 2], device(z, x, c, 1 - y)
+            ),
+        )
+        for p, (source, inside) in enumerate(((tok, x_s), (cot, cot_s)))
+    ]
+    me = (lax.axis_index("dp"), y)
+    signal_exchange = Exchange(total, lambda to: signals.at[to // 2], sig_s.at[me], b_send, b_recv)
+    exchange = Exchange(total, lambda to: products.at[to // 2, to % 2], arrived.at[me], a_send, a_recv)
+    gather = Gather(
+        batches, line, [seg_qkv, seg_proj, seg_fc1, seg_fc2], outs, z_send, z_recv, send_sem, recv_sem
+    )
+    ticks = Ticks(len(batches), gather.stages())
     greet_all(total)
-    exchange.start()
-    for copy in pairs[0][:2]:
+    signal_exchange.start()
+    ticks.run(0, 1)
+    for copy in pairs[0]:
         copy.start()
     for copy in own:
         copy.wait()
@@ -446,21 +433,51 @@
         for copy in copies:
             copy.wait()
 
-    ticks.run(0, 2)
+    for j in range(6):
+        ada_flat[:, j * half_cols : (j + 1) * half_cols] = ada[:, j, :]
+    signal_exchange.wait()
+    slots, owners = sig_s.shape[1], sig_s.shape[0]
+    for slot in range(slots):
+        rows_in = sig_s[:, 0, slot, : ada.shape[0]].astype(BF16)
+        for j in range(8):
+            block = jnp.broadcast_to(extra[j : j + 1], (owners, half_cols))
+            if j < 6:
+                block = block + mm(rows_in, ada_flat[:, j * half_cols : (j + 1) * half_cols])
+            products[:, slot, j, :] = block
+    exchange.start()
+    ticks.run(1, 2)
+    for copy in pairs[1]:
+        copy.start()
+    ticks.run(2, 4)
     exchange.wait()
-    parts = jnp.sum(arrived[...].reshape(total // 2, 2, 8, half_cols), 0)
-    mod_ref[:, :half_cols] = parts[0]
-    mod_ref[:, half_cols:] = parts[1]
-    ticks.run(2, 4)
-    wait_loads(pairs[0][:2])
-    pairs[0][2].start()
-    start_loads(pairs[1][:2])
-    pairs[0][2].wait()
-    ticks.run(4, 5)
+    for half in range(2):
+        mod_ref[:, half * half_cols : (half + 1) * half_cols] = jnp.sum(arrived[:, half], 0)
+    entries = width // owners
+    spread, owner_of = owner_maps(owners, entries, width, model)
+    letters = [arrived[:, half, 6, :] for half in range(2)]
+    piece = heads * entries * 2
+    blocks = [
+        jnp.concatenate([letter[:, r * piece : (r + 1) * piece] for letter in letters], 1) for r in range(4)
+    ] + [
+        letters[half][:, (4 + 2 * part) * piece : (6 + 2 * part) * piece] for half in range(2) for part in range(2)
+    ]
+    turned_out = mm(jnp.concatenate(blocks, 0).astype(BF16), spread)
+    for r in range(8):
+        row = jnp.sum(turned_out[r * owners : (r + 1) * owners] * owner_of, 0, keepdims=True)
+        if r < 4:
+            vecs[r : r + 1] = row
+        else:
+            hidden_bias[0:1, (r - 4) * model : (r - 3) * model] = row
+    boosts[...] = jnp.zeros_like(boosts)
+    for half in range(2):
+        lift = jnp.exp(arrived[0, half, 7:8, : 2 * heads])
+        for sub in range(2):
+            boosts[half * 2 + sub, 0:1, 0:heads] = lift[:, sub * heads : (sub + 1) * heads]
+    wait_loads(pairs[0])
     normed, _ = norm_rows(x_s[...].astype(F32))
     one_s[...] = (normed * (1.0 + mod_ref[2:3]) + mod_ref[4:5]).astype(BF16)
     acc_s[...] = jnp.zeros_like(acc_s)
-    ticks.run(5, 7)
+    ticks.run(4, 5)
     gather.finish(0)
     gather.finish(1)
     start_loads(load_attend(0))
@@ -468,14 +485,13 @@
     ones = jnp.ones((x_s.shape[0], width), BF16)
 
     def attend(i, carry):
-        def before_third():
-            ticks.run(8, 9)
+        @pl.when(i == 2)
+        def _():
+            ticks.run(5, 6)
             gather.finish(2)
-            gather.finish(3)
             start_loads(load_attend(2))
             start_loads(load_attend(3))
 
-        switch_on(i, {1: lambda: ticks.run(7, 8), 2: before_third, 3: lambda: ticks.run(9, 10)})
         slot = lax.rem(i, 2)
         at = slot * 2 + i // 2
         wait_loads([
@@ -529,9 +545,13 @@
         return carry
 
     lax.fori_loop(0, 4, attend, 0)
-    ticks.run(10, 11)
-    wait_loads(pairs[1][:2])
-    pairs[1][2].start()
+    saves = [
+        pltpu.make_async_copy(inside, outside, save_sem.at[n])
+        for n, (inside, outside) in enumerate(
+            ((ql_ref, ql_f), (kl_ref, kl_f), (vl_ref, vl_f), (mix_ref, mix_f), (x_s, x_f))
+        )
+    ]
+    start_loads(saves)
     attended = acc_s[...] + vecs[2:3]
     att_ref[...] = attended.astype(BF16)
     middle = x_s[...].astype(F32) + mod_ref[0:1] * attended
@@ -540,7 +560,7 @@
     two = (normed * (1.0 + mod_ref[3:4]) + mod_ref[5:6]).astype(BF16)
     one_s[...] = two
     twot_s[...] = two.T
-    pairs[1][2].wait()
+    wait_loads(pairs[1])
     back = (mod_ref[1:2] * cot_s[...].astype(F32)).astype(BF16)
     back_s[...] = back
     backt_s[...] = back.T
@@ -560,18 +580,14 @@
 
         def before(p):
             def act():
-                if p > 0:
-                    ticks.run(10 + 2 * p, 11 + 2 * p)
-                gather.finish(4 + 2 * p)
-                gather.finish(5 + 2 * p)
+                ticks.run(6 + p, 7 + p)
+                gather.finish(3 + p)
                 start_loads(load_feed(0, p))
                 start_loads(load_feed(1, p))
 
             return act
 
-        cases = {2 * p: before(p) for p in range(4)}
-        cases.update({2 * p + 1: (lambda p=p: ticks.run(11 + 2 * p, 12 + 2 * p)) for p in range(3)})
-        switch_on(i, cases)
+        switch_on(i, {2 * p: before(p) for p in range(4)})
         wait_loads(load_feed(half, part))
         weights = w_s[half].reshape(model, 1024)
         w1, w2 = weights[:, :512], weights[:, 512:]
@@ -616,59 +632,62 @@
     gb1_ref[1:8] = jnp.zeros((7, gb1_ref.shape[1]), F32)
     for half in range(2):
         wait_loads(store_feed(half, 3))
+    wait_loads(saves)
     gather.sent()
 
 
-def run_ahead(chunks, line, products, segments, tok, cot, vecs, hidden_bias, boosts, kmask, qmask, width, cid):
+def run_ahead(batches, line, signals, ada, extra, segments, tok, cot, kmask, qmask, hidden_cols, width, cid):
     padded, model = tok.shape[1:]
     rows = 2 * padded
-    total, count = 8 * line, len(chunks)
+    total, count = 8 * line, sum(len(batch) for batch in batches)
     own_rows = segments[0].shape[0]
-    hidden_cols = hidden_bias.shape[1]
     anywhere, inside = pl.BlockSpec(memory_space=pl.ANY), pl.BlockSpec(memory_space=pltpu.VMEM)
     full = [jax.ShapeDtypeStruct((2, line, 2, 2) + s.shape, BF16) for s in segments]
     flat = jax.ShapeDtypeStruct((rows, model), BF16)
     turned = jax.ShapeDtypeStruct((model, rows), BF16)
+    flat_s, turned_s, wide_s = (
+        pltpu.VMEM((rows, model), BF16), pltpu.VMEM((model, rows), BF16), pltpu.VMEM((rows, model), F32)
+    )
     block = (line, 2, 2, own_rows)
     dma = pltpu.SemaphoreType.DMA
+    letters = pltpu.VMEM((total // 2, 2, 8, model // 2), F32)
     return pl.pallas_call(
-        functools.partial(ahead_kernel, chunks, line, width),
-        in_specs=[anywhere] * 7 + [inside] * 5,
-        out_shape=full + [flat, flat, full[2], full[3]] + [
-            jax.ShapeDtypeStruct((8, model), F32), turned, turned, flat, flat,
+        functools.partial(ahead_kernel, batches, line, width),
+        in_specs=[inside] * 7 + [anywhere] * 2 + [inside] * 2,
+        out_shape=full + [full[2], full[3], turned, turned, flat, flat, flat] + [
+            jax.ShapeDtypeStruct((model // 256, 8, 128), F32), jax.ShapeDtypeStruct((8, model), F32),
             jax.ShapeDtypeStruct((model // 256, 2, 8, rows), F32), flat,
             jax.ShapeDtypeStruct((rows, model), F32), jax.ShapeDtypeStruct((8, model), F32),
-            jax.ShapeDtypeStruct((8, hidden_cols), F32),
+            jax.ShapeDtypeStruct((8, hidden_cols), F32), jax.ShapeDtypeStruct((total // 2, 2, 8, 128), F32),
+            jax.ShapeDtypeStruct((own_rows, 3 * model), BF16),
         ],
-        out_specs=[anywhere] * 8 + [inside] * 10,
+        out_specs=[anywhere] * 11 + [inside] * 9,
         scratch_shapes=[
-            pltpu.VMEM(products.shape, F32), pltpu.VMEM((rows, model), BF16),
-            pltpu.VMEM((rows, model), BF16), pltpu.VMEM((rows, model), BF16),
-            pltpu.VMEM((rows, model), BF16), pltpu.VMEM((rows, model), F32), pltpu.VMEM((rows, model), F32),
-            pltpu.VMEM((model, rows), BF16), pltpu.VMEM((rows, model), BF16), pltpu.VMEM((model, rows), BF16),
-            pltpu.VMEM((rows, model), F32), pltpu.VMEM((2,) + block + (1024,), BF16),
-            pltpu.VMEM((2, 2) + block + (512,), BF16),
-            dma((total,)), dma((total,)), dma((4,)), dma((2, 4)),
-            dma((count, 2, line - 1)), dma((count, 2, line - 1)), dma((count, 7)), dma((count, 7)),
-            dma((2,)), dma((2, 2)), dma((2, 2)),
+            letters, letters, pltpu.VMEM((8, model), F32),
+            pltpu.VMEM((8, hidden_cols), F32), flat_s, turned_s, turned_s, flat_s, flat_s,
+            flat_s, flat_s, flat_s, wide_s, wide_s, turned_s, flat_s, turned_s, wide_s,
+            pltpu.VMEM((2,) + block + (1024,), BF16), pltpu.VMEM((2, 2) + block + (512,), BF16),
+            dma((total,)), dma((total,)), dma((total,)), dma((total,)), dma((5,)), dma((4,)), dma((2, 3)),
+            dma((count, line - 1)), dma((count, line - 1)), dma((count, 7)), dma((count, 7)),
+            dma((2, 2)), dma((2, 2)),
         ],
         compiler_params=pltpu.CompilerParams(
             collective_id=cid, has_side_effects=True, vmem_limit_bytes=VMEM_LIMIT
         ),
         name="ahead",
-    )(products, *segments, tok, cot, vecs, hidden_bias, boosts, kmask, qmask)
-
-
-def behind_kernel(chunks, line, width, levels, *refs):
-    count = len(chunks)
+    )(signals, ada, extra, *segments, tok, cot, kmask, qmask)
+
+
+def behind_kernel(batches, line, width, levels, *refs):
+    count = sum(len(batch) for batch in batches)
     (x_f, qkv_f, proj_f, g1_f, g2_f, result, ql_f, kl_f, vl_f, mix_f,
-     gmid_ref, mod_ref, feed_rows, stat_ref, boosts, kmask_ref, qmask_ref) = refs[:17]
-    (gqkv_f, gproj_f, act_pair, tok_pair) = refs[17:21]
-    landing = refs[21 : 21 + count]
-    (t_qkv, t_proj, t_fc1, t_fc2, sums_ref, rows_ref, mods_ref) = refs[21 + count : 28 + count]
+     gmid_ref, mod_ref, feed_rows, hidden_ref, stat_ref, boosts, kmask_ref, qmask_ref) = refs[:18]
+    (gqkv_f, gproj_f, act_far, tok_far) = refs[18:22]
+    landing = refs[22 : 22 + count]
+    (t_qkv, t_proj, t_fc1, t_fc2, mods_ref, x_s) = refs[22 + count : 28 + count]
     rest = refs[28 + count :]
     first_b, second_b, line_b = rest[:count], rest[count : 2 * count], rest[2 * count : 3 * count]
-    (core_s, own_s, x_s, ga_s, gat_s, onet_s, acc_s, turn_s, flat_s, w_s, grad_s, gm_s,
+    (core_s, own_s, ga_s, gat_s, onet_s, acc_s, turn_s, flat_s, w_s, grad_s, gm_s, vec_s, rows_ref, heads_s,
      a_send, a_recv, pair_sem, x_sem, w_sem, grad_sem,
      own_sem, load_sem, send_sem, recv_sem, z_send, z_recv) = rest[3 * count :]
     z, x, c, y = where_am_i()
@@ -678,37 +697,35 @@
     heads = 256 // width
     partner = device(z, x, c, 1 - y)
     scatter = Scatter(
-        chunks, line, [gqkv_f, gproj_f, g1_f, g2_f], [t_qkv, t_proj, t_fc1, t_fc2], landing, core_s, own_s,
+        batches, line, [gqkv_f, gproj_f, g1_f, g2_f], [t_qkv, t_proj, t_fc1, t_fc2], landing, core_s, own_s,
         first_b, second_b, line_b, (own_sem, load_sem, send_sem, recv_sem, z_send, z_recv),
     )
-    ticks = Ticks(count, scatter.stages())
-    mine, others = pl.ds(y * padded, padded), pl.ds((1 - y) * padded, padded)
+    ticks = Ticks(len(batches), scatter.stages())
+    others = pl.ds((1 - y) * padded, padded)
     pairs = [
-        (
-            pltpu.make_async_copy(source.at[mine], target.at[y], pair_sem.at[p, 0]),
-            remote(source.at[others], target.at[y], pair_sem.at[p, 1], pair_sem.at[p, 2], partner),
-        )
-        for p, (source, target) in enumerate(((result, act_pair), (x_s, tok_pair)))
+        remote(source.at[others], target, pair_sem.at[p, 0], pair_sem.at[p, 1], partner)
+        for p, (source, target) in enumerate(((result, act_far), (x_s, tok_far)))
     ]
     load_x = pltpu.make_async_copy(x_f, x_s, x_sem.at[0])
     load_x.start()
     greet_all(total)
     ticks.run(0, 1)
+    pairs[0].start()
 
     def load_group(i):
-        slot = lax.rem(i, 2)
-        sub, at = i // 2, slot * 2 + i // 2
+        half = lax.rem(i, 2)
+        sub, at = i // 2, half * 2 + i // 2
         turned = pl.ds(pl.multiple_of(at * 256, 256), 256)
         cols = columns(at * 256, 256)
         pieces = [
-            (qkv_f.at[slot, :, :, :, :, columns(sub * 768, 768)], w_s.at[slot, :, :, :, :, pl.ds(0, 768)]),
-            (proj_f.at[slot, :, :, :, :, columns(sub * 256, 256)], w_s.at[slot, :, :, :, :, pl.ds(768, 256)]),
-            (ql_f.at[turned], turn_s.at[slot, 0]),
-            (kl_f.at[turned], turn_s.at[slot, 1]),
-            (vl_f.at[:, cols], flat_s.at[slot, 0]),
-            (mix_f.at[:, cols], flat_s.at[slot, 1]),
+            (qkv_f.at[half, :, :, :, :, columns(sub * 768, 768)], w_s.at[:, :, :, :, pl.ds(0, 768)]),
+            (proj_f.at[half, :, :, :, :, columns(sub * 256, 256)], w_s.at[:, :, :, :, pl.ds(768, 256)]),
+            (ql_f.at[turned], turn_s.at[0]),
+            (kl_f.at[turned], turn_s.at[1]),
+            (vl_f.at[:, cols], flat_s.at[0]),
+            (mix_f.at[:, cols], flat_s.at[1]),
         ]
-        return [pltpu.make_async_copy(s, t, w_sem.at[slot, n]) for n, (s, t) in enumerate(pieces)]
+        return [pltpu.make_async_copy(s, t, w_sem.at[n]) for n, (s, t) in enumerate(pieces)]
 
     def store_group(i):
         half, sub = lax.rem(i, 2), i // 2
@@ -736,7 +753,12 @@
     attend_grad = (mod_ref[0:1] * gmid_ref[...]).astype(BF16)
     ga_s[...] = attend_grad
     gat_s[...] = attend_grad.T
-    rows_ref[2:3] = jnp.sum(attend_grad.astype(F32), 0, keepdims=True)
+    vec_s[2:3] = jnp.sum(attend_grad.astype(F32), 0, keepdims=True)
+    vec_s[3:4] = feed_rows[3:4]
+    for part in range(4):
+        vec_s[4 + part : 5 + part] = hidden_ref[0:1, part * model : (part + 1) * model]
+    heads_s[...] = jnp.zeros_like(heads_s)
+    lane = lax.broadcasted_iota(jnp.int32, (1, half_cols), 1)
     ticks.run(2, 3)
     load_x.wait()
     normed, _ = norm_rows(x_s[...].astype(F32))
@@ -757,22 +779,16 @@
         slot = lax.rem(i, 2)
         at = slot * 2 + i // 2
 
-        @pl.when(i < 3)
-        def _():
-            start_loads(load_group(i + 1))
-
         wait_loads(load_group(i))
         boost = boosts[at]
-        weights = w_s[slot].reshape(model, 1024)
-        mixed = flat_s[slot, 1]
-        values = flat_s[slot, 0]
-        q_all_low, k_all_low = turn_s[slot, 0], turn_s[slot, 1]
+        weights = w_s[...].reshape(model, 1024)
+        mixed = flat_s[1]
+        values = flat_s[0]
+        q_all_low, k_all_low = turn_s[0], turn_s[1]
         mixed_grad = mm(ga_s[...], weights[:, 768:]).astype(BF16)
         mixed_turned, v_turned, q_plain = mixed_grad.T, values.T, q_all_low.T
         dq_rows, dk_rows, dv_cols, scales = [], [], [], []
         for head in range(heads):
-            if head == 2:
-                switch_on(i, {n: (lambda n=n: ticks.run(3 + 2 * n, 4 + 2 * n)) for n in range(4)})
             part = slice(head * width, (head + 1) * width)
             lift = boost[0:1, head : head + 1]
             q_bf, k_bf = q_all_low[part], k_all_low[part]
@@ -808,56 +824,61 @@
         def _():
             wait_loads(store_group(i))
 
+        switch_on(i, {1: lambda: ticks.run(4, 5), 2: lambda: ticks.run(5, 6)})
         shape = grad_s.shape[:4]
         grad_s[:, :, :, :, 0:768] = mm(onet_s[...], triple).astype(BF16).reshape(shape + (768,))
         grad_s[:, :, :, :, 768:1024] = mm(gat_s[...], mixed).astype(BF16).reshape(shape + (256,))
         start_loads(store_group(i))
         acc_s[...] += mm_nt(triple, weights[:, :768])
-        sums_ref[at, 0:1, :] = jnp.sum(dq.astype(F32), 0, keepdims=True)
-        sums_ref[at, 1:2, :] = jnp.sum(dv.astype(F32), 0, keepdims=True)
-        sums_ref[at, 2:4, :] = jnp.zeros((2, 256), F32)
+        spot = columns(at * 256, 256)
+        vec_s[0:1, spot] = jnp.sum(dq.astype(F32), 0, keepdims=True)
+        vec_s[1:2, spot] = jnp.sum(dv.astype(F32), 0, keepdims=True)
         for head in range(heads):
-            sums_ref[at, 4 + head : 5 + head, :] = jnp.broadcast_to(scales[head], (1, 256))
-
-        def end(n):
-            def act():
-                if n == 1:
-                    start_loads(pairs[0])
-                ticks.run(4 + 2 * n, 5 + 2 * n)
-
-            return act
-
-        switch_on(i, {n: end(n) for n in range(3)})
+            heads_s[0:1] += jnp.where(lane == at * heads + head, scales[head], 0.0)
+
+        @pl.when(i < 3)
+        def _():
+            start_loads(load_group(i + 1))
+
+        switch_on(i, {0: lambda: ticks.run(3, 4)})
         return carry
 
     lax.fori_loop(0, 4, group, 0)
     wait_loads(store_group(3))
-    ticks.run(10, 11)
+    ticks.run(6, 7)
     grad = acc_s[...]
     normed, inverse = norm_rows(x_s[...].astype(F32))
     x_s[...] = (
         gmid_ref[...] + norm_rows_back(grad * (1.0 + mod_ref[2:3]), normed, inverse)
     ).astype(BF16)
-    start_loads(pairs[1])
+    pairs[1].start()
     rows_ref[0:1] = jnp.sum(grad * normed, 0, keepdims=True)
     rows_ref[1:2] = jnp.sum(grad, 0, keepdims=True)
-    rows_ref[3:8] = jnp.zeros((5, model), F32)
-    for n, row in enumerate((feed_rows[4:5], feed_rows[0:1], rows_ref[0:1], feed_rows[1:2], rows_ref[1:2], feed_rows[2:3])):
-        for half in range(2):
-            gm_s[half, n : n + 1] = row[:, half * half_cols : (half + 1) * half_cols]
-    gm_s[:, 6:8] = jnp.zeros((2, 2, half_cols), F32)
-    exchange = Exchange(total, lambda to: gm_s.at[lax.rem(to, 2)], mods_ref, a_send, a_recv)
+    owners = total // 2
+    spread, owner_of = owner_maps(owners, width // owners, width, model)
+    picked = jnp.concatenate([owner_of * vec_s[r : r + 1] for r in range(8)], 0)
+    moved = sum(mm_nt(part, spread) for part in split_three(picked))
+    small = jnp.concatenate([moved[r * owners : (r + 1) * owners] for r in range(8)], 1)
+    mod_rows = (feed_rows[4:5], feed_rows[0:1], rows_ref[0:1], feed_rows[1:2], rows_ref[1:2], feed_rows[2:3])
+    for half in range(2):
+        for n, row in enumerate(mod_rows):
+            gm_s[:, half, n, :] = jnp.broadcast_to(
+                row[:, half * half_cols : (half + 1) * half_cols], (owners, half_cols)
+            )
+        gm_s[:, half, 6, :] = small
+        gm_s[:, half, 7, :] = jnp.broadcast_to(heads_s[0:1], (owners, half_cols))
+    exchange = Exchange(total, lambda to: gm_s.at[to // 2, to % 2], mods_ref.at[lax.axis_index("dp"), y], a_send, a_recv)
     exchange.start()
-    ticks.run(11, ticks.total)
+    ticks.run(7, ticks.total)
     exchange.wait()
-    for pair in pairs:
-        wait_loads(pair)
+    wait_loads(pairs)
     scatter.sent()
 
 
-def run_behind(chunks, line, levels, saved, inner, width, cid):
+def run_behind(batches, line, levels, saved, inner, width, cid):
     x_f, qkv_f, proj_f, g1_f, g2_f, result, ql, kl, vl, mix = saved
     rows, model = x_f.shape
+    chunks = [chunk for batch in batches for chunk in batch]
     total, count = 8 * line, len(chunks)
     own_rows = qkv_f.shape[4]
     anywhere, inside = pl.BlockSpec(memory_space=pl.ANY), pl.BlockSpec(memory_space=pltpu.VMEM)
@@ -867,30 +888,28 @@
         landing.append(jax.ShapeDtypeStruct((2, line, 2, own_rows, cols), BF16))
         first_b.append(pltpu.VMEM(((line, 2) if kind == 0 else (2, line)) + (own_rows, cols), BF16))
         second_b.append(pltpu.VMEM((line, own_rows, cols), BF16))
-        line_b.append(pltpu.VMEM((line + 1, own_rows, cols), BF16))
-    most = max(chunk[3] for chunk in chunks)
+        line_b.append(pltpu.VMEM((line - 1, own_rows, cols), BF16))
+    most = max(sum(chunk[3] for chunk in batch) for batch in batches)
     sources = [qkv_f, proj_f, g1_f, g2_f]
     block = (line, 2, 2, own_rows)
     made = pl.pallas_call(
-        functools.partial(behind_kernel, chunks, line, width, levels),
-        in_specs=[anywhere] * 10 + [inside] * 7,
+        functools.partial(behind_kernel, batches, line, width, levels),
+        in_specs=[anywhere] * 10 + [inside] * 8,
         out_shape=[jax.ShapeDtypeStruct(qkv_f.shape, BF16), jax.ShapeDtypeStruct(proj_f.shape, BF16)]
-        + [jax.ShapeDtypeStruct((2, rows // 2, model), BF16)] * 2 + landing
+        + [jax.ShapeDtypeStruct((rows // 2, model), BF16)] * 2 + landing
         + [jax.ShapeDtypeStruct(s.shape[4:], F32) for s in sources]
-        + [
-            jax.ShapeDtypeStruct((model // 256, 8, 256), F32), jax.ShapeDtypeStruct((8, model), F32),
-            jax.ShapeDtypeStruct((total, 8, model // 2), F32),
-        ],
-        out_specs=[anywhere] * (4 + count) + [inside] * 7,
+        + [jax.ShapeDtypeStruct((total // 2, 2, 8, model // 2), F32), jax.ShapeDtypeStruct((rows, model), BF16)],
+        out_specs=[anywhere] * (4 + count) + [inside] * 6,
         scratch_shapes=first_b + second_b + line_b + [
             pltpu.VMEM((3, 2, line, 2, own_rows, most), BF16), pltpu.VMEM((2, 2, line, 2, own_rows, most), BF16),
-            pltpu.VMEM((rows, model), BF16), pltpu.VMEM((rows, model), BF16), pltpu.VMEM((model, rows), BF16),
-            pltpu.VMEM((model, rows), BF16), pltpu.VMEM((rows, model), F32), pltpu.VMEM((2, 2, 256, rows), BF16),
-            pltpu.VMEM((2, 2, rows, 256), BF16), pltpu.VMEM((2,) + block + (1024,), BF16),
-            pltpu.VMEM(block + (1024,), BF16), pltpu.VMEM((2, 8, model // 2), F32),
-            dma((total,)), dma((total,)), dma((2, 3)), dma((1,)), dma((2, 6)), dma((2,)),
+            pltpu.VMEM((rows, model), BF16), pltpu.VMEM((model, rows), BF16),
+            pltpu.VMEM((model, rows), BF16), pltpu.VMEM((rows, model), F32), pltpu.VMEM((2, 256, rows), BF16),
+            pltpu.VMEM((2, rows, 256), BF16), pltpu.VMEM(block + (1024,), BF16),
+            pltpu.VMEM(block + (1024,), BF16), pltpu.VMEM((total // 2, 2, 8, model // 2), F32), pltpu.VMEM((8, model), F32), pltpu.VMEM((8, model), F32),
+            pltpu.VMEM((8, model // 2), F32),
+            dma((total,)), dma((total,)), dma((2, 2)), dma((1,)), dma((6,)), dma((2,)),
             dma((count,)), dma((count,)), dma((count, 3)), dma((count, 3)),
-            dma((count, 2, line)), dma((count, 2, line)),
+            dma((count, line - 1)), dma((count, line - 1)),
         ],
         compiler_params=pltpu.CompilerParams(
             collective_id=cid, has_side_effects=True, vmem_limit_bytes=VMEM_LIMIT
@@ -905,15 +924,23 @@
 
 
 def gather_list():
-    return [(0, 1, 0, 768), (1, 1, 0, 256), (0, 0, 768, 768), (1, 1, 256, 256)] + [
-        (segment, int((segment, part) not in ((2, 1), (3, 3))), part * 512, 512) for part in range(4) for segment in (2, 3)
+    def both(segment, start, cols):
+        return [(segment, 0, start, cols, 0, 16), (segment, 1, start, cols, 16, 48)]
+
+    attend = [both(0, 0, 512), both(0, 512, 256) + both(1, 0, 256), both(0, 768, 768) + both(1, 256, 256)]
+    return attend + [
+        [(2, 0, part * 512, 384, 0, 64), (2, 1, part * 512 + 384, 128, 0, 64), (3, 1, part * 512, 512, 0, 64)]
+        for part in range(4)
     ]
 
 
 def scatter_list():
-    return [
-        (segment, int((segment, part) not in ((2, 1), (3, 3))), part * 512, 512) for part in range(4) for segment in (2, 3)
-    ] + [(0, 0, 0, 512), (0, 1, 512, 256), (1, 1, 0, 256), (0, 1, 768, 512), (0, 1, 1280, 256), (1, 0, 256, 256)]
+    feed = [[(s, 0, 0, 128), (s, 1, 128, 384)] for s in (2, 3)]
+    feed += [
+        [(2, 0, part * 512, 384), (2, 1, part * 512 + 384, 128), (3, 1, part * 512, 512)] for part in range(1, 4)
+    ]
+    attend = [[(0, 0, 0, 256), (0, 1, 256, 512), (1, 1, 0, 256)], [(0, 0, 768, 256), (0, 1, 1024, 512)]]
+    return feed + attend + [[(1, 0, 256, 128), (1, 1, 384, 128)]]
 
 
 def on_device_paired(
@@ -941,33 +968,15 @@
 
     cond_slots = to_slots(condition).astype(F32)
     signal = jax.nn.silu(cond_slots).astype(BF16)
-    small = jnp.concatenate(
-        [qv_bias.reshape(-1), out_bias.reshape(-1), fc1_bias.reshape(-1)] + list(split_three(head_log_scale))
-    )
-    signal_out = signal.reshape(slots, n_dp, own_rows).transpose(1, 0, 2).reshape(n_dp, 1, slots * own_rows)
-    letters = jnp.concatenate(
-        [jnp.broadcast_to(signal_out, (n_dp, 2, slots * own_rows)), jnp.broadcast_to(small, (n_dp, 2) + small.shape)], 2
-    ).reshape(n_dev, -1)
-    letters = lax.all_to_all(letters, ("dp", "mp"), 0, 0, tiled=True).reshape(n_dp, 2, -1)
-    signal_rows = letters[:, 0, : slots * own_rows].reshape(n_dev, own_rows)
-    small_full = letters[:, :, slots * own_rows :].transpose(1, 0, 2)
-    spread_small = small_full[:, :, :scale_at].reshape(2, n_dp, vectors, entries)
-    spread_small = spread_small.transpose(0, 2, 1, 3).reshape(2, vectors, n_dp * entries).astype(F32)
-    block_rows = spread_small[:, : 4 * local_heads].reshape(2, 4, own_cols).transpose(1, 0, 2).reshape(4, model)
-    vecs = jnp.pad(block_rows, ((0, 4), (0, 0)))
-    hidden_bias = spread_small[:, 4 * local_heads :].reshape(1, 2 * hidden_cols)
-    scale_all = sum(
-        small_full[:, 0, scale_at + i * local_heads : scale_at + (i + 1) * local_heads].astype(F32) for i in range(3)
-    )
-    boost = jnp.exp(scale_all.reshape(groups, -1))
-    boosts = jnp.zeros((groups, 8, 128), F32).at[:, 0, : boost.shape[1]].set(boost)
-
-    ada_flat = ada_weight.reshape(own_rows, 6 * own_cols)
+    signals = signal.reshape(slots, n_dp, own_rows).transpose(1, 0, 2).astype(F32)
+    signals = jnp.pad(signals, ((0, 0), (0, 8 - slots), (0, 128 - own_rows)))
     bias_own = lax.dynamic_update_slice(
         jnp.zeros((6, local_heads, width), F32), ada_bias.astype(F32), (0, 0, lax.axis_index("dp") * entries)
-    )
-    products = jnp.dot(signal_rows, ada_flat, preferred_element_type=F32) + bias_own.reshape(1, 6 * own_cols)
-    products = jnp.pad(products.reshape(n_dev, 6, own_cols), ((0, 0), (0, 2), (0, 0)))
+    ).reshape(6, own_cols)
+    small = jnp.concatenate([qv_bias.reshape(-1), out_bias.reshape(-1), fc1_bias.reshape(-1)]).astype(F32)
+    extra = jnp.concatenate(
+        [bias_own, jnp.pad(small, (0, own_cols - scale_at))[None], jnp.pad(head_log_scale, (0, own_cols - local_heads))[None]]
+    )
 
     lengths = lax.dynamic_index_in_dim(to_slots(scale_lengths), mine, 0, keepdims=False)
     kmask, qmask = build_masks(lengths, half_rows, padded)
@@ -975,49 +984,50 @@
         qkv_weight.reshape(3, own_rows, 2, 256).transpose(1, 2, 0, 3).reshape(own_rows, 3 * own_cols),
         proj_weight.T, fc1_weight, fc2_weight.T,
     ]
-    (qkv_f, proj_f, _, _, x_f, _, g1_f, g2_f, mods, q_low, k_low, v_low, mixed, stats, result, grad_middle,
-     feed_rows, g_hidden) = run_ahead(
-        gather_list(), line, products, segments, pad_rows(to_slots(tokens), padded), pad_rows(cotangent, padded),
-        vecs, hidden_bias, boosts, kmask, qmask, width, 1,
-    )
-    act_pair, tok_pair, (t_qkv, t_proj, t_fc1, t_fc2, sums, back_rows, arrived) = run_behind(
+    (qkv_f, proj_f, _, _, g1_f, g2_f, q_low, k_low, v_low, mixed, x_f, boosts, mods, stats, result, grad_middle,
+     feed_rows, g_hidden, sig_all, ada_flat) = run_ahead(
+        gather_list(), line, signals, ada_weight, extra, segments, pad_rows(to_slots(tokens), padded),
+        pad_rows(cotangent, padded), kmask, qmask, 2 * hidden_cols, width, 1,
+    )
+    act_far, tok_far, (t_qkv, t_proj, t_fc1, t_fc2, arrived, token_grad) = run_behind(
         scatter_list(), line, scale_lengths.shape[1],
         [x_f, qkv_f, proj_f, g1_f, g2_f, result, q_low, k_low, v_low, mixed],
-        [grad_middle, mods, feed_rows, stats, boosts, kmask, qmask], width, 2,
+        [grad_middle, mods, feed_rows, g_hidden, stats, boosts, kmask, qmask], width, 2,
     )
     qkv_total = t_qkv.reshape(own_rows, 2, 3, 256).transpose(2, 0, 1, 3).reshape(qkv_weight.shape)
-    activations = act_pair[:, :half_rows]
-    tokens_grad = to_slots(tok_pair[:, :half_rows])
-
-    all_mods = arrived[:, :6].reshape(n_dev, 6 * own_cols)
+
+    def both_slots(image, far, swapped):
+        near = jnp.where(mine == 0, image[:half_rows], image[padded : padded + half_rows])
+        first = (mine == 0) != swapped
+        return jnp.stack([jnp.where(first, near, far[:half_rows]), jnp.where(first, far[:half_rows], near)])
+
+    activations = both_slots(result, act_far, False)
+    tokens_grad = both_slots(token_grad, tok_far, swap)
+
+    all_mods = arrived[:, :, :6].reshape(n_dev, 6 * own_cols)
+    signal_part = lax.dot_general(
+        all_mods, ada_flat.astype(F32), (((1,), (1,)), ((), ())), precision=precise, preferred_element_type=F32
+    ).reshape(n_dp, 1, slots * own_rows)
+    signal_part = jnp.broadcast_to(signal_part, (n_dp, 2, slots * own_rows)).reshape(n_dev, slots * own_rows)
+    signal_part = lax.all_to_all(signal_part, ("dp", "mp"), 0, 0, tiled=True)
+    signal_grad = signal_part.reshape(n_dp, 2, slots, own_rows).sum(1).transpose(1, 0, 2).reshape(slots, model)
+    signal_rows = sig_all[:, 0, :slots, :own_rows].reshape(n_dev, own_rows)
     ada_weight_grad = lax.dot_general(
-        signal_rows.astype(F32), all_mods, (((0,), (0,)), ((), ())), precision=precise, preferred_element_type=F32
+        signal_rows, all_mods, (((0,), (0,)), ((), ())), precision=precise, preferred_element_type=F32
     ).reshape(ada_weight.shape)
+    small_total = arrived[:, :, 6:].sum((0, 1))
+    by_head = small_total[0].reshape(8, 2 * local_heads, entries)
+    bias_total = lax.dynamic_slice_in_dim(by_head[:4], mine * local_heads, local_heads, 1)
+    hidden_total = lax.dynamic_slice_in_dim(by_head[4:], mine * 2, 2, 0).reshape(fc1_bias.shape)
+    scale_total = lax.dynamic_slice_in_dim(small_total[1], mine * local_heads, local_heads, 0)
     ada_bias_grad = lax.dynamic_slice_in_dim(
         jnp.sum(all_mods, 0).reshape(6, local_heads, width), lax.axis_index("dp") * entries, entries, 2
     )
-    signal_part = lax.dot_general(
-        all_mods, ada_flat.astype(F32), (((1,), (1,)), ((), ())), precision=precise, preferred_element_type=F32
-    )
-    bias_grads = jnp.stack([sums[:, 0].reshape(model), sums[:, 1].reshape(model), back_rows[2], feed_rows[3]])
-    bias_grads = bias_grads.reshape(4, 2, local_heads, n_dp, entries).transpose(3, 1, 0, 2, 4)
-    hidden_grads = g_hidden[0].reshape(2, fc1_bias.shape[0], n_dp, entries).transpose(2, 0, 1, 3)
-    scale_grads = jnp.broadcast_to(sums[:, 4:, 0].reshape(1, 2, local_heads), (n_dp, 2, local_heads))
-    signal_part = jnp.broadcast_to(signal_part.reshape(n_dp, 1, slots * own_rows), (n_dp, 2, slots * own_rows))
-    letters = jnp.concatenate(
-        [signal_part, bias_grads.reshape(n_dp, 2, -1), hidden_grads.reshape(n_dp, 2, -1), scale_grads], 2
-    ).reshape(n_dev, -1)
-    letters = lax.all_to_all(letters, ("dp", "mp"), 0, 0, tiled=True).reshape(n_dp, 2, -1)
-    signal_grad = letters[:, :, : slots * own_rows].sum(1).reshape(n_dp, slots, own_rows)
-    signal_grad = signal_grad.transpose(1, 0, 2).reshape(slots, model)
-    small_total = letters[:, :, slots * own_rows :].sum((0, 1))
-    bias_total = small_total[: 4 * local_heads * entries].reshape(2, 2, local_heads, entries)
-    hidden_total = small_total[4 * local_heads * entries : scale_at].reshape(fc1_bias.shape)
     pull = jax.vjp(jax.nn.silu, cond_slots)[1]
     condition_grad = to_slots(pull(signal_grad)[0]).astype(BF16)
     return (
-        activations, tokens_grad, condition_grad, ada_weight_grad, ada_bias_grad, qkv_total, bias_total[0],
-        small_total[scale_at:], t_proj.T, bias_total[1], t_fc1, hidden_total, t_fc2.T,
+        activations, tokens_grad, condition_grad, ada_weight_grad, ada_bias_grad, qkv_total, bias_total[:2],
+        scale_total, t_proj.T, bias_total[2:], t_fc1, hidden_total, t_fc2.T,
     )
 
 

time: 466 us -> 392 us (0.84)
  Pallas kernels: 398 us -> 341 us
  local copies, waits for them, and re-layouts: 37.3 us -> 28.1 us
  starting transfers between devices: 11.5 us -> 3.17 us
    pallas_call x2, Pallas kernels: 398 us -> 341 us  [the longest x1 185 us: run_ahead(): pl.pallas_call(functools.partial(ahead_kernel, batches, line, width), in_...]
    all_to_all x2 -> x1, starting transfers between devices: 11.5 us -> 3.17 us  [on_device_paired(): signal_part = lax.all_to_all(signal_part, ('dp', 'mp'), 0, 0, tiled=True)]
    unnamed x36 -> x42, local copies, waits for them, and re-layouts: 15 us -> 13.7 us
  transfers between devices with their start and end apart: 2 -> 1, of which waited for: 0 -> 0; matrix products, arithmetic and copies ran while one was open for 5% -> 4% of each run, Pallas kernels for 0% -> 0%
where the time goes in v3:
time: 392 us; the launch traced here: 389 us
  Pallas kernels  341 us (87%)
  local copies, waits for them, and re-layouts  28.1 us (7%)
  other arithmetic  12.3 us (3%)
    pallas_call x1, Pallas kernels, run_ahead(): pl.pallas_call(functools.partial(ahead_kernel, batches, line, width), in_...  185 us
    pallas_call x1, Pallas kernels, run_behind(): pl.pallas_call(functools.partial(behind_kernel, batches, line, width, lev...  156 us
    unnamed x42, local copies, waits for them, and re-layouts  13.7 us
  transfers between devices with their start and end apart: 1, of which 0 were waited for; matrix products, arithmetic and copies ran while one was open for 4% of the time, Pallas kernels for 0%

profile of v3, /device:TPU:0, one launch (start us, length us, event | category | flops | bytes accessed | tf_op | source)
XLA Modules:
  0.0 389.2 jit_solution(4109814424587812222)
XLA Ops:
  1.3 0.8 broadcast_select_fusion.9
  2.1 0.1 select_reduce_fusion
  2.2 0.1 convert_reduce_fusion
  2.4 5.3 %fusion.36 = (bf16[1,340,1024]{2,0,1:T(2,128)(2,1)S(1)}, bf16[1,340,1024]{2,0,1:T(2,128)(2,1)}) fusion(bf16[2,340,1024]{2,0,1:T(2,128)(2,1)} %param.15), kind=kLoop, calls=%fused_computation.89 | loop fusion | bytes 2785280 | tf_op jit(solution)/shard_map/slice | solution.py:967
  7.8 0.1 stack.45
  7.8 0.1 stack.46
  8.0 0.6 pad_convert_fusion.refs_0_
  8.6 0.1 copy.157
  8.7 0.7 dynamic_update_slice.3
  9.4 0.1 reshape.132
  9.5 0.1 copy.160
  9.6 0.1 reshape.135
  9.8 0.1 copy.158
  9.9 0.1 reshape.133
  10.0 0.1 copy.159
  10.1 0.1 reshape.134
  10.2 1.7 copy.164
  11.9 0.1 reshape.136
  12.0 0.2 copy.197
  12.1 0.9 reshape.137.refs_3_
  13.0 2.0 copy.165.refs_1_
  15.1 0.7 fusion.7.refs_9_.refs_16_
  15.7 0.7 select_convert_fusion.refs_10_.refs_17_
  16.4 1.8 broadcast_select_fusion.1
  18.2 1.3 fusion.2.refs_7_
  19.4 1.2 pad.27.refs_8_
  20.7 0.1 fusion.31
  20.8 0.6 pad_maximum_fusion.2.refs_2_
  21.4 185.3 %ahead.1 = (bf16[2,4,2,2,64,1536]{5,4,3,2,1,0:T(8,128)(2,1)}, bf16[2,4,2,2,64,512]{5,4,3,2,1,0:T(8,128)(2,1)}, bf16[2,4,2,2,64,2048]{5,4,3,2,1,0:T(8,128)(2,1)},...) custom-call(f32[16,8,128]{2,1,0:T(8,128)} %pad_convert_fusion.refs_0, ...), custom_call_target="tpu_custom_call" | custom-call | tf_op jit(solution)/shard_map/ahead/pallas_call | solution.py:654
  206.7 155.9 %behind.1 = (bf16[2,4,2,2,64,1536]{5,4,3,2,1,0:T(8,128)(2,1)}, bf16[2,4,2,2,64,512]{5,4,3,2,1,0:T(8,128)(2,1)}, bf16[352,1024]{1,0:T(8,128)(2,1)}, bf16[352,1024...) custom-call(bf16[704,1024]{1,0:T(8,128)(2,1)} %get-tuple-element.40., ...), custom_call_target="tpu_custom_call" | custom-call | tf_op jit(solution)/shard_map/behind/pallas_call | solution.py:895
  362.7 1.2 slice_reduce_fusion.3
  363.9 0.2 copy.179
  364.1 0.4 fusion.37
  364.6 0.1 broadcast_in_dim.67
  364.6 0.6 broadcast_in_dim.68
  365.2 3.2 all-to-all-start
  368.4 1.1 slice_reduce_fusion
  369.6 0.8 slice.104
  370.4 1.9 fusion.3
  372.3 0.1 reshape.141
  372.4 0.1 constant_dynamic-slice_fusion.4
  372.4 0.1 slice.107
  372.5 0.1 slice.112
  372.7 1.6 select_bitcast_fusion.1
  374.2 0.1 pad_maximum_fusion.1
  374.4 0.1 pad_maximum_fusion
  374.6 0.6 fusion.33
  375.1 2.5 copy.171
  377.7 2.5 copy.170
  380.2 0.3 reshape.142
  380.5 0.2 copy.168
  380.7 1.1 reshape.143
  381.8 0.7 copy.172
  382.5 0.7 copy.173
  383.1 0.7 copy.174
  383.8 0.7 copy.175
  384.5 0.5 broadcast.162
  385.0 0.7 reduce.14
  385.7 0.1 reshape.139
  385.8 0.1 reshape.140
  385.9 0.6 pad_maximum_fusion.3
  386.5 0.7 copy.202
  387.2 0.8 copy.203
  388.0 0.8 copy.204
  (48 shorter events, 0.3 us)
Async XLA Ops:
  2.4 5.4 %copy-start.8 = (bf16[2,1024]{1,0:T(2,128)(2,1)S(1)}, bf16[2,1024]{1,0:T(2,128)(2,1)}, u32[]{:S(2)}) copy-start(bf16[2,1024]{1,0:T(2,128)(2,1)} %param.16) | copy-start | bytes 12292
  2.4 6.2 %copy-start.9 = (bf16[6,8,4]{1,2,0:T(4,128)(2,1)S(1)}, bf16[6,8,4]{1,2,0:T(4,128)(2,1)}, u32[]{:S(2)}) copy-start(bf16[6,8,4]{1,2,0:T(4,128)(2,1)} %param.21) | copy-start | bytes 1156
  2.4 7.1 %copy-start.12 = (bf16[32,4]{0,1:T(4,128)(2,1)S(1)}, bf16[32,4]{0,1:T(4,128)(2,1)}, u32[]{:S(2)}) copy-start(bf16[32,4]{0,1:T(4,128)(2,1)} %param.28) | copy-start | bytes 772
  2.4 7.4 %copy-start.10 = (bf16[2,8,4]{1,2,0:T(4,128)(2,1)S(1)}, bf16[2,8,4]{1,2,0:T(4,128)(2,1)}, u32[]{:S(2)}) copy-start(bf16[2,8,4]{1,2,0:T(4,128)(2,1)} %param.23) | copy-start | bytes 388
  2.4 7.6 %copy-start.11 = (bf16[2,8,4]{1,2,0:T(4,128)(2,1)S(1)}, bf16[2,8,4]{1,2,0:T(4,128)(2,1)}, u32[]{:S(2)}) copy-start(bf16[2,8,4]{1,2,0:T(4,128)(2,1)} %param.26) | copy-start | bytes 388
  2.4 7.8 %copy-start.13 = (f32[8]{0:T(128)S(1)}, f32[8]{0:T(128)}, u32[]{:S(2)}) copy-start(f32[8]{0:T(128)} %param.24) | copy-start | bytes 100
  9.4 2.5 copy-start.6
  362.7 1.4 copy-start.5
  363.8 8.8 %copy-start.1 = (bf16[704,1024]{1,0:T(8,128)(2,1)S(1)}, bf16[704,1024]{1,0:T(8,128)(2,1)}, u32[]{:S(2)}) copy-start(bf16[704,1024]{1,0:T(8,128)(2,1)} %get-tuple-element.56) | copy-start | bytes 4325380
  364.1 8.6 %copy-start = (bf16[704,1024]{1,0:T(8,128)(2,1)S(1)}, bf16[704,1024]{1,0:T(8,128)(2,1)}, u32[]{:S(2)}) copy-start(bf16[704,1024]{1,0:T(8,128)(2,1)} %get-tuple-element.39.refs_5_) | copy-start | bytes 4325380
  365.2 19.2 %all-to-all-start = ((f32[32,1,128]{2,1,0:T(1,128)}), f32[32,1,128]{2,1,0:T(1,128)S(1)}, u32[]{:S(2)}, u32[]{:S(2)}) async-start(f32[32,1,128]{2,1,0:T(1,128)} %bitcast.12), calls=%async_computation | async-start | bytes 32768 | tf_op jit(solution)/shard_map/all_to_all | solution.py:1012
  377.7 2.5 copy-start.4
  380.2 6.4 %copy-start.7 = (f32[64,512]{1,0:T(8,128)S(1)}, f32[64,512]{1,0:T(8,128)}, u32[]{:S(2)}) copy-start(f32[64,512]{1,0:T(8,128)} %get-tuple-element.62) | copy-start | bytes 393220
  380.2 7.0 %copy-start.3 = (f32[64,2048]{1,0:T(8,128)S(1)}, f32[64,2048]{1,0:T(8,128)}, u32[]{:S(2)}) copy-start(f32[64,2048]{1,0:T(8,128)} %get-tuple-element.220) | copy-start | bytes 1572868
  380.7 7.3 %copy-start.2 = (f32[64,2048]{1,0:T(8,128)S(1)}, f32[64,2048]{1,0:T(8,128)}, u32[]{:S(2)}) copy-start(f32[64,2048]{1,0:T(8,128)} %get-tuple-element.64) | copy-start | bytes 1572868
